TPU v7x, 256 devices: a whole 4x4x8 slice. The times are simulated.
256 devices in a mesh: subj: 64 (over y, z, core), strip: 4 (over x).
Axes of the slice: x: 4, y: 4, z: 8, core: 2. Of those that a mesh axis runs over, the one named last changes fastest.
Arguments:
- displacement: bfloat16 [128, 3, 4, 512, 512], P('subj', None, None, None, 'strip'), may hold values from -0.14941406 to 0.14941406
- age: float32 [128], replicated, may hold values from -4 to 4
- group_codes: int32 [128], replicated, may hold values from 0 to 2, as said below
- perms: int32 [256, 128], replicated, may hold values from 0 to 127, each once within a row
Outputs:
- t_map: float32 [2, 512, 512], P(None, 'subj', 'strip')
- peaks: float32 [256], replicated
Inputs may be any that keep to these rules, and one draw needn't show every extreme that they name: `group_codes`: each of the three groups holds 42 or more subjects.
All inputs are finite; a program needn't handle non-finite values.
Results may differ from a plain program's by a relative error of at most 0.0014.
Values may be sent and summed in bfloat16 or wider, within the bound.
No kernel may reach another device: no remote copies, remote signals or barrier semaphores. Data moves between devices by JAX's collectives and lax.ppermute only.
A program may use at most 128 MiB of HBM per device.

v0:
```python
import math

import jax
import jax.numpy as jnp
from jax import lax
from jax.sharding import PartitionSpec as P


def extended(cells, sides, width):
    for axis, dim in sides:
        count = lax.axis_size(axis)
        ends = count - 1
        head = lax.slice_in_dim(cells, 0, width, axis=dim)
        tail = lax.slice_in_dim(cells, cells.shape[dim] - width, cells.shape[dim], axis=dim)
        cells = jnp.concatenate(
            [
                lax.ppermute(tail, axis, [(i, (i + 1) % count) for i in range(ends)]),
                cells,
                lax.ppermute(head, axis, [((i + 1) % count, i) for i in range(ends)]),
            ],
            axis=dim,
        )
    return cells


def invert_small(matrix):
    size = matrix.shape[0]
    work = jnp.concatenate([matrix, jnp.eye(size, dtype=matrix.dtype)], axis=1)
    for column in range(size):
        pivot_row = work[column] / work[column, column]
        work = work - work[:, column : column + 1] * pivot_row[None, :]
        work = work.at[column].set(pivot_row)
    return work[:, size:]


def build_design(age, group_codes):
    ones = jnp.ones_like(age)
    first = (group_codes == 1).astype(age.dtype)
    second = (group_codes == 2).astype(age.dtype)
    return jnp.stack([ones, first, second, age], axis=1)


def log_volume(dz, dx, dy):
    j00 = 1.0 + dz[:, 0]
    j01 = dx[:, 0]
    j02 = dy[:, 0]
    j10 = dz[:, 1]
    j11 = 1.0 + dx[:, 1]
    j12 = dy[:, 1]
    j20 = dz[:, 2]
    j21 = dx[:, 2]
    j22 = 1.0 + dy[:, 2]
    det = (
        j00 * (j11 * j22 - j12 * j21)
        - j01 * (j10 * j22 - j12 * j20)
        + j02 * (j10 * j21 - j11 * j20)
    )
    return jnp.log(det)


def residual_terms(proj, yty, ginv):
    rss = yty[None]
    effect = None
    for row in range(4):
        coef = (
            ginv[row, 0] * proj[:, 0]
            + ginv[row, 1] * proj[:, 1]
            + ginv[row, 2] * proj[:, 2]
            + ginv[row, 3] * proj[:, 3]
        )
        rss = rss - proj[:, row] * coef
        if row == 2:
            effect = coef
    return (effect, rss)


def finish(effect, rss, padded, ginv, subjects):
    beside_all = (
        padded[:, :, :-2, 1:-1]
        + padded[:, :, 2:, 1:-1]
        + padded[:, :, 1:-1, :-2]
        + padded[:, :, 1:-1, 2:]
    )
    smooth = 0.4 * rss + 0.15 * beside_all
    variance = ginv[2, 2] * (smooth / (subjects - 4) + 1e-06)
    return effect / jnp.sqrt(variance)


def rss_border(rss):
    return extended(rss.astype(jnp.bfloat16), (("subj", 2), ("strip", 3)), 1).astype(rss.dtype)


def on_device(displacement, age, group_codes, perms):
    subjects = group_codes.shape[0]
    nperm = perms.shape[0]
    inner = displacement[:, :, 1:-1]
    rows = extended(inner, (("strip", 4),), 1)
    wide = rows.astype(jnp.float32)
    dy = (wide[..., 2:] - wide[..., :-2]) * 0.5
    full = displacement.astype(jnp.float32)
    dz = (full[:, :, 2:] - full[:, :, :-2]) * 0.5
    center = wide[..., 1:-1]
    padx = jnp.pad(center, ((0, 0), (0, 0), (0, 0), (1, 1), (0, 0)))
    dx = (padx[:, :, :, 2:] - padx[:, :, :, :-2]) * 0.5
    log_jac = log_volume(dz, dx, dy)
    design = build_design(age, group_codes)
    gram = jnp.dot(design.T, design, precision=lax.Precision.HIGHEST)
    ginv = invert_small(gram)
    permuted = jnp.transpose(design[perms], (0, 2, 1)).reshape(nperm * 4, subjects)
    zrows = jnp.concatenate([design.T, permuted], axis=0)
    regrouped = lax.all_to_all(log_jac, "subj", split_axis=2, concat_axis=0, tiled=True)
    shape = regrouped.shape
    ymat = regrouped.reshape(shape[0], -1)
    project_proj = jnp.dot(zrows, ymat, precision=lax.Precision.HIGHEST)
    squares = jnp.sum(ymat * ymat, axis=0)
    proj = project_proj.reshape((zrows.shape[0],) + shape[1:])
    yty = squares.reshape((1,) + shape[1:])
    cells = proj.shape[1:]
    proj = proj.reshape((nperm + 1, 4) + cells)
    yty = yty[0]

    def block_stats(block):
        effect, rss = residual_terms(block, yty, ginv)
        padded = rss_border(rss)
        return finish(effect, rss, padded, ginv, subjects)

    width = math.gcd(nperm, 128)
    t_map = block_stats(proj[0:1])[0]

    def block_peaks(index):
        block = lax.dynamic_slice_in_dim(proj, 1 + index * width, width, 0)
        local = jnp.max(jnp.abs(block_stats(block)), axis=(1, 2, 3))
        return lax.pmax(local, ("subj", "strip"))

    peaks = lax.map(block_peaks, jnp.arange(nperm // width, dtype=jnp.int32)).reshape(nperm)
    return (t_map, peaks)


def solution(mesh):
    placed = (P("subj", None, None, None, "strip"), P(), P(), P())
    return jax.shard_map(
        on_device,
        mesh=mesh,
        in_specs=placed,
        out_specs=(P(None, "subj", "strip"), P()),
        check_vma=False,
    )
```

profile of v0, /device:TPU:1, one launch (start us, length us, event | category | flops | bytes accessed | tf_op | source)
XLA Modules:
  0.0 490.3 jit_solution(14559308134933103604)
XLA Ops:
  0.6 4.2 fusion.44
  10.0 4.6 collective-permute-start.4
  35.0 3.8 copy.68
  38.7 9.4 %maximum_convert_fusion.1 = f32[2,3,2,512,130]{4,2,0,3,1:T(2,128)S(1)} fusion(bf16[2,3,2,512,1]{4,2,0,3,1:T(2,128)(2,1)} %copy.68, bf16[2,3,2,512,128]{4,2,0,3,1:T(2,128)(2,1)S(1)} %copy.85, bf16[2,3,2,512,1]{4,2,0,3,1:T(2,128)(2,1)S(1)} %copy.67), kind=kLoop, calls=%fused_computation.25 | loop fusion | flops 4792320 | bytes 4792320 | tf_op jit(solution)/shard_map/convert_element_type | solution.py:98
  48.2 6.7 %fusion.43 = (f32[2,3,2,512,128]{4,2,0,3,1:T(2,128)S(1)}, f32[2,3,2,512,128]{4,2,0,3,1:T(2,128)S(1)}) fusion(f32[2,3,2,512,130]{4,2,0,3,1:T(2,128)S(1)} %maximum_convert_fusion.1), kind=kLoop, calls=%fused_computation.97 | loop fusion | flops 1572864 | bytes 15728640 | tf_op jit(solution)/shard_map/slice | solution.py:102
  60.5 13.1 %all-to-all-start = ((f32[2,2,512,128]{3,1,0,2:T(2,128)}), f32[2,2,512,128]{3,1,0,2:T(2,128)S(1)}, u32[]{:S(2)}, u32[]{:S(2)}) async-start(f32[2,2,512,128]{3,1,0,2:T(2,128)} %fusion.13), calls=%async_computation | async-start | bytes 2097152 | tf_op jit(solution)/shard_map/all_to_all | solution.py:111
  73.7 109.0 %gather_fusion = f32[32768,4]{1,0:T(8,128)} fusion(f32[128,4]{1,0:T(8,128)S(1)} %copy.61, s32[32768]{0:T(1024)S(1)} %fusion.21), kind=kCustom, calls=%fused_computation | custom fusion | bytes 1179648 | tf_op jit(solution)/shard_map/gather | solution.py:109
  182.7 9.4 %copy.62 = f32[256,128,4]{1,2,0:T(4,128)S(1)} copy(f32[256,128,4]{2,1,0:T(8,128)} %bitcast.213) | data formatting | bytes 1048576 | tf_op jit(solution)/shard_map/gather | solution.py:109
  195.7 7.0 %fusion.16 = f32[1028,2048]{1,0:T(8,128)S(1)} fusion(f32[128,2048]{1,0:T(8,128)S(1)} %reshape.592, f32[1024,128]{1,0:T(8,128)S(1)} %bitcast.219, f32[4,128]{1,0:T(4,128)S(1)} %fusion.53), kind=kOutput, calls=%fused_computation.39 | convolution fusion | flops 3233939968 | bytes 9996288 | tf_op jit(solution)/shard_map/dot_general | solution.py:114
  206.0 10.0 %fusion.38 = (bf16[1,2,8,128]{3,2,1,0:T(8,128)(2,1)S(1)}, f32[1,2,8,128]{3,2,1,0:T(8,128)S(1)}) fusion(f32[]{:T(128)} %bitcast.63, f32[]{:T(128)} %bitcast.62, f32[]{:T(128)} %bitcast.61, f32[]{:T(128)} %bitcast.60, f32[]{:T(128)} %bitcast.49, f32[]{:T(128)} %bitcast.47, f32[]{:T(128)} %bitcast.45, f32[]{:T(128)} %bitcast.35, f32[]{:T(128)} %bitcast.59, ...), kind=kLoop, calls=%fused_computation.93 | loop fusion | flops 75776 | bytes 53312 | tf_op jit(solution)/shard_map/convert_element_type | solution.py:90
  216.0 3.5 collective-permute-start.6
  221.5 5.4 %copy.79 = f32[129,8,16,128]{3,2,1,0:T(8,128)S(1)} copy(f32[129,8,16,128]{3,1,2,0:T(8,128)} %bitcast.214) | data formatting | bytes 16908288
  227.0 3.5 slice.570
  241.2 248.2 %while.16 = (s32[]{:T(128)}, f32[2,128]{1,0:T(2,128)S(1)}, f32[4,4]{1,0:T(4,128)S(1)}, s32[2]{0:T(128)S(1)}, f32[257,4,2,8,128]{4,3,2,1,0:T(8,128)}, /*index=5*/...) while((s32[]{:T(128)}, f32[2,128]{1,0:T(2,128)S(1)}, ...), condition=%wide.region_4.5_spmd, body=%wide.region_1.4_spmd.sunk | while | flops 19974152 | bytes 23606440 | solution.py:135
  243.4 14.6 %fusion.64 = (bf16[128,2,8,128]{3,2,1,0:T(8,128)(2,1)S(1)}, f32[128,2,8,128]{3,2,1,0:T(8,128)}) fusion(f32[]{:T(128)} %bitcast.192, f32[]{:T(128)} %bitcast.193, f32[]{:T(128)} %bitcast.194, f32[]{:T(128)} %bitcast.195, f32[]{:T(128)} %bitcast.196, f32[]{:T(128)} %bitcast.197, f32[]{:T(128)} %bitcast.198, f32[]{:T(128)} %bitcast.199, f32[]{:T(128)} %bitcast.200, ...), kind=kLoop, calls=%fused_computation.92.clone.1 | loop fusion | flops 9699328 | bytes 5775440 | tf_op jit(solution)/shard_map/while/body/eval_jaxpr/convert_element_type | solution.py:90
  260.1 5.1 %collective-permute-start.1 = (bf16[128,2,1,128]{3,2,1,0:T(2,128)(2,1)S(1)}, bf16[128,2,1,128]{3,2,1,0:T(2,128)(2,1)S(1)}, u32[]{:S(2)}, u32[]{:S(2)}) collective-permute-start(bf16[128,2,1,128]{3,2,1,0:T(2,128)(2,1)S(1)} %get-tuple-element.291), channel_id=1, source_target_pairs={{0,4},{4,8},{8,12},{12,16},{16,20},{20,24},{24,28},{28,32},{32,36}... | collective-permute-start | bytes 196616 | tf_op jit(solution)/shard_map/while/body/eval_jaxpr/ppermute | solution.py:17
  271.0 4.0 collective-permute-start.3
  280.2 7.4 %fusion.67 = f32[128]{0:T(128)S(1)} fusion(f32[128,2,10,130]{3,2,1,0:T(8,128)S(1)} %maximum_convert_fusion.4, f32[128,2,8,128]{3,2,1,0:T(8,128)S(1)} %copy-done, f32[257,4,2,8,128]{4,3,2,1,0:T(8,128)} %get-tuple-element.327, s32[]{:T(128)S(6)} %select_n.16, s32[]{:T(128)S(6)} %add.631, s32[]{:T(128)S(6)} %add.630, s32[]{:T(128)S(6)} %add.629, ...), kind=kLoop, calls=%fused_computation.20.clone.1 | loop fusion | flops 4980608 | bytes 9437728 | tf_op jit(solution)/shard_map/while/body/eval_jaxpr/reduce_max | solution.py:132
  287.6 80.0 %pmax.11 = f32[1,128]{1,0:T(1,128)S(1)} all-reduce(f32[1,128]{1,0:T(1,128)S(1)} %bitcast.224), channel_id=1, replica_groups=mesh['subj'=64,'strip'=4] {'subj','strip'}, use_global_device_ids=true, to_apply=%region_3.3 | all-reduce | flops 128 | bytes 1024 | tf_op jit(solution)/shard_map/while/body/eval_jaxpr/pmax | solution.py:133
  369.6 14.6 %fusion.64 = (bf16[128,2,8,128]{3,2,1,0:T(8,128)(2,1)S(1)}, f32[128,2,8,128]{3,2,1,0:T(8,128)}) fusion(f32[]{:T(128)} %bitcast.192, f32[]{:T(128)} %bitcast.193, f32[]{:T(128)} %bitcast.194, f32[]{:T(128)} %bitcast.195, f32[]{:T(128)} %bitcast.196, f32[]{:T(128)} %bitcast.197, f32[]{:T(128)} %bitcast.198, f32[]{:T(128)} %bitcast.199, f32[]{:T(128)} %bitcast.200, ...), kind=kLoop, calls=%fused_computation.92.clone.1 | loop fusion | flops 9699328 | bytes 5775440 | tf_op jit(solution)/shard_map/while/body/eval_jaxpr/convert_element_type | solution.py:90
  386.9 3.6 collective-permute-start.1
  396.3 4.0 collective-permute-start.3
  405.6 7.4 %fusion.67 = f32[128]{0:T(128)S(1)} fusion(f32[128,2,10,130]{3,2,1,0:T(8,128)S(1)} %maximum_convert_fusion.4, f32[128,2,8,128]{3,2,1,0:T(8,128)S(1)} %copy-done, f32[257,4,2,8,128]{4,3,2,1,0:T(8,128)} %get-tuple-element.327, s32[]{:T(128)S(6)} %select_n.16, s32[]{:T(128)S(6)} %add.631, s32[]{:T(128)S(6)} %add.630, s32[]{:T(128)S(6)} %add.629, ...), kind=kLoop, calls=%fused_computation.20.clone.1 | loop fusion | flops 4980608 | bytes 9437728 | tf_op jit(solution)/shard_map/while/body/eval_jaxpr/reduce_max | solution.py:132
  413.0 76.5 %pmax.11 = f32[1,128]{1,0:T(1,128)S(1)} all-reduce(f32[1,128]{1,0:T(1,128)S(1)} %bitcast.224), channel_id=1, replica_groups=mesh['subj'=64,'strip'=4] {'subj','strip'}, use_global_device_ids=true, to_apply=%region_3.3 | all-reduce | flops 128 | bytes 1024 | tf_op jit(solution)/shard_map/while/body/eval_jaxpr/pmax | solution.py:133
  (120 shorter events, 80.7 us)
Async XLA Ops:
  4.8 9.8 %copy-start.7 = (s32[128]{0:T(128)S(1)}, s32[128]{0:T(128)}, u32[]{:S(2)}) copy-start(s32[128]{0:T(128)} %param.16) | copy-start | bytes 1540
  4.8 9.8 %copy-start.5 = (f32[128]{0:T(128)S(1)}, f32[128]{0:T(128)}, u32[]{:S(2)}) copy-start(f32[128]{0:T(128)} %param.15) | copy-start | bytes 1540
  4.8 15.2 %copy-start.2 = (bf16[2,3,4,512,128]{4,3,2,1,0:T(8,128)(2,1)S(1)}, bf16[2,3,4,512,128]{4,3,2,1,0:T(8,128)(2,1)}, u32[]{:S(2)}) copy-start(bf16[2,3,4,512,128]{4,3,2,1,0:T(8,128)(2,1)} %param.14) | copy-start | bytes 9437188
  6.8 28.1 %collective-permute-start.5 = (bf16[2,3,2,512,1]{3,1,4,2,0:T(4,128)(2,1)S(1)}, bf16[2,3,2,512,1]{3,1,4,2,0:T(4,128)(2,1)S(1)}, u32[]{:S(2)}, u32[]{:S(2)}) collective-permute-start(bf16[2,3,2,512,1]{3,1,4,2,0:T(4,128)(2,1)S(1)} %copy.73), channel_id=1, source_target_pairs={{1,0},{2,1},{3,2},{5,4},{6,5},{7,6},{9,8},{10,9},{11,10},{13,12},{... | collective-permute-start | bytes 36872 | tf_op jit(solution)/shard_map/ppermute | solution.py:19
  10.0 22.5 %collective-permute-start.4 = (bf16[2,3,2,512,1]{3,1,4,2,0:T(4,128)(2,1)S(1)}, bf16[2,3,2,512,1]{3,1,4,2,0:T(4,128)(2,1)S(1)}, u32[]{:S(2)}, u32[]{:S(2)}) collective-permute-start(bf16[2,3,2,512,1]{3,1,4,2,0:T(4,128)(2,1)S(1)} %copy.72), channel_id=1, source_target_pairs={{0,1},{1,2},{2,3},{4,5},{5,6},{6,7},{8,9},{9,10},{10,11},{12,13},{... | collective-permute-start | bytes 36872 | tf_op jit(solution)/shard_map/ppermute | solution.py:17
  54.9 2.2 copy-start.3
  57.1 16.6 %copy-start.4 = (s32[256,128]{1,0:T(8,128)S(1)}, s32[256,128]{1,0:T(8,128)}, u32[]{:S(2)}) copy-start(s32[256,128]{1,0:T(8,128)} %param.17) | copy-start | bytes 393220
  60.5 134.8 %all-to-all-start = ((f32[2,2,512,128]{3,1,0,2:T(2,128)}), f32[2,2,512,128]{3,1,0,2:T(2,128)S(1)}, u32[]{:S(2)}, u32[]{:S(2)}) async-start(f32[2,2,512,128]{3,1,0,2:T(2,128)} %fusion.13), calls=%async_computation | async-start | bytes 2097152 | tf_op jit(solution)/shard_map/all_to_all | solution.py:111
  202.7 3.3 copy-start.1
  216.0 14.5 %collective-permute-start.6 = (bf16[1,2,1,128]{3,2,1,0:T(2,128)(2,1)S(1)}, bf16[1,2,1,128]{3,2,1,0:T(2,128)(2,1)S(1)}, u32[]{:S(2)}, u32[]{:S(2)}) collective-permute-start(bf16[1,2,1,128]{3,2,1,0:T(2,128)(2,1)S(1)} %get-tuple-element.194), channel_id=1, source_target_pairs={{0,4},{4,8},{8,12},{12,16},{16,20},{20,24},{24,28},{28,32},{32,36}... | collective-permute-start | bytes 1544 | tf_op jit(solution)/shard_map/ppermute | solution.py:17
  219.5 11.0 %collective-permute-start.7 = (bf16[1,2,1,128]{3,2,1,0:T(2,128)(2,1)S(1)}, bf16[1,2,1,128]{3,2,1,0:T(2,128)(2,1)S(1)}, u32[]{:S(2)}, u32[]{:S(2)}) collective-permute-start(bf16[1,2,1,128]{3,2,1,0:T(2,128)(2,1)S(1)} %get-tuple-element.195), channel_id=1, source_target_pairs={{4,0},{8,4},{12,8},{16,12},{20,16},{24,20},{28,24},{32,28},{36,32}... | collective-permute-start | bytes 1544 | tf_op jit(solution)/shard_map/ppermute | solution.py:19
  230.6 4.4 collective-permute-start.8
  233.7 4.4 collective-permute-start.9
  258.1 7.7 %collective-permute-start = (bf16[128,2,1,128]{3,2,1,0:T(2,128)(2,1)S(1)}, bf16[128,2,1,128]{3,2,1,0:T(2,128)(2,1)S(1)}, u32[]{:S(2)}, u32[]{:S(2)}) collective-permute-start(bf16[128,2,1,128]{3,2,1,0:T(2,128)(2,1)S(1)} %get-tuple-element.290), channel_id=1, source_target_pairs={{4,0},{8,4},{12,8},{16,12},{20,16},{24,20},{28,24},{32,28},{36,32}... | collective-permute-start | bytes 196616 | tf_op jit(solution)/shard_map/while/body/eval_jaxpr/ppermute | solution.py:19
  260.1 7.0 %collective-permute-start.1 = (bf16[128,2,1,128]{3,2,1,0:T(2,128)(2,1)S(1)}, bf16[128,2,1,128]{3,2,1,0:T(2,128)(2,1)S(1)}, u32[]{:S(2)}, u32[]{:S(2)}) collective-permute-start(bf16[128,2,1,128]{3,2,1,0:T(2,128)(2,1)S(1)} %get-tuple-element.291), channel_id=1, source_target_pairs={{0,4},{4,8},{8,12},{12,16},{16,20},{20,24},{24,28},{28,32},{32,36}... | collective-permute-start | bytes 196616 | tf_op jit(solution)/shard_map/while/body/eval_jaxpr/ppermute | solution.py:17
  268.9 6.1 %collective-permute-start.2 = (bf16[128,2,10,1]{0,1,3,2:T(2,128)(2,1)S(1)}, bf16[128,2,10,1]{0,1,3,2:T(2,128)(2,1)S(1)}, u32[]{:S(2)}, u32[]{:S(2)}) collective-permute-start(bf16[128,2,10,1]{0,1,3,2:T(2,128)(2,1)S(1)} %copy.92), channel_id=1, source_target_pairs={{1,0},{2,1},{3,2},{5,4},{6,5},{7,6},{9,8},{10,9},{11,10},{13,12},{... | collective-permute-start | bytes 15368 | tf_op jit(solution)/shard_map/while/body/eval_jaxpr/ppermute | solution.py:19
  271.0 5.5 %collective-permute-start.3 = (bf16[128,2,10,1]{0,1,3,2:T(2,128)(2,1)S(1)}, bf16[128,2,10,1]{0,1,3,2:T(2,128)(2,1)S(1)}, u32[]{:S(2)}, u32[]{:S(2)}) collective-permute-start(bf16[128,2,10,1]{0,1,3,2:T(2,128)(2,1)S(1)} %copy.94), channel_id=1, source_target_pairs={{0,1},{1,2},{2,3},{4,5},{5,6},{6,7},{8,9},{9,10},{10,11},{12,13},{... | collective-permute-start | bytes 15368 | tf_op jit(solution)/shard_map/while/body/eval_jaxpr/ppermute | solution.py:17
  278.0 2.2 copy-start
  384.3 6.9 %collective-permute-start = (bf16[128,2,1,128]{3,2,1,0:T(2,128)(2,1)S(1)}, bf16[128,2,1,128]{3,2,1,0:T(2,128)(2,1)S(1)}, u32[]{:S(2)}, u32[]{:S(2)}) collective-permute-start(bf16[128,2,1,128]{3,2,1,0:T(2,128)(2,1)S(1)} %get-tuple-element.290), channel_id=1, source_target_pairs={{4,0},{8,4},{12,8},{16,12},{20,16},{24,20},{28,24},{32,28},{36,32}... | collective-permute-start | bytes 196616 | tf_op jit(solution)/shard_map/while/body/eval_jaxpr/ppermute | solution.py:19
  386.9 5.5 %collective-permute-start.1 = (bf16[128,2,1,128]{3,2,1,0:T(2,128)(2,1)S(1)}, bf16[128,2,1,128]{3,2,1,0:T(2,128)(2,1)S(1)}, u32[]{:S(2)}, u32[]{:S(2)}) collective-permute-start(bf16[128,2,1,128]{3,2,1,0:T(2,128)(2,1)S(1)} %get-tuple-element.291), channel_id=1, source_target_pairs={{0,4},{4,8},{8,12},{12,16},{16,20},{20,24},{24,28},{28,32},{32,36}... | collective-permute-start | bytes 196616 | tf_op jit(solution)/shard_map/while/body/eval_jaxpr/ppermute | solution.py:17
  394.3 6.1 %collective-permute-start.2 = (bf16[128,2,10,1]{0,1,3,2:T(2,128)(2,1)S(1)}, bf16[128,2,10,1]{0,1,3,2:T(2,128)(2,1)S(1)}, u32[]{:S(2)}, u32[]{:S(2)}) collective-permute-start(bf16[128,2,10,1]{0,1,3,2:T(2,128)(2,1)S(1)} %copy.92), channel_id=1, source_target_pairs={{1,0},{2,1},{3,2},{5,4},{6,5},{7,6},{9,8},{10,9},{11,10},{13,12},{... | collective-permute-start | bytes 15368 | tf_op jit(solution)/shard_map/while/body/eval_jaxpr/ppermute | solution.py:19
  396.3 5.5 %collective-permute-start.3 = (bf16[128,2,10,1]{0,1,3,2:T(2,128)(2,1)S(1)}, bf16[128,2,10,1]{0,1,3,2:T(2,128)(2,1)S(1)}, u32[]{:S(2)}, u32[]{:S(2)}) collective-permute-start(bf16[128,2,10,1]{0,1,3,2:T(2,128)(2,1)S(1)} %copy.94), channel_id=1, source_target_pairs={{0,1},{1,2},{2,3},{4,5},{5,6},{6,7},{8,9},{9,10},{10,11},{12,13},{... | collective-permute-start | bytes 15368 | tf_op jit(solution)/shard_map/while/body/eval_jaxpr/ppermute | solution.py:17
  403.4 2.2 copy-start
  489.5 0.6 copy-start.6
where the time goes:
time: 496 us; the launch traced here: 490 us
  local copies, waits for them, and re-layouts  168 us (34%)
  blocking collectives  156 us (31%)
  other arithmetic  96 us (19%)
  starting transfers between devices  52.5 us (11%)
  matrix products  7.13 us (1%)
  waiting for transfers between devices  6.96 us (1%)
    pmax x2, blocking collectives, block_peaks(): return lax.pmax(local, ('subj', 'strip'))  156 us
    gather x2, local copies, waits for them, and re-layouts, on_device(): design[perms]  118 us
    convert_element_type x3, other arithmetic, rss_border(): rss.astype(jnp.bfloat16)  39.1 us
    ppermute x7, starting transfers between devices, extended(): lax.ppermute(tail, axis, [(i, (i + 1) % count) for i in range(ends)])  27.8 us
    unnamed x21, local copies, waits for them, and re-layouts  19.7 us
    reduce_max x2, other arithmetic, block_peaks(): local = jnp.max(jnp.abs(block_stats(block)), axis=(1, 2, 3))  14.8 us
    all_to_all x1, starting transfers between devices, on_device(): lax.all_to_all(log_jac, 'subj', split_axis=2, concat_axis=0, tiled=True)  13.1 us
    ppermute x7, starting transfers between devices, extended(): lax.ppermute(head, axis, [((i + 1) % count, i) for i in range(ends)])  11.6 us
  transfers between devices with their start and end apart: 15, of which 5 were waited for; matrix products, arithmetic and copies ran while one was open for 32% of the time, Pallas kernels for 0%

commit v1 on v0

v1 whole, which is shorter than its diff:
```python
import functools

import jax
import jax.numpy as jnp
from jax import lax
from jax.experimental import pallas as pl
from jax.experimental.pallas import tpu as pltpu
from jax.sharding import PartitionSpec as P

F32, BF16 = jnp.float32, jnp.bfloat16
LANES = 128
ROWS = 512
BLOCK = 16
CHUNK = 40
PER = 2
COMPS, PLANES = 3, 4
PERMS, GROUP = 256, 272
REACH = 0.6
LEVELS = 32767.0


def slot(subject, comp, plane):
    return 4 * ((subject * COMPS + comp) * PLANES + plane)


def encode(y):
    level = jnp.sqrt(jnp.sqrt(jnp.abs(y) * (1.0 / REACH))) * LEVELS + 0.5
    return jnp.where(y < 0, -level, level)


def decode(code):
    part = code * (REACH**0.25 / LEVELS)
    return (part * jnp.abs(part)) * (part * part)


def log_det(dz, dx, dy):
    j00, j01, j02 = 2.0 + dz[0], dx[0], dy[0]
    j10, j11, j12 = dz[1], 2.0 + dx[1], dy[1]
    j20, j21, j22 = dz[2], dx[2], 2.0 + dy[2]
    det = (
        j00 * (j11 * j22 - j12 * j21)
        - j01 * (j10 * j22 - j12 * j20)
        + j02 * (j10 * j21 - j11 * j20)
    )
    return jnp.log(det * 0.125)


def edges_kernel(disp_ref, out_ref):
    rows = out_ref.shape[0]
    step = 16
    group = lax.broadcasted_iota(jnp.int32, (step, LANES), 1) // 4

    def body(i, carry):
        at = pl.ds(pl.multiple_of(i * step, step), step)
        acc = jnp.zeros((step, LANES), F32)
        for s in range(PER):
            for c in range(COMPS):
                for q in range(PLANES):
                    k = slot(s, c, q)
                    rolled = pltpu.roll(disp_ref[s, c, q, at, :].astype(F32), (k + 2) % LANES, 1)
                    acc = jnp.where(group == k // 4, rolled, acc)
        out_ref[at, :] = acc.astype(BF16)
        return carry

    lax.fori_loop(0, rows // step, body, 0)


def strip_edges(disp):
    rows = 128
    return pl.pallas_call(
        edges_kernel,
        grid=(ROWS // rows,),
        in_specs=[pl.BlockSpec((PER, COMPS, PLANES, rows, LANES), lambda i: (0, 0, 0, i, 0))],
        out_specs=pl.BlockSpec((rows, LANES), lambda i: (i, 0)),
        out_shape=jax.ShapeDtypeStruct((ROWS, LANES), BF16),
        cost_estimate=pl.CostEstimate(flops=10**6, bytes_accessed=3_200_000, transcendentals=0),
        name="strip_edges",
    )(disp)


def inner_kernel(disp_ref, out_ref, pad_ref):
    pad = 8
    for k in range(COMPS * 2):
        pad_ref[k, 0:pad, :] = jnp.zeros((pad, LANES), F32)
        pad_ref[k, pad + ROWS : 2 * pad + ROWS, :] = jnp.zeros((pad, LANES), F32)
        pad_ref[k, pad : pad + ROWS, :] = disp_ref[0, k // 2, 1 + k % 2].astype(F32)
    step = 32

    def body(i, carry):
        base = pl.multiple_of(i * step, step)
        for p in range(2):
            dz, dx, dy = [], [], []
            for c in range(COMPS):
                up = disp_ref[0, c, p + 2, pl.ds(base, step), :].astype(F32)
                down = disp_ref[0, c, p, pl.ds(base, step), :].astype(F32)
                dz.append(up - down)
                center = pad_ref[c * 2 + p, pl.ds(base + pad, step), :]
                dx.append(
                    pad_ref[c * 2 + p, pl.ds(base + pad + 1, step), :]
                    - pad_ref[c * 2 + p, pl.ds(base + pad - 1, step), :]
                )
                dy.append(pltpu.roll(center, LANES - 1, 1) - pltpu.roll(center, 1, 1))
            out_ref[p, pl.ds(base, step), :] = log_det(dz, dx, dy)
        return carry

    lax.fori_loop(0, ROWS // step, body, 0)


def inner_log(disp):
    return pl.pallas_call(
        inner_kernel,
        grid=(PER,),
        in_specs=[pl.BlockSpec((1, COMPS, PLANES, ROWS, LANES), lambda s: (s, 0, 0, 0, 0))],
        out_specs=pl.BlockSpec((2, ROWS, LANES), lambda s: (s, 0, 0)),
        out_shape=jax.ShapeDtypeStruct((PER * 2, ROWS, LANES), F32),
        scratch_shapes=[pltpu.VMEM((COMPS * 2, ROWS + 16, LANES), F32)],
        cost_estimate=pl.CostEstimate(flops=2 * 10**7, bytes_accessed=4_200_000, transcendentals=262144),
        name="inner_log",
    )(disp)


def chunk_kernel(chunks, log_ref, own_ref, left_ref, right_ref, out_ref, side_ref, fix_ref, far_ref, send_ref):
    pad = 8
    strips = lax.axis_size("strip")
    me = lax.axis_index("strip")
    keep_left = (me > 0).astype(F32)
    keep_right = (me < strips - 1).astype(F32)
    for k in range(2):
        side_ref[k, 0:pad, :] = jnp.zeros((pad, LANES), F32)
        side_ref[k, pad + ROWS : 2 * pad + ROWS, :] = jnp.zeros((pad, LANES), F32)
    lane = lax.broadcasted_iota(jnp.int32, (ROWS, LANES), 1)
    low = (lane & 3) < 2
    own = own_ref[...].astype(F32)
    side_ref[0, pad : pad + ROWS, :] = jnp.where(low, left_ref[...].astype(F32), own)
    side_ref[1, pad : pad + ROWS, :] = jnp.where(low, own, right_ref[...].astype(F32))
    for k in range(PER * 2):
        fix_ref[k, 0:pad, :] = jnp.zeros((pad, LANES), F32)
        fix_ref[k, pad + ROWS : 2 * pad + ROWS, :] = jnp.zeros((pad, LANES), F32)
    step = 16
    here = lax.broadcasted_iota(jnp.int32, (step, LANES), 1)

    def body(i, carry):
        base = pl.multiple_of(i * step, step)
        sides = []
        for k in range(2):
            center = side_ref[k, pl.ds(base + pad, step), :]
            dx = (
                side_ref[k, pl.ds(base + pad + 1, step), :]
                - side_ref[k, pl.ds(base + pad - 1, step), :]
            )
            dy = pltpu.roll(center, LANES - 1, 1) - pltpu.roll(center, 1, 1)
            dz = pltpu.roll(center, LANES - 4, 1) - pltpu.roll(center, 4, 1)

            def comps(field):
                return [field] + [pltpu.roll(field, LANES - slot(0, c, 0), 1) for c in (1, 2)]

            sides.append(log_det(comps(dz), comps(dx), comps(dy)))
        left, right = sides
        inner = jnp.where((here & 3) == 2, left, right)
        outer = jnp.where((here & 3) == 1, left * keep_left, right * keep_right)
        far_ref[pl.ds(base, step), :] = encode(outer)
        for s in range(PER):
            for p in range(2):
                at = slot(s, 0, p + 1) + 2
                moved = pltpu.roll(inner, LANES - at, 1)
                whole = jnp.where(
                    (here == 0) | (here == LANES - 1), moved, log_ref[s * 2 + p, pl.ds(base, step), :]
                )
                code = encode(whole)
                fix_ref[s * 2 + p, pl.ds(base + pad, step), :] = code
                target = pl.multiple_of((2 * i + p) * CHUNK, 8) + s * BLOCK
                send_ref[pl.ds(pl.multiple_of(target, 8), step), :] = code
        return carry

    lax.fori_loop(0, ROWS // step, body, 0)
    blocks = ROWS // BLOCK
    far = far_ref[...].T
    for s in range(PER):
        for p in range(2):
            row = p * CHUNK + PER * BLOCK + s * 4
            send_ref[pl.ds(row, blocks, stride=2 * CHUNK), :] = fix_ref[
                s * 2 + p, pl.ds(pad - 1, blocks, stride=BLOCK), :
            ]
            send_ref[pl.ds(row + 1, blocks, stride=2 * CHUNK), :] = fix_ref[
                s * 2 + p, pl.ds(pad + BLOCK, blocks, stride=BLOCK), :
            ]
            for side in range(2):
                line = slot(s, 0, p + 1) + 1 + side
                many = LANES // BLOCK
                for b in range(ROWS // LANES):
                    piece = far[line : line + 1, b * LANES : (b + 1) * LANES]
                    send_ref[
                        pl.ds(row + 2 + side + b * many * 2 * CHUNK, many, stride=2 * CHUNK), :
                    ] = jnp.broadcast_to(piece, (many, LANES))
    per = 4 * CHUNK

    def pack(i, carry):
        at = pl.ds(pl.multiple_of(i * per, 32), per)
        out_ref[at, :] = send_ref[at, :].astype(jnp.int32).astype(jnp.int16)
        return carry

    lax.fori_loop(0, chunks * CHUNK // per, pack, 0)


def chunked(log, own, left, right, chunks):
    return pl.pallas_call(
        functools.partial(chunk_kernel, chunks),
        out_shape=jax.ShapeDtypeStruct((chunks * CHUNK, LANES), jnp.int16),
        scratch_shapes=[
            pltpu.VMEM((2, ROWS + 16, LANES), F32),
            pltpu.VMEM((PER * 2, ROWS + 16, LANES), F32),
            pltpu.VMEM((ROWS, LANES), F32),
            pltpu.VMEM((chunks * CHUNK, LANES), F32),
        ],
        cost_estimate=pl.CostEstimate(flops=10**7, bytes_accessed=2 * 10**6, transcendentals=10**6),
        name="chunked",
    )(log, own, left, right)


def designs_kernel(age_ref, code_ref, perms_ref, out_ref):
    subjects = age_ref.shape[1]
    half = subjects // PER

    def total(v):
        return jnp.sum(v, axis=1, keepdims=True)

    def centred(v):
        return v - total(v) * (1.0 / subjects)

    basis = []
    for raw in (
        (code_ref[...] == 1).astype(F32),
        age_ref[...],
        (code_ref[...] == 2).astype(F32),
    ):
        v = centred(raw)
        for _ in range(2):
            for q in basis:
                v = v - q * total(q * v)
            v = centred(v)
        basis.append(v / jnp.sqrt(total(v * v)))
    lane = lax.broadcasted_iota(jnp.int32, (8, subjects), 1)
    order = PER * (lane % half) + lane // half
    for k, q in enumerate(basis):
        table = jnp.broadcast_to(q, (8, subjects))

        def put(row, values):
            high = values.astype(BF16)
            rest = (values - high.astype(F32)).astype(BF16)
            at = pl.ds(k * GROUP + row, 16)
            out_ref[at, 0:subjects] = high
            out_ref[at, subjects : 2 * subjects] = high
            out_ref[at, 2 * subjects : 3 * subjects] = rest

        for g in range(PERMS // 16):
            two = []
            for h in range(2):
                who = jnp.take_along_axis(perms_ref[g * 16 + h * 8 : g * 16 + h * 8 + 8, :], order, axis=1)
                two.append(jnp.take_along_axis(table, who, axis=1))
            put(g * 16, jnp.concatenate(two, axis=0))
        plain = jnp.take_along_axis(table, order, axis=1)
        put(PERMS, jnp.concatenate([plain, plain], axis=0))


def design_rows(age, codes, perms):
    subjects = age.shape[0]
    return pl.pallas_call(
        designs_kernel,
        out_shape=jax.ShapeDtypeStruct((3 * GROUP, 3 * subjects), BF16),
        cost_estimate=pl.CostEstimate(flops=4 * 10**6, bytes_accessed=800_000, transcendentals=0),
        name="design_rows",
    )(age.reshape(1, subjects), codes.reshape(1, subjects), perms)


def stats_kernel(senders, code_ref, rows_ref, tmap_ref, peaks_ref, value_ref, y_ref, sum_ref, rss_ref, top_ref, best_ref):
    subjects = PER * senders
    lane = lax.broadcasted_iota(jnp.int32, (subjects, LANES), 1)
    shift = (lax.axis_index("subj") // 2 % (LANES // BLOCK)) * BLOCK
    per = 4 * CHUNK

    def unpack(i, carry):
        at = pl.ds(pl.multiple_of(i * per, 32), per)
        value_ref[at, :] = decode(code_ref[at, :].astype(F32))
        return carry

    lax.fori_loop(0, senders * CHUNK // per, unpack, 0)

    def gathered(offsets):
        return jnp.concatenate(
            [value_ref[pl.ds(offset, senders, stride=CHUNK), :] for offset in offsets], axis=0
        )

    def place(block, y):
        y = y - jnp.sum(y, axis=0, keepdims=True) * (1.0 / subjects)
        at = slice(block * LANES, (block + 1) * LANES)
        sum_ref[0:1, at] = jnp.sum(y * y, axis=0, keepdims=True)
        high = y.astype(BF16)
        y_ref[0:subjects, at] = high
        y_ref[subjects : 2 * subjects, at] = (y - high.astype(F32)).astype(BF16)
        y_ref[2 * subjects : 3 * subjects, at] = high

    extra = PER * BLOCK
    for r in range(BLOCK):
        place(r, gathered([r, BLOCK + r]))
    for h in range(2):
        place(BLOCK + h, gathered([extra + h, extra + 4 + h]))
    first = pltpu.roll(gathered([extra + 2, extra + 6]), LANES - shift, 1)
    second = pltpu.roll(gathered([extra + 3, extra + 7]), LANES + BLOCK - shift, 1)
    place(BLOCK + 2, jnp.where(lane < BLOCK, first, jnp.where(lane < 2 * BLOCK, second, 0.0)))

    blocks = BLOCK + 3
    for start in range(0, blocks, 2):
        at = slice(start * LANES, min(start + 2, blocks) * LANES)
        proj = jnp.dot(rows_ref[...], y_ref[:, at], preferred_element_type=F32)
        q1, q2, q3 = (proj[k * GROUP : (k + 1) * GROUP] for k in range(3))
        rss_ref[:, at] = sum_ref[0:1, at] - q1 * q1 - q2 * q2 - q3 * q3
        top_ref[:, at] = q3

    here = lax.broadcasted_iota(jnp.int32, (8, LANES), 1)
    scale = 1.0 / (subjects - 4)

    def pseudo_t(g, r):
        at = pl.ds(pl.multiple_of(g * 8, 8), 8)

        def block(b):
            return rss_ref[at, b * LANES : (b + 1) * LANES]

        mine = block(r)
        above = block(r - 1 if r > 0 else BLOCK)
        below = block(r + 1 if r < BLOCK - 1 else BLOCK + 1)
        ends = jnp.take_along_axis(
            block(BLOCK + 2), jnp.where(here == 0, r, jnp.where(here == LANES - 1, BLOCK + r, 0)), axis=1
        )
        before = jnp.where(here == 0, ends, pltpu.roll(mine, 1, 1))
        after = jnp.where(here == LANES - 1, ends, pltpu.roll(mine, LANES - 1, 1))
        beside = (above + below) + (before + after)
        variance = (0.4 * scale) * mine + (0.15 * scale) * beside + 1e-06
        return top_ref[at, r * LANES : (r + 1) * LANES] * lax.rsqrt(variance)

    def body(g, carry):
        best = jnp.zeros((8, LANES), F32)
        for r in range(BLOCK):
            best = jnp.maximum(best, jnp.abs(pseudo_t(g, r)))
        best_ref[pl.ds(pl.multiple_of(g * 8, 8), 8), :] = best
        return carry

    lax.fori_loop(0, PERMS // 8, body, 0)
    for r in range(BLOCK):
        tmap_ref[r : r + 1, :] = pseudo_t(PERMS // 8, r)[0:1, :]
    peaks_ref[...] = jnp.max(best_ref[...].T, axis=0, keepdims=True)


def block_stats(codes, rows, senders):
    subjects = PER * senders
    columns = (BLOCK + 3) * LANES
    return pl.pallas_call(
        functools.partial(stats_kernel, senders),
        out_shape=(
            jax.ShapeDtypeStruct((BLOCK, LANES), F32),
            jax.ShapeDtypeStruct((1, PERMS), F32),
        ),
        scratch_shapes=[
            pltpu.VMEM((senders * CHUNK, LANES), F32),
            pltpu.VMEM((3 * subjects, columns), BF16),
            pltpu.VMEM((8, columns), F32),
            pltpu.VMEM((GROUP, columns), F32),
            pltpu.VMEM((GROUP, columns), F32),
            pltpu.VMEM((PERMS, LANES), F32),
        ],
        compiler_params=pltpu.CompilerParams(vmem_limit_bytes=32 * 2**20),
        cost_estimate=pl.CostEstimate(flops=2 * 10**9, bytes_accessed=10**6, transcendentals=10**6),
        name="block_stats",
    )(codes, rows)


def on_device(displacement, age, group_codes, perms):
    senders = lax.axis_size("subj")
    strips = lax.axis_size("strip")
    own = strip_edges(displacement)
    left = lax.ppermute(own, "strip", [(i, i + 1) for i in range(strips - 1)])
    right = lax.ppermute(own, "strip", [(i + 1, i) for i in range(strips - 1)])
    log = inner_log(displacement)
    rows = design_rows(age, group_codes, perms)
    sent = chunked(log, own, left, right, senders)
    codes = lax.all_to_all(
        sent.reshape(senders, CHUNK, LANES), "subj", split_axis=0, concat_axis=0, tiled=True
    )
    tested, peaks = block_stats(codes.reshape(senders * CHUNK, LANES), rows, senders)

    odd = lax.axis_index("subj") % 2 == 1
    low, high = tested[: BLOCK // 2], tested[BLOCK // 2 :]
    kept = jnp.where(odd, high, low)
    swapped = lax.ppermute(
        jnp.where(odd, low, high), "subj", [(i, i ^ 1) for i in range(senders)]
    )
    t_map = jnp.stack([jnp.where(odd, swapped, kept), jnp.where(odd, kept, swapped)])

    everyone = senders * strips
    mine = jnp.broadcast_to(peaks.astype(jnp.float16).reshape(1, 2, LANES), (everyone, 2, LANES))
    theirs = lax.all_to_all(mine, ("subj", "strip"), split_axis=0, concat_axis=0, tiled=True)
    return t_map, jnp.max(theirs, axis=0).astype(F32).reshape(PERMS)


def solution(mesh):
    placed = (P("subj", None, None, None, "strip"), P(), P(), P())
    return jax.shard_map(
        on_device,
        mesh=mesh,
        in_specs=placed,
        out_specs=(P(None, "subj", "strip"), P()),
        check_vma=False,
    )
```

time: 496 us -> 97.3 us (0.20); the launches traced: 490 us -> 96.9 us
  local copies, waits for them, and re-layouts: 168 us -> 3.13 us
  blocking collectives: 156 us -> 0 us
  other arithmetic: 96 us -> 1.48 us
  Pallas kernels: 0 us -> 37.2 us
  starting transfers between devices: 52.5 us -> 27.9 us
  waiting for transfers between devices: 6.96 us -> 26.4 us
  matrix products: 7.13 us -> 0 us
    pmax x2 -> x0, blocking collectives: 156 us -> none  [block_peaks(): return lax.pmax(local, ('subj', 'strip'))]
    gather x2 -> x0, local copies, waits for them, and re-layouts: 118 us -> none  [on_device(): design[perms]]
    convert_element_type x9 -> x2, other arithmetic: 55.4 us -> 0.59 us  [the longest x1 0.57 us: on_device(): return (t_map, jnp.max(theirs, axis=0).astype(F32).reshape(PERMS))]
    pallas_call x0 -> x5, Pallas kernels: none -> 37.2 us  [the longest x1 11.3 us: chunked(): pl.pallas_call(functools.partial(chunk_kernel, chunks), out_shape=jax.Sha...]
    ppermute x14 -> x3, starting transfers between devices: 39.4 us -> 5.61 us  [the longest x1 3.94 us: on_device(): left = lax.ppermute(own, 'strip', [(i, i + 1) for i in range(strips - 1)])]
    all_to_all x1 -> x2, waiting for transfers between devices: 0.01 us -> 26.4 us  [the longest x1 14.3 us: on_device(): lax.all_to_all(sent.reshape(senders, CHUNK, LANES), 'subj', split_axis=0,...]
    unnamed x21 -> x6, local copies, waits for them, and re-layouts: 19.7 us -> 2.41 us
    slice x25 -> x0, local copies, waits for them, and re-layouts: 15.6 us -> none  [the longest x9 7 us: extended(): lax.slice_in_dim(cells, cells.shape[dim] - width, cells.shape[dim], axis=...]
  transfers between devices with their start and end apart: 15 -> 5, of which waited for: 5 -> 2; matrix products, arithmetic and copies ran while one was open for 32% -> 1% of each run, Pallas kernels for 0% -> 13%
where the time goes in v1:
time: 97.3 us; the launch traced here: 96.9 us
  Pallas kernels  37.2 us (38%)
  starting transfers between devices  27.9 us (29%)
  waiting for transfers between devices  26.4 us (27%)
  local copies, waits for them, and re-layouts  3.13 us (3%)
  other arithmetic  1.48 us (2%)
    all_to_all x1, waiting for transfers between devices, on_device(): lax.all_to_all(sent.reshape(senders, CHUNK, LANES), 'subj', split_axis=0,...  14.3 us
    all_to_all x1, starting transfers between devices, on_device(): lax.all_to_all(sent.reshape(senders, CHUNK, LANES), 'subj', split_axis=0,...  12.6 us
    all_to_all x1, waiting for transfers between devices, on_device(): lax.all_to_all(mine, ('subj', 'strip'), split_axis=0, concat_axis=0, tile...  12.1 us
    pallas_call x1, Pallas kernels, chunked(): pl.pallas_call(functools.partial(chunk_kernel, chunks), out_shape=jax.Sha...  11.3 us
    all_to_all x1, starting transfers between devices, on_device(): lax.all_to_all(mine, ('subj', 'strip'), split_axis=0, concat_axis=0, tile...  9.73 us
    pallas_call x1, Pallas kernels, block_stats(): pl.pallas_call(functools.partial(stats_kernel, senders), out_shape=(jax.S...  8.1 us
    pallas_call x1, Pallas kernels, inner_log(): pl.pallas_call(inner_kernel, grid=(PER,), in_specs=[pl.BlockSpec((1, COMP...  6.6 us
    pallas_call x1, Pallas kernels, design_rows(): pl.pallas_call(designs_kernel, out_shape=jax.ShapeDtypeStruct((3 * GROUP,...  5.83 us
  transfers between devices with their start and end apart: 5, of which 2 were waited for; matrix products, arithmetic and copies ran while one was open for 1% of the time, Pallas kernels for 13%

profile of v1, /device:TPU:1, one launch (start us, length us, event | category | flops | bytes accessed | tf_op | source)
XLA Modules:
  0.0 96.9 jit_solution(1357718466628591980)
XLA Ops:
  0.6 5.4 %strip_edges.1.own_ref = bf16[512,128]{1,0:T(8,128)(2,1)} custom-call(bf16[2,3,4,512,128]{4,3,2,1,0:T(8,128)(2,1)} %disp_ref.3), custom_call_target="tpu_custom_call" | custom-call | flops 1000000 | bytes 3200000 | tf_op jit(solution)/shard_map/strip_edges/pallas_call | solution.py:70
  6.0 3.9 %collective-permute-start = (bf16[512,128]{1,0:T(8,128)(2,1)}, bf16[512,128]{1,0:T(8,128)(2,1)S(1)}, u32[]{:S(2)}, u32[]{:S(2)}) collective-permute-start(bf16[512,128]{1,0:T(8,128)(2,1)} %strip_edges.1.own_ref), channel_id=1, source_target_pairs={{0,1},{1,2},{2,3},{4,5},{5,6},{6,7},{8,9},{9,10},{10,11},{12,13},{... | collective-permute-start | bytes 393224 | tf_op jit(solution)/shard_map/ppermute | solution.py:380
  10.0 1.3 %collective-permute-start.1 = (bf16[512,128]{1,0:T(8,128)(2,1)}, bf16[512,128]{1,0:T(8,128)(2,1)S(1)}, u32[]{:S(2)}, u32[]{:S(2)}) collective-permute-start(bf16[512,128]{1,0:T(8,128)(2,1)} %strip_edges.1.own_ref), channel_id=1, source_target_pairs={{1,0},{2,1},{3,2},{5,4},{6,5},{7,6},{9,8},{10,9},{11,10},{13,12},{... | collective-permute-start | bytes 393224 | tf_op jit(solution)/shard_map/ppermute | solution.py:381
  11.3 6.6 %inner_log.1.log_ref = f32[4,512,128]{2,1,0:T(8,128)} custom-call(bf16[2,3,4,512,128]{4,3,2,1,0:T(8,128)(2,1)} %disp_ref.3), custom_call_target="tpu_custom_call" | custom-call | flops 20000000 | bytes 4200000 | tf_op jit(solution)/shard_map/inner_log/pallas_call | solution.py:110
  17.9 0.0 collective-permute-done.left_ref
  17.9 0.0 copy-start.1
  17.9 0.0 collective-permute-done.1.right_ref
  17.9 0.7 copy-done.1
  18.5 0.0 copy-start.2
  18.6 0.7 copy-done.2
  19.2 11.3 %chunked.1 = s16[2560,128]{1,0:T(8,128)(2,1)} custom-call(f32[4,512,128]{2,1,0:T(8,128)} %inner_log.1.log_ref, bf16[512,128]{1,0:T(8,128)(2,1)} %strip_edges.1.own_ref, bf16[512,128]{1,0:T(8,128)(2,1)} %copy-done.1, bf16[512,128]{1,0:T(8,128)(2,1)} %copy-done.2), custom_call_target="tpu_custom_call" | custom-call | flops 10000000 | bytes 2000000 | tf_op jit(solution)/shard_map/chunked/pallas_call | solution.py:206
  30.5 12.6 %all-to-all-start = ((s16[64,40,128]{2,1,0:T(8,128)(2,1)}), s16[64,40,128]{2,1,0:T(8,128)(2,1)S(1)}, u32[]{:S(2)}, u32[]{:S(2)}) async-start(s16[64,40,128]{2,1,0:T(8,128)(2,1)} %bitcast.13), calls=%async_computation | async-start | bytes 1310720 | tf_op jit(solution)/shard_map/all_to_all | solution.py:385
  43.1 5.8 %design_rows.1.rows_ref = bf16[816,384]{1,0:T(8,128)(2,1)} custom-call(f32[1,128]{1,0:T(1,128)} %bitcast.14, s32[1,128]{1,0:T(1,128)} %bitcast.15, s32[256,128]{1,0:T(8,128)} %perms_ref.1), custom_call_target="tpu_custom_call" | custom-call | flops 4000000 | bytes 800000 | tf_op jit(solution)/shard_map/design_rows/pallas_call | solution.py:267
  49.0 14.3 %all-to-all-done = s16[64,40,128]{2,1,0:T(8,128)(2,1)S(1)} async-done(((s16[64,40,128]{2,1,0:T(8,128)(2,1)}), s16[64,40,128]{2,1,0:T(8,128)(2,1)S(1)}, u32[]{:S(2)}, u32[]{:S(2)}) %all-to-all-start) | async-done | bytes 655392 | tf_op jit(solution)/shard_map/all_to_all | solution.py:385
  63.2 1.1 %copy-done = bf16[816,384]{1,0:T(8,128)(2,1)S(1)} copy-done((bf16[816,384]{1,0:T(8,128)(2,1)S(1)}, bf16[816,384]{1,0:T(8,128)(2,1)}, u32[]{:S(2)}) %copy-start) | copy-done | bytes 626712
  64.3 8.1 %block_stats.1 = (f32[16,128]{1,0:T(8,128)S(1)}, f32[1,256]{1,0:T(1,128)S(1)}) custom-call(s16[2560,128]{1,0:T(8,128)(2,1)S(1)} %bitcast.12, bf16[816,384]{1,0:T(8,128)(2,1)S(1)} %copy-done), custom_call_target="tpu_custom_call" | custom-call | flops 2000000000 | bytes 1000000 | tf_op jit(solution)/shard_map/block_stats/pallas_call | solution.py:356
  72.4 0.4 collective-permute-start.2
  72.8 0.7 broadcast_in_dim.8
  73.6 9.7 %all-to-all-start.1 = ((f16[256,2,128]{2,1,0:T(2,128)(2,1)}), f16[256,2,128]{2,1,0:T(2,128)(2,1)S(1)}, u32[]{:S(2)}, u32[]{:S(2)}) async-start(f16[256,2,128]{2,1,0:T(2,128)(2,1)} %broadcast_in_dim.8), calls=%async_computation.1 | async-start | bytes 262144 | tf_op jit(solution)/shard_map/all_to_all | solution.py:400
  83.3 0.0 collective-permute-done.2
  83.3 0.6 pad_maximum_fusion
  83.9 12.1 %all-to-all-done.1 = f16[256,2,128]{2,1,0:T(2,128)(2,1)S(1)} async-done(((f16[256,2,128]{2,1,0:T(2,128)(2,1)}), f16[256,2,128]{2,1,0:T(2,128)(2,1)S(1)}, u32[]{:S(2)}, u32[]{:S(2)}) %all-to-all-start.1) | async-done | bytes 131104 | tf_op jit(solution)/shard_map/all_to_all | solution.py:400
  96.0 0.3 reduce_max.9
  96.3 0.6 bitcast_convert_fusion
  (4 shorter events, 0.0 us)
Async XLA Ops:
  6.0 11.9 %collective-permute-start = (bf16[512,128]{1,0:T(8,128)(2,1)}, bf16[512,128]{1,0:T(8,128)(2,1)S(1)}, u32[]{:S(2)}, u32[]{:S(2)}) collective-permute-start(bf16[512,128]{1,0:T(8,128)(2,1)} %strip_edges.1.own_ref), channel_id=1, source_target_pairs={{0,1},{1,2},{2,3},{4,5},{5,6},{6,7},{8,9},{9,10},{10,11},{12,13},{... | collective-permute-start | bytes 393224 | tf_op jit(solution)/shard_map/ppermute | solution.py:380
  10.0 7.9 %collective-permute-start.1 = (bf16[512,128]{1,0:T(8,128)(2,1)}, bf16[512,128]{1,0:T(8,128)(2,1)S(1)}, u32[]{:S(2)}, u32[]{:S(2)}) collective-permute-start(bf16[512,128]{1,0:T(8,128)(2,1)} %strip_edges.1.own_ref), channel_id=1, source_target_pairs={{1,0},{2,1},{3,2},{5,4},{6,5},{7,6},{9,8},{10,9},{11,10},{13,12},{... | collective-permute-start | bytes 393224 | tf_op jit(solution)/shard_map/ppermute | solution.py:381
  17.9 0.7 copy-start.1
  18.5 0.7 copy-start.2
  30.5 32.7 %all-to-all-start = ((s16[64,40,128]{2,1,0:T(8,128)(2,1)}), s16[64,40,128]{2,1,0:T(8,128)(2,1)S(1)}, u32[]{:S(2)}, u32[]{:S(2)}) async-start(s16[64,40,128]{2,1,0:T(8,128)(2,1)} %bitcast.13), calls=%async_computation | async-start | bytes 1310720 | tf_op jit(solution)/shard_map/all_to_all | solution.py:385
  63.2 1.1 %copy-start = (bf16[816,384]{1,0:T(8,128)(2,1)S(1)}, bf16[816,384]{1,0:T(8,128)(2,1)}, u32[]{:S(2)}) copy-start(bf16[816,384]{1,0:T(8,128)(2,1)} %design_rows.1.rows_ref) | copy-start | bytes 1880068
  72.4 10.9 %collective-permute-start.2 = (f32[8,128]{1,0:T(8,128)S(1)}, f32[8,128]{1,0:T(8,128)S(1)}, u32[]{:S(2)}, u32[]{:S(2)}) collective-permute-start(f32[8,128]{1,0:T(8,128)S(1)} %slice_select_fusion.1), channel_id=1, source_target_pairs={{0,4},{4,0},{8,12},{12,8},{16,20},{20,16},{24,28},{28,24},{32,36},... | collective-permute-start | bytes 12296 | tf_op jit(solution)/shard_map/ppermute | solution.py:393
  73.6 22.5 %all-to-all-start.1 = ((f16[256,2,128]{2,1,0:T(2,128)(2,1)}), f16[256,2,128]{2,1,0:T(2,128)(2,1)S(1)}, u32[]{:S(2)}, u32[]{:S(2)}) async-start(f16[256,2,128]{2,1,0:T(2,128)(2,1)} %broadcast_in_dim.8), calls=%async_computation.1 | async-start | bytes 262144 | tf_op jit(solution)/shard_map/all_to_all | solution.py:400

commit v2 on v1

v2 whole, which is shorter than its diff:
```python
import functools

import jax
import jax.numpy as jnp
from jax import lax
from jax.experimental import pallas as pl
from jax.experimental.pallas import tpu as pltpu
from jax.sharding import PartitionSpec as P

F32, BF16, I16 = jnp.float32, jnp.bfloat16, jnp.int16
LANES = 128
ROWS = 512
BLOCK = 16
MAIN, TAIL = 32, 8
CHUNK = MAIN + TAIL
PAIR = 2 * CHUNK
PER = 2
COMPS, PLANES = 3, 4
PERMS, GROUP = 256, 272
REACH = 0.6
LEVELS = 32767.0
CENTRE = 0.4 / 0.15
FLOOR = 1e-06 / (CENTRE + 4.0)


def encode(y):
    half = y * lax.rsqrt(jnp.maximum(jnp.abs(y), 1e-30))
    fourth = half * lax.rsqrt(jnp.maximum(jnp.abs(half), 1e-15))
    shift = 1.5 * 2.0**23
    return (fourth * (LEVELS / REACH**0.25) + shift) - shift


def decode(code):
    part = code * (REACH**0.25 / LEVELS)
    return (part * jnp.abs(part)) * (part * part)


def packed(code):
    return code.astype(jnp.int32).astype(I16)


def log_det(dz, dx, dy):
    j00, j01, j02 = 2.0 + dz[0], dx[0], dy[0]
    j10, j11, j12 = dz[1], 2.0 + dx[1], dy[1]
    j20, j21, j22 = dz[2], dx[2], 2.0 + dy[2]
    det = (
        j00 * (j11 * j22 - j12 * j21)
        - j01 * (j10 * j22 - j12 * j20)
        + j02 * (j10 * j21 - j11 * j20)
    )
    return jnp.log(det * 0.125)


def edges_kernel(disp_ref, low_ref, high_ref):
    row = lax.broadcasted_iota(jnp.int32, (32, 2 * LANES), 0)
    lane = lax.broadcasted_iota(jnp.int32, (32, 2 * LANES), 1)
    column = jnp.where(row < 16, row // 8, row // 8 - 2 + LANES - 2)
    for c in range(COMPS):
        acc = jnp.zeros((32, low_ref.shape[1]), F32)
        for q in range(PLANES):
            pick = ((row % 8 == 2 * q + lane // LANES) & (lane % LANES == column)).astype(F32)
            both = jnp.concatenate([disp_ref[0, c, q], disp_ref[1, c, q]], axis=1)
            acc = acc + lax.dot_general(
                pick.astype(BF16), both, (((1,), (1,)), ((), ())), preferred_element_type=F32
            )
        low_ref[c * 16 : c * 16 + 16, :] = acc[0:16].astype(BF16)
        high_ref[c * 16 : c * 16 + 16, :] = acc[16:32].astype(BF16)


def strip_edges(disp):
    rows = 256
    out = jax.ShapeDtypeStruct((COMPS * 16, ROWS), BF16)
    return pl.pallas_call(
        edges_kernel,
        grid=(ROWS // rows,),
        in_specs=[pl.BlockSpec((PER, COMPS, PLANES, rows, LANES), lambda i: (0, 0, 0, i, 0))],
        out_specs=[pl.BlockSpec((COMPS * 16, rows), lambda i: (0, i))] * 2,
        out_shape=(out, out),
        compiler_params=pltpu.CompilerParams(vmem_limit_bytes=8 * 2**20),
        cost_estimate=pl.CostEstimate(flops=10**8, bytes_accessed=3_200_000, transcendentals=0),
        name="strip_edges",
    )(disp)


def inner_kernel(disp_ref, out_ref, beside_ref, field_ref, pad_ref, code_ref, in_sem):
    pad, step, parts = 8, 16, 4
    rows = ROWS // parts
    zeros = jnp.zeros((pad, LANES), F32)
    copies = [
        [
            pltpu.make_async_copy(
                disp_ref.at[s, :, :, h * rows : (h + 1) * rows, :],
                field_ref.at[s, :, :, h * rows : (h + 1) * rows, :],
                in_sem.at[s, h],
            )
            for h in range(parts)
        ]
        for s in range(PER)
    ]
    for s in range(PER):
        for h in range(parts):
            copies[s][h].start()
    for k in range(2):
        code_ref[k, 0:pad, :] = zeros
        code_ref[k, pad + ROWS : 2 * pad + ROWS, :] = zeros
        for c in range(COMPS):
            pad_ref[k, c, 0:pad, :] = zeros
            pad_ref[k, c, pad + ROWS : 2 * pad + ROWS, :] = zeros

    for s in range(PER):
        for h in range(parts + 1):
            if h < parts:
                copies[s][h].wait()
                for p in range(2):
                    for c in range(COMPS):
                        pad_ref[p, c, pad + h * rows : pad + (h + 1) * rows, :] = field_ref[
                            s, c, 1 + p, h * rows : (h + 1) * rows, :
                        ].astype(F32)
            if h > 0:

                def body(i, carry):
                    base = pl.multiple_of(i * step, step)
                    for p in range(2):
                        dz, dx, dy = [], [], []
                        for c in range(COMPS):
                            up = field_ref[s, c, p + 2, pl.ds(base, step), :].astype(F32)
                            down = field_ref[s, c, p, pl.ds(base, step), :].astype(F32)
                            dz.append(up - down)
                            center = pad_ref[p, c, pl.ds(base + pad, step), :]
                            dx.append(
                                pad_ref[p, c, pl.ds(base + pad + 1, step), :]
                                - pad_ref[p, c, pl.ds(base + pad - 1, step), :]
                            )
                            dy.append(pltpu.roll(center, LANES - 1, 1) - pltpu.roll(center, 1, 1))
                        code = encode(log_det(dz, dx, dy))
                        code_ref[p, pl.ds(base + pad, step), :] = code
                        out_ref[i, 48 * p + 16 * s : 48 * p + 16 * s + 16, :] = packed(code)
                    return carry

                many = rows // step
                lax.fori_loop((h - 1) * many, h * many, body, 0, unroll=many)
        blocks = ROWS // BLOCK
        for p in range(2):
            beside_ref[2 * p + s, 0] = code_ref[p, pl.ds(pad - 1, blocks, stride=BLOCK), :]
            beside_ref[2 * p + s, 1] = code_ref[p, pl.ds(pad + BLOCK, blocks, stride=BLOCK), :]


def inner_codes(disp):
    blocks = ROWS // BLOCK
    return pl.pallas_call(
        inner_kernel,
        in_specs=[pl.BlockSpec(memory_space=pl.ANY)],
        out_shape=(
            jax.ShapeDtypeStruct((blocks, PAIR, LANES), I16),
            jax.ShapeDtypeStruct((2 * PER, 2, blocks, LANES), F32),
        ),
        scratch_shapes=[
            pltpu.VMEM((PER, COMPS, PLANES, ROWS, LANES), BF16),
            pltpu.VMEM((2, COMPS, ROWS + 16, LANES), F32),
            pltpu.VMEM((2, ROWS + 32, LANES), F32),
            pltpu.SemaphoreType.DMA((PER, 4)),
        ],
        compiler_params=pltpu.CompilerParams(vmem_limit_bytes=16 * 2**20),
        cost_estimate=pl.CostEstimate(flops=2 * 10**7, bytes_accessed=4_200_000, transcendentals=262144),
        name="inner_codes",
    )(disp)


def tail_kernel(low_ref, high_ref, left_ref, right_ref, beside_ref, chunk_ref, out_ref, pad_ref, side_ref, tail_ref, send_ref, sem):
    del chunk_ref
    strips = lax.axis_size("strip")
    me = lax.axis_index("strip")
    keep_left = (me > 0).astype(F32)
    keep_right = (me < strips - 1).astype(F32)
    lane = lax.broadcasted_iota(jnp.int32, (8, ROWS), 1)

    def columns(ref):
        return [[ref[16 * c + 8 * e : 16 * c + 8 * e + 8, :] for e in range(2)] for c in range(COMPS)]

    def codes(around):
        dz, dx, dy = [], [], []
        for before, center, after in around:
            dz.append(pltpu.roll(center, 6, 0) - pltpu.roll(center, 2, 0))
            dx.append(
                jnp.where(lane == ROWS - 1, 0.0, pltpu.roll(center, ROWS - 1, 1))
                - jnp.where(lane == 0, 0.0, pltpu.roll(center, 1, 1))
            )
            dy.append(after - before)
        return encode(log_det(dz, dx, dy))

    low, high, left, right = (
        columns(ref[...].astype(F32)) for ref in (low_ref, high_ref, left_ref, right_ref)
    )
    wide_left = [left[c] + low[c] for c in range(COMPS)]
    wide_right = [high[c] + right[c] for c in range(COMPS)]
    four = [
        codes([w[0:3] for w in wide_left]) * keep_left,
        codes([w[1:4] for w in wide_left]),
        codes([w[0:3] for w in wide_right]),
        codes([w[1:4] for w in wide_right]) * keep_right,
    ]
    zeros = jnp.zeros((8, LANES), F32)
    for k in range(4):
        pad_ref[k, :, 0:LANES] = zeros
        pad_ref[k, :, LANES : LANES + ROWS] = four[k]
        pad_ref[k, :, LANES + ROWS : 2 * LANES + ROWS] = zeros
    here = lax.broadcasted_iota(jnp.int32, (8, LANES), 1)
    blocks = ROWS // BLOCK
    for j in range(blocks):
        start = LANES + j * BLOCK - 1
        line = zeros
        for k in range(4):
            window, offset = start // LANES, start % LANES
            first = pltpu.roll(
                pad_ref[k, :, window * LANES : (window + 1) * LANES], (32 * k - offset) % LANES, 1
            )
            if offset + 18 > LANES:
                second = pltpu.roll(
                    pad_ref[k, :, (window + 1) * LANES : (window + 2) * LANES], (32 * k - offset) % LANES, 1
                )
                first = jnp.where(here - 32 * k < LANES - offset, first, second)
            line = first if k == 0 else jnp.where(here < 32 * k, line, first)
        side_ref[j * 8 : j * 8 + 8, :] = line
    for p in range(2):
        for s in range(PER):
            row = TAIL * p + 4 * s
            for h in range(2):
                tail_ref[pl.ds(row + h, blocks, stride=2 * TAIL), :] = beside_ref[2 * p + s, h]
            tail_ref[pl.ds(row + 2, blocks, stride=2 * TAIL), :] = side_ref[
                pl.ds(2 + 2 * p + s, blocks, stride=8), :
            ]
            tail_ref[pl.ds(row + 3, blocks, stride=2 * TAIL), :] = jnp.zeros((blocks, LANES), F32)
    send_ref[...] = packed(tail_ref[0 : blocks * 2 * TAIL, :]).reshape(blocks, 2 * TAIL, LANES)
    copy = pltpu.make_async_copy(send_ref, out_ref.at[:, MAIN : MAIN + 2 * TAIL, :], sem)
    copy.start()
    copy.wait()


def with_tails(low, high, left, right, beside, chunks):
    blocks = ROWS // BLOCK
    vmem = pl.BlockSpec(memory_space=pltpu.VMEM)
    anywhere = pl.BlockSpec(memory_space=pl.ANY)
    return pl.pallas_call(
        tail_kernel,
        in_specs=[vmem] * 5 + [anywhere],
        out_specs=anywhere,
        out_shape=jax.ShapeDtypeStruct(chunks.shape, chunks.dtype),
        input_output_aliases={5: 0},
        scratch_shapes=[
            pltpu.VMEM((4, 8, ROWS + 2 * LANES), F32),
            pltpu.VMEM((blocks * 8 + 8, LANES), F32),
            pltpu.VMEM((blocks * 2 * TAIL + 16, LANES), F32),
            pltpu.VMEM((blocks, 2 * TAIL, LANES), I16),
            pltpu.SemaphoreType.DMA,
        ],
        compiler_params=pltpu.CompilerParams(vmem_limit_bytes=8 * 2**20),
        cost_estimate=pl.CostEstimate(flops=10**6, bytes_accessed=5 * 10**5, transcendentals=5 * 10**4),
        name="with_tails",
    )(low, high, left, right, beside, chunks)


def designs_kernel(age_ref, code_ref, perms_ref, out_ref):
    subjects = age_ref.shape[1]
    half = subjects // PER

    def total(v):
        return jnp.sum(v, axis=1, keepdims=True)

    def centred(v):
        return v - total(v) * (1.0 / subjects)

    basis = []
    for raw in (
        (code_ref[...] == 1).astype(F32),
        age_ref[...],
        (code_ref[...] == 2).astype(F32),
    ):
        v = centred(raw)
        for _ in range(2):
            for q in basis:
                v = v - q * total(q * v)
            v = centred(v)
        basis.append(v / jnp.sqrt(total(v * v)))
    scale = (0.15 / (subjects - 4)) ** 0.5
    lane = lax.broadcasted_iota(jnp.int32, (8, subjects), 1)
    order = PER * (lane % half) + lane // half
    for k, q in enumerate(basis):
        table = jnp.broadcast_to(q * scale, (8, subjects))

        def put(row, values):
            high = values.astype(BF16)
            rest = (values - high.astype(F32)).astype(BF16)
            at = pl.ds(k * GROUP + row, 16)
            out_ref[at, 0:subjects] = high
            out_ref[at, subjects : 2 * subjects] = high
            out_ref[at, 2 * subjects : 3 * subjects] = rest

        for g in range(PERMS // 16):
            two = []
            for h in range(2):
                who = jnp.take_along_axis(perms_ref[g * 16 + h * 8 : g * 16 + h * 8 + 8, :], order, axis=1)
                two.append(jnp.take_along_axis(table, who, axis=1))
            put(g * 16, jnp.concatenate(two, axis=0))
        plain = jnp.take_along_axis(table, order, axis=1)
        put(PERMS, jnp.concatenate([plain, plain], axis=0))


def design_rows(age, codes, perms):
    subjects = age.shape[0]
    return pl.pallas_call(
        designs_kernel,
        out_shape=jax.ShapeDtypeStruct((3 * GROUP, 3 * subjects), BF16),
        compiler_params=pltpu.CompilerParams(vmem_limit_bytes=8 * 2**20),
        cost_estimate=pl.CostEstimate(flops=4 * 10**6, bytes_accessed=800_000, transcendentals=0),
        name="design_rows",
    )(age.reshape(1, subjects), codes.reshape(1, subjects), perms)


def stats_kernel(senders, code_ref, rows_ref, tmap_ref, peaks_ref, value_ref, y_ref, sum_ref, rss_ref, top_ref, best_ref):
    subjects = PER * senders
    lane = lax.broadcasted_iota(jnp.int32, (subjects, LANES), 1)
    odd = lax.axis_index("subj") % 2
    main = odd * TAIL
    tail = (1 - odd) * MAIN
    per = 4 * CHUNK

    def unpack(i, carry):
        at = pl.ds(pl.multiple_of(i * per, 32), per)
        value_ref[at, :] = decode(code_ref[at, :].astype(F32))
        return carry

    lax.fori_loop(0, senders * CHUNK // per, unpack, 0)

    def gathered(offsets):
        return jnp.concatenate(
            [value_ref[pl.ds(offset, senders, stride=CHUNK), :] for offset in offsets], axis=0
        )

    def place(block, y):
        y = y - jnp.sum(y, axis=0, keepdims=True) * (1.0 / subjects)
        at = pl.ds(pl.multiple_of(block * LANES, LANES), LANES)
        sum_ref[0:1, at] = jnp.sum(y * y, axis=0, keepdims=True) * (0.15 / (subjects - 4)) + FLOOR
        high = y.astype(BF16)
        y_ref[0:subjects, at] = high
        y_ref[subjects : 2 * subjects, at] = (y - high.astype(F32)).astype(BF16)
        y_ref[2 * subjects : 3 * subjects, at] = high

    sides = gathered([tail + 2, tail + 6])

    def mended(y, r):
        index = jnp.where(lane == 0, 33 + r, jnp.where(lane == LANES - 1, 65 + r, 0))
        ends = jnp.take_along_axis(sides, index, axis=1)
        return jnp.where((lane == 0) | (lane == LANES - 1), ends, y)

    def place_row(r, carry):
        place(r, mended(gathered([main + r, main + BLOCK + r]), r))
        return carry

    lax.fori_loop(0, BLOCK, place_row, 0, unroll=8)
    place(BLOCK, mended(gathered([tail, tail + 4]), -1))
    place(BLOCK + 1, mended(gathered([tail + 1, tail + 5]), BLOCK))
    place(BLOCK + 2, sides)

    blocks = BLOCK + 3
    for start in range(0, blocks, 2):
        at = slice(start * LANES, min(start + 2, blocks) * LANES)
        proj = jnp.dot(rows_ref[...], y_ref[:, at], preferred_element_type=F32)
        q1, q2, q3 = (proj[k * GROUP : (k + 1) * GROUP] for k in range(3))
        rss_ref[:, at] = sum_ref[0:1, at] - q1 * q1 - q2 * q2 - q3 * q3
        top_ref[:, at] = q3

    here = lax.broadcasted_iota(jnp.int32, (8, LANES), 1)
    unscale = ((subjects - 4) / 0.15) ** 0.5

    def pseudo_t(g, r):
        at = pl.ds(pl.multiple_of(g * 8, 8), 8)

        def block(b):
            return rss_ref[at, b * LANES : (b + 1) * LANES]

        mine = block(r)
        above = block(r - 1 if r > 0 else BLOCK)
        below = block(r + 1 if r < BLOCK - 1 else BLOCK + 1)
        ends = jnp.take_along_axis(
            block(BLOCK + 2), jnp.where(here == 0, 1 + r, jnp.where(here == LANES - 1, 97 + r, 0)), axis=1
        )
        before = jnp.where(here == 0, ends, pltpu.roll(mine, 1, 1))
        after = jnp.where(here == LANES - 1, ends, pltpu.roll(mine, LANES - 1, 1))
        beside = (above + below) + (before + after)
        variance = CENTRE * mine + beside
        return top_ref[at, r * LANES : (r + 1) * LANES] * lax.rsqrt(variance)

    def body(g, carry):
        best = jnp.zeros((8, LANES), F32)
        for r in range(BLOCK):
            best = jnp.maximum(best, jnp.abs(pseudo_t(g, r)))
        best_ref[pl.ds(pl.multiple_of(g * 8, 8), 8), :] = best
        return carry

    lax.fori_loop(0, PERMS // 8, body, 0, unroll=8)
    for r in range(BLOCK):
        tmap_ref[r : r + 1, :] = pseudo_t(PERMS // 8, r)[0:1, :] * unscale
    peaks_ref[...] = jnp.max(best_ref[...].T, axis=0, keepdims=True) * unscale


def block_stats(codes, rows, senders):
    subjects = PER * senders
    columns = (BLOCK + 3) * LANES
    return pl.pallas_call(
        functools.partial(stats_kernel, senders),
        out_shape=(
            jax.ShapeDtypeStruct((BLOCK, LANES), F32),
            jax.ShapeDtypeStruct((1, PERMS), F32),
        ),
        scratch_shapes=[
            pltpu.VMEM((senders * CHUNK + CHUNK, LANES), F32),
            pltpu.VMEM((3 * subjects, columns), BF16),
            pltpu.VMEM((8, columns), F32),
            pltpu.VMEM((GROUP, columns), F32),
            pltpu.VMEM((GROUP, columns), F32),
            pltpu.VMEM((PERMS, LANES), F32),
        ],
        compiler_params=pltpu.CompilerParams(vmem_limit_bytes=24 * 2**20),
        cost_estimate=pl.CostEstimate(flops=2 * 10**9, bytes_accessed=10**6, transcendentals=10**6),
        name="block_stats",
    )(codes, rows)


def on_device(displacement, age, group_codes, perms):
    senders = lax.axis_size("subj")
    strips = lax.axis_size("strip")
    low, high = strip_edges(displacement)
    left = lax.ppermute(high, "strip", [(i, i + 1) for i in range(strips - 1)])
    right = lax.ppermute(low, "strip", [(i + 1, i) for i in range(strips - 1)])
    chunks, beside = inner_codes(displacement)
    rows = design_rows(age, group_codes, perms)
    sent = with_tails(low, high, left, right, beside, chunks)
    codes = lax.all_to_all(
        sent.reshape(senders, CHUNK, LANES), "subj", split_axis=0, concat_axis=0, tiled=True
    )
    tested, peaks = block_stats(codes.reshape(senders * CHUNK, LANES), rows, senders)

    odd = lax.axis_index("subj") % 2 == 1
    low, high = tested[: BLOCK // 2], tested[BLOCK // 2 :]
    kept = jnp.where(odd, high, low)
    swapped = lax.ppermute(
        jnp.where(odd, low, high), "subj", [(i, i ^ 1) for i in range(senders)]
    )
    t_map = jnp.stack([jnp.where(odd, swapped, kept), jnp.where(odd, kept, swapped)])

    everyone = senders * strips
    mine = jnp.broadcast_to(peaks.astype(jnp.float16).reshape(1, 2, LANES), (everyone, 2, LANES))
    theirs = lax.all_to_all(mine, ("subj", "strip"), split_axis=0, concat_axis=0, tiled=True)
    return t_map, jnp.max(theirs, axis=0).astype(F32).reshape(PERMS)


def solution(mesh):
    placed = (P("subj", None, None, None, "strip"), P(), P(), P())
    return jax.shard_map(
        on_device,
        mesh=mesh,
        in_specs=placed,
        out_specs=(P(None, "subj", "strip"), P()),
        check_vma=False,
    )
```

time: 97.3 us -> 77.9 us (0.80)
  Pallas kernels: 37.2 us -> 16.3 us
  waiting for transfers between devices: 26.4 us -> 28.2 us
    pallas_call x2, Pallas kernels: 17.9 us -> 4.74 us  [the longest x1 3.59 us: inner_codes(): pl.pallas_call(inner_kernel, in_specs=[pl.BlockSpec(memory_space=pl.ANY)]...]
    pallas_call x1, Pallas kernels: 5.4 us -> 1.4 us  [strip_edges(): pl.pallas_call(edges_kernel, grid=(ROWS // rows,), in_specs=[pl.BlockSpec...]
    pallas_call x1, Pallas kernels: 5.83 us -> 3.96 us  [design_rows(): pl.pallas_call(designs_kernel, out_shape=jax.ShapeDtypeStruct((3 * GROUP,...]
    pallas_call x1, Pallas kernels: 8.1 us -> 6.24 us  [block_stats(): pl.pallas_call(functools.partial(stats_kernel, senders), out_shape=(jax.S...]
    all_to_all x1, waiting for transfers between devices: 14.3 us -> 16.1 us  [on_device(): lax.all_to_all(sent.reshape(senders, CHUNK, LANES), 'subj', split_axis=0,...]
    all_to_all x1, starting transfers between devices: 12.6 us -> 13.7 us  [on_device(): lax.all_to_all(sent.reshape(senders, CHUNK, LANES), 'subj', split_axis=0,...]
    all_to_all x1, starting transfers between devices: 9.73 us -> 8.68 us  [on_device(): lax.all_to_all(mine, ('subj', 'strip'), split_axis=0, concat_axis=0, tile...]
    unnamed x6 -> x10, local copies, waits for them, and re-layouts: 2.41 us -> 1.91 us
  transfers between devices with their start and end apart: 5 -> 5, of which waited for: 2 -> 2; matrix products, arithmetic and copies ran while one was open for 1% -> 2% of each run, Pallas kernels for 13% -> 10%
where the time goes in v2:
time: 77.9 us; the launch traced here: 77.6 us
  waiting for transfers between devices  28.2 us (36%)
  starting transfers between devices  28.1 us (36%)
  Pallas kernels  16.3 us (21%)
  local copies, waits for them, and re-layouts  2.62 us (3%)
  other arithmetic  1.48 us (2%)
  between operations  0.82 us (1%)
    all_to_all x1, waiting for transfers between devices, on_device(): lax.all_to_all(sent.reshape(senders, CHUNK, LANES), 'subj', split_axis=0,...  16.1 us
    all_to_all x1, starting transfers between devices, on_device(): lax.all_to_all(sent.reshape(senders, CHUNK, LANES), 'subj', split_axis=0,...  13.7 us
    all_to_all x1, waiting for transfers between devices, on_device(): lax.all_to_all(mine, ('subj', 'strip'), split_axis=0, concat_axis=0, tile...  12.1 us
    all_to_all x1, starting transfers between devices, on_device(): lax.all_to_all(mine, ('subj', 'strip'), split_axis=0, concat_axis=0, tile...  8.68 us
    pallas_call x1, Pallas kernels, block_stats(): pl.pallas_call(functools.partial(stats_kernel, senders), out_shape=(jax.S...  6.24 us
    ppermute x1, starting transfers between devices, on_device(): left = lax.ppermute(high, 'strip', [(i, i + 1) for i in range(strips - 1)])  4.08 us
    pallas_call x1, Pallas kernels, design_rows(): pl.pallas_call(designs_kernel, out_shape=jax.ShapeDtypeStruct((3 * GROUP,...  3.96 us
    pallas_call x1, Pallas kernels, inner_codes(): pl.pallas_call(inner_kernel, in_specs=[pl.BlockSpec(memory_space=pl.ANY)]...  3.59 us
  transfers between devices with their start and end apart: 5, of which 2 were waited for; matrix products, arithmetic and copies ran while one was open for 2% of the time, Pallas kernels for 10%

profile of v2, /device:TPU:1, one launch (start us, length us, event | category | flops | bytes accessed | tf_op | source)
XLA Modules:
  0.0 77.6 jit_solution(17139955826480834695)
XLA Ops:
  0.6 0.0 copy-start
  0.6 1.9 %copy-done = bf16[2,3,4,512,128]{4,3,2,1,0:T(8,128)(2,1)S(1)} copy-done((bf16[2,3,4,512,128]{4,3,2,1,0:T(8,128)(2,1)S(1)}, bf16[2,3,4,512,128]{4,3,2,1,0:T(8,128)(2,1)}, u32[]{:S(2)}) %copy-start) | copy-done | bytes 3145752
  2.5 1.4 %strip_edges.1 = (bf16[48,512]{1,0:T(8,128)(2,1)S(1)}, bf16[48,512]{1,0:T(8,128)(2,1)S(1)}) custom-call(bf16[2,3,4,512,128]{4,3,2,1,0:T(8,128)(2,1)S(1)} %copy-done), custom_call_target="tpu_custom_call" | custom-call | flops 100000000 | bytes 3200000 | tf_op jit(solution)/shard_map/strip_edges/pallas_call | solution.py:73
  3.9 0.0 copy-start.2
  3.9 0.0 copy-start.3
  4.0 0.0 copy-start.4
  4.0 4.1 %collective-permute-start = (bf16[48,512]{1,0:T(8,128)(2,1)S(1)}, bf16[48,512]{1,0:T(8,128)(2,1)S(1)}, u32[]{:S(2)}, u32[]{:S(2)}) collective-permute-start(bf16[48,512]{1,0:T(8,128)(2,1)S(1)} %get-tuple-element.9.high_ref), channel_id=1, source_target_pairs={{0,1},{1,2},{2,3},{4,5},{5,6},{6,7},{8,9},{9,10},{10,11},{12,13},{... | collective-permute-start | bytes 147464 | tf_op jit(solution)/shard_map/ppermute | solution.py:433
  8.1 1.3 %collective-permute-start.1 = (bf16[48,512]{1,0:T(8,128)(2,1)S(1)}, bf16[48,512]{1,0:T(8,128)(2,1)S(1)}, u32[]{:S(2)}, u32[]{:S(2)}) collective-permute-start(bf16[48,512]{1,0:T(8,128)(2,1)S(1)} %get-tuple-element.8.low_ref), channel_id=1, source_target_pairs={{1,0},{2,1},{3,2},{5,4},{6,5},{7,6},{9,8},{10,9},{11,10},{13,12},{... | collective-permute-start | bytes 147464 | tf_op jit(solution)/shard_map/ppermute | solution.py:434
  9.4 3.6 %inner_codes.1 = (s16[32,80,128]{2,1,0:T(8,128)(2,1)}, f32[4,2,32,128]{3,2,1,0:T(8,128)S(1)}) custom-call(bf16[2,3,4,512,128]{4,3,2,1,0:T(8,128)(2,1)S(1)} %copy-done.1), custom_call_target="tpu_custom_call" | custom-call | flops 20000000 | bytes 4200000 | tf_op jit(solution)/shard_map/inner_codes/pallas_call | solution.py:150
  13.0 0.0 collective-permute-done.left_ref
  13.0 0.0 collective-permute-done.1.right_ref
  13.0 1.2 %with_tails.1 = s16[32,80,128]{2,1,0:T(8,128)(2,1)} custom-call(bf16[48,512]{1,0:T(8,128)(2,1)S(1)} %get-tuple-element.8.low_ref, bf16[48,512]{1,0:T(8,128)(2,1)S(1)} %get-tuple-element.9.high_ref, bf16[48,512]{1,0:T(8,128)(2,1)S(1)} %collective-permute-done.left_ref, ...), custom_call_target="tpu_custom_call", output_to_operand_aliasing={{}: (5, {})} | custom-call | flops 1000000 | bytes 500000 | tf_op jit(solution)/shard_map/with_tails/pallas_call | solution.py:243
  14.1 13.7 %all-to-all-start = ((s16[64,40,128]{2,1,0:T(8,128)(2,1)}), s16[64,40,128]{2,1,0:T(8,128)(2,1)S(1)}, u32[]{:S(2)}, u32[]{:S(2)}) async-start(s16[64,40,128]{2,1,0:T(8,128)(2,1)} %bitcast), calls=%async_computation | async-start | bytes 1310720 | tf_op jit(solution)/shard_map/all_to_all | solution.py:438
  27.9 4.0 %design_rows.1.rows_ref = bf16[816,384]{1,0:T(8,128)(2,1)S(1)} custom-call(f32[1,128]{1,0:T(1,128)S(1)} %bitcast.13, s32[1,128]{1,0:T(1,128)S(1)} %bitcast.14, s32[256,128]{1,0:T(8,128)S(1)} %copy-done.2), custom_call_target="tpu_custom_call" | custom-call | flops 4000000 | bytes 800000 | tf_op jit(solution)/shard_map/design_rows/pallas_call | solution.py:310
  31.8 16.1 %all-to-all-done = s16[64,40,128]{2,1,0:T(8,128)(2,1)S(1)} async-done(((s16[64,40,128]{2,1,0:T(8,128)(2,1)}), s16[64,40,128]{2,1,0:T(8,128)(2,1)S(1)}, u32[]{:S(2)}, u32[]{:S(2)}) %all-to-all-start) | async-done | bytes 655392 | tf_op jit(solution)/shard_map/all_to_all | solution.py:438
  48.0 6.2 %block_stats.1 = (f32[16,128]{1,0:T(8,128)S(1)}, f32[1,256]{1,0:T(1,128)S(1)}) custom-call(s16[2560,128]{1,0:T(8,128)(2,1)S(1)} %bitcast.12, bf16[816,384]{1,0:T(8,128)(2,1)S(1)} %design_rows.1.rows_ref), custom_call_target="tpu_custom_call" | custom-call | flops 2000000000 | bytes 1000000 | tf_op jit(solution)/shard_map/block_stats/pallas_call | solution.py:409
  54.2 0.4 collective-permute-start.2
  54.6 0.7 broadcast_in_dim.8
  55.3 8.7 %all-to-all-start.1 = ((f16[256,2,128]{2,1,0:T(2,128)(2,1)}), f16[256,2,128]{2,1,0:T(2,128)(2,1)S(1)}, u32[]{:S(2)}, u32[]{:S(2)}) async-start(f16[256,2,128]{2,1,0:T(2,128)(2,1)} %broadcast_in_dim.8), calls=%async_computation.1 | async-start | bytes 262144 | tf_op jit(solution)/shard_map/all_to_all | solution.py:453
  64.0 0.0 collective-permute-done.2
  64.0 0.6 pad_maximum_fusion
  64.7 12.1 %all-to-all-done.1 = f16[256,2,128]{2,1,0:T(2,128)(2,1)S(1)} async-done(((f16[256,2,128]{2,1,0:T(2,128)(2,1)}), f16[256,2,128]{2,1,0:T(2,128)(2,1)S(1)}, u32[]{:S(2)}, u32[]{:S(2)}) %all-to-all-start.1) | async-done | bytes 131104 | tf_op jit(solution)/shard_map/all_to_all | solution.py:453
  76.8 0.3 reduce_max.9
  77.1 0.6 bitcast_convert_fusion
  (8 shorter events, 0.0 us)
Async XLA Ops:
  0.6 1.9 %copy-start = (bf16[2,3,4,512,128]{4,3,2,1,0:T(8,128)(2,1)S(1)}, bf16[2,3,4,512,128]{4,3,2,1,0:T(8,128)(2,1)}, u32[]{:S(2)}) copy-start(bf16[2,3,4,512,128]{4,3,2,1,0:T(8,128)(2,1)} %disp_ref.3) | copy-start | bytes 9437188
  2.5 6.8 %copy-start.1 = (bf16[2,3,4,512,128]{4,3,2,1,0:T(8,128)(2,1)S(1)}, bf16[2,3,4,512,128]{4,3,2,1,0:T(8,128)(2,1)}, u32[]{:S(2)}) copy-start(bf16[2,3,4,512,128]{4,3,2,1,0:T(8,128)(2,1)} %disp_ref.3) | copy-start | bytes 9437188
  3.9 23.9 %copy-start.2 = (s32[256,128]{1,0:T(8,128)S(1)}, s32[256,128]{1,0:T(8,128)}, u32[]{:S(2)}) copy-start(s32[256,128]{1,0:T(8,128)} %perms_ref.1) | copy-start | bytes 393220
  3.9 23.9 %copy-start.3 = (f32[128]{0:T(128)S(1)}, f32[128]{0:T(128)}, u32[]{:S(2)}) copy-start(f32[128]{0:T(128)} %param.5) | copy-start | bytes 1540
  4.0 23.9 %copy-start.4 = (s32[128]{0:T(128)S(1)}, s32[128]{0:T(128)}, u32[]{:S(2)}) copy-start(s32[128]{0:T(128)} %param.6) | copy-start | bytes 1540
  4.0 9.0 %collective-permute-start = (bf16[48,512]{1,0:T(8,128)(2,1)S(1)}, bf16[48,512]{1,0:T(8,128)(2,1)S(1)}, u32[]{:S(2)}, u32[]{:S(2)}) collective-permute-start(bf16[48,512]{1,0:T(8,128)(2,1)S(1)} %get-tuple-element.9.high_ref), channel_id=1, source_target_pairs={{0,1},{1,2},{2,3},{4,5},{5,6},{6,7},{8,9},{9,10},{10,11},{12,13},{... | collective-permute-start | bytes 147464 | tf_op jit(solution)/shard_map/ppermute | solution.py:433
  8.1 4.9 %collective-permute-start.1 = (bf16[48,512]{1,0:T(8,128)(2,1)S(1)}, bf16[48,512]{1,0:T(8,128)(2,1)S(1)}, u32[]{:S(2)}, u32[]{:S(2)}) collective-permute-start(bf16[48,512]{1,0:T(8,128)(2,1)S(1)} %get-tuple-element.8.low_ref), channel_id=1, source_target_pairs={{1,0},{2,1},{3,2},{5,4},{6,5},{7,6},{9,8},{10,9},{11,10},{13,12},{... | collective-permute-start | bytes 147464 | tf_op jit(solution)/shard_map/ppermute | solution.py:434
  14.1 33.8 %all-to-all-start = ((s16[64,40,128]{2,1,0:T(8,128)(2,1)}), s16[64,40,128]{2,1,0:T(8,128)(2,1)S(1)}, u32[]{:S(2)}, u32[]{:S(2)}) async-start(s16[64,40,128]{2,1,0:T(8,128)(2,1)} %bitcast), calls=%async_computation | async-start | bytes 1310720 | tf_op jit(solution)/shard_map/all_to_all | solution.py:438
  54.2 9.8 %collective-permute-start.2 = (f32[8,128]{1,0:T(8,128)S(1)}, f32[8,128]{1,0:T(8,128)S(1)}, u32[]{:S(2)}, u32[]{:S(2)}) collective-permute-start(f32[8,128]{1,0:T(8,128)S(1)} %slice_select_fusion.1), channel_id=1, source_target_pairs={{0,4},{4,0},{8,12},{12,8},{16,20},{20,16},{24,28},{28,24},{32,36},... | collective-permute-start | bytes 12296 | tf_op jit(solution)/shard_map/ppermute | solution.py:446
  55.3 21.4 %all-to-all-start.1 = ((f16[256,2,128]{2,1,0:T(2,128)(2,1)}), f16[256,2,128]{2,1,0:T(2,128)(2,1)S(1)}, u32[]{:S(2)}, u32[]{:S(2)}) async-start(f16[256,2,128]{2,1,0:T(2,128)(2,1)} %broadcast_in_dim.8), calls=%async_computation.1 | async-start | bytes 262144 | tf_op jit(solution)/shard_map/all_to_all | solution.py:453

commit v3 on v2

--- a/solution.py
+++ b/solution.py
@@ -18,6 +18,7 @@
 COMPS, PLANES = 3, 4
 PERMS, GROUP = 256, 272
 REACH = 0.6
+REACH_T = 6800.0
 LEVELS = 32767.0
 CENTRE = 0.4 / 0.15
 FLOOR = 1e-06 / (CENTRE + 4.0)
@@ -329,7 +330,7 @@
         value_ref[at, :] = decode(code_ref[at, :].astype(F32))
         return carry
 
-    lax.fori_loop(0, senders * CHUNK // per, unpack, 0)
+    lax.fori_loop(0, senders * CHUNK // per, unpack, 0, unroll=4)
 
     def gathered(offsets):
         return jnp.concatenate(
@@ -345,18 +346,20 @@
         y_ref[subjects : 2 * subjects, at] = (y - high.astype(F32)).astype(BF16)
         y_ref[2 * subjects : 3 * subjects, at] = high
 
-    sides = gathered([tail + 2, tail + 6])
+    far = lane // 2 + jnp.where(lane % 2 == 0, 97, 1)
+    near = (lane - 36) // 2 + jnp.where(lane % 2 == 0, 64, 32)
+    sides = jnp.take_along_axis(
+        gathered([tail + 2, tail + 6]),
+        jnp.where(lane < 32, far, jnp.where((lane >= 36) & (lane < 72), near, 0)),
+        axis=1,
+    )
 
     def mended(y, r):
-        index = jnp.where(lane == 0, 33 + r, jnp.where(lane == LANES - 1, 65 + r, 0))
-        ends = jnp.take_along_axis(sides, index, axis=1)
+        ends = pltpu.roll(sides, LANES - 39 - 2 * r, 1)
         return jnp.where((lane == 0) | (lane == LANES - 1), ends, y)
 
-    def place_row(r, carry):
+    for r in range(BLOCK):
         place(r, mended(gathered([main + r, main + BLOCK + r]), r))
-        return carry
-
-    lax.fori_loop(0, BLOCK, place_row, 0, unroll=8)
     place(BLOCK, mended(gathered([tail, tail + 4]), -1))
     place(BLOCK + 1, mended(gathered([tail + 1, tail + 5]), BLOCK))
     place(BLOCK + 2, sides)
@@ -381,9 +384,7 @@
         mine = block(r)
         above = block(r - 1 if r > 0 else BLOCK)
         below = block(r + 1 if r < BLOCK - 1 else BLOCK + 1)
-        ends = jnp.take_along_axis(
-            block(BLOCK + 2), jnp.where(here == 0, 1 + r, jnp.where(here == LANES - 1, 97 + r, 0)), axis=1
-        )
+        ends = pltpu.roll(block(BLOCK + 2), LANES - 1 - 2 * r, 1)
         before = jnp.where(here == 0, ends, pltpu.roll(mine, 1, 1))
         after = jnp.where(here == LANES - 1, ends, pltpu.roll(mine, LANES - 1, 1))
         beside = (above + below) + (before + after)
@@ -397,20 +398,27 @@
         best_ref[pl.ds(pl.multiple_of(g * 8, 8), 8), :] = best
         return carry
 
-    lax.fori_loop(0, PERMS // 8, body, 0, unroll=8)
+    lax.fori_loop(0, PERMS // 8, body, 0, unroll=32)
+    half = BLOCK // 2
     for r in range(BLOCK):
-        tmap_ref[r : r + 1, :] = pseudo_t(PERMS // 8, r)[0:1, :] * unscale
-    peaks_ref[...] = jnp.max(best_ref[...].T, axis=0, keepdims=True) * unscale
-
-
-def block_stats(codes, rows, senders):
+        tmap_ref[(r // half + odd) % 2, r % half : r % half + 1, :] = (
+            pseudo_t(PERMS // 8, r)[0:1, :] * unscale
+        )
+    code = jnp.max(best_ref[...].T, axis=0, keepdims=True) * (unscale / REACH_T)
+    code = jnp.minimum(jnp.sqrt(jnp.sqrt(code)), 1.0) * LEVELS + 0.5
+    lines = jnp.concatenate([code[:, k * LANES : (k + 1) * LANES] for k in range(PERMS // LANES)] * 4, axis=0)
+    everyone = peaks_ref.shape[0]
+    peaks_ref[...] = jnp.broadcast_to(packed(lines)[None], (everyone // 4, 8, LANES)).reshape(everyone, 2, LANES)
+
+
+def block_stats(codes, rows, senders, everyone):
     subjects = PER * senders
     columns = (BLOCK + 3) * LANES
     return pl.pallas_call(
         functools.partial(stats_kernel, senders),
         out_shape=(
-            jax.ShapeDtypeStruct((BLOCK, LANES), F32),
-            jax.ShapeDtypeStruct((1, PERMS), F32),
+            jax.ShapeDtypeStruct((2, BLOCK // 2, LANES), F32),
+            jax.ShapeDtypeStruct((everyone, PERMS // LANES, LANES), I16),
         ),
         scratch_shapes=[
             pltpu.VMEM((senders * CHUNK + CHUNK, LANES), F32),
@@ -438,20 +446,16 @@
     codes = lax.all_to_all(
         sent.reshape(senders, CHUNK, LANES), "subj", split_axis=0, concat_axis=0, tiled=True
     )
-    tested, peaks = block_stats(codes.reshape(senders * CHUNK, LANES), rows, senders)
+    everyone = senders * strips
+    tested, mine = block_stats(codes.reshape(senders * CHUNK, LANES), rows, senders, everyone)
 
     odd = lax.axis_index("subj") % 2 == 1
-    low, high = tested[: BLOCK // 2], tested[BLOCK // 2 :]
-    kept = jnp.where(odd, high, low)
-    swapped = lax.ppermute(
-        jnp.where(odd, low, high), "subj", [(i, i ^ 1) for i in range(senders)]
-    )
-    t_map = jnp.stack([jnp.where(odd, swapped, kept), jnp.where(odd, kept, swapped)])
-
-    everyone = senders * strips
-    mine = jnp.broadcast_to(peaks.astype(jnp.float16).reshape(1, 2, LANES), (everyone, 2, LANES))
+    swapped = lax.ppermute(tested[1], "subj", [(i, i ^ 1) for i in range(senders)])
+    t_map = jnp.stack([jnp.where(odd, swapped, tested[0]), jnp.where(odd, tested[0], swapped)])
+
     theirs = lax.all_to_all(mine, ("subj", "strip"), split_axis=0, concat_axis=0, tiled=True)
-    return t_map, jnp.max(theirs, axis=0).astype(F32).reshape(PERMS)
+    root = theirs.astype(F32) * (REACH_T**0.25 / LEVELS)
+    return t_map, jnp.max((root * root) * (root * root), axis=0).reshape(PERMS)
 
 
 def solution(mesh):

time: 77.9 us -> 75.7 us (0.972)
  Pallas kernels: 16.3 us -> 14.9 us
    pallas_call x1, Pallas kernels: 6.24 us -> 4.8 us  [block_stats(): pl.pallas_call(functools.partial(stats_kernel, senders), out_shape=(jax.S...]
  transfers between devices with their start and end apart: 5 -> 5, of which waited for: 2 -> 2; matrix products, arithmetic and copies ran while one was open for 2% -> 1% of each run, Pallas kernels for 10% -> 10%
where the time goes in v3:
time: 75.7 us; the launch traced here: 75.4 us
  waiting for transfers between devices  28.3 us (37%)
  starting transfers between devices  28 us (37%)
  Pallas kernels  14.9 us (20%)
  local copies, waits for them, and re-layouts  1.91 us (3%)
  other arithmetic  1.48 us (2%)
  between operations  0.79 us (1%)
    all_to_all x1, waiting for transfers between devices, on_device(): lax.all_to_all(sent.reshape(senders, CHUNK, LANES), 'subj', split_axis=0,...  16.1 us
    all_to_all x1, starting transfers between devices, on_device(): lax.all_to_all(sent.reshape(senders, CHUNK, LANES), 'subj', split_axis=0,...  13.7 us
    all_to_all x1, waiting for transfers between devices, on_device(): lax.all_to_all(mine, ('subj', 'strip'), split_axis=0, concat_axis=0, tile...  12.1 us
    all_to_all x1, starting transfers between devices, on_device(): lax.all_to_all(mine, ('subj', 'strip'), split_axis=0, concat_axis=0, tile...  8.69 us
    pallas_call x1, Pallas kernels, block_stats(): pl.pallas_call(functools.partial(stats_kernel, senders), out_shape=(jax.S...  4.8 us
    ppermute x1, starting transfers between devices, on_device(): left = lax.ppermute(high, 'strip', [(i, i + 1) for i in range(strips - 1)])  4.08 us
    pallas_call x1, Pallas kernels, design_rows(): pl.pallas_call(designs_kernel, out_shape=jax.ShapeDtypeStruct((3 * GROUP,...  3.96 us
    pallas_call x1, Pallas kernels, inner_codes(): pl.pallas_call(inner_kernel, in_specs=[pl.BlockSpec(memory_space=pl.ANY)]...  3.59 us
  transfers between devices with their start and end apart: 5, of which 2 were waited for; matrix products, arithmetic and copies ran while one was open for 1% of the time, Pallas kernels for 10%

profile of v3, /device:TPU:1, one launch (start us, length us, event | category | flops | bytes accessed | tf_op | source)
XLA Modules:
  0.0 75.4 jit_solution(4420680586588783956)
XLA Ops:
  0.6 1.9 %copy-done = bf16[2,3,4,512,128]{4,3,2,1,0:T(8,128)(2,1)S(1)} copy-done((bf16[2,3,4,512,128]{4,3,2,1,0:T(8,128)(2,1)S(1)}, bf16[2,3,4,512,128]{4,3,2,1,0:T(8,128)(2,1)}, u32[]{:S(2)}) %copy-start) | copy-done | bytes 3145752
  2.5 1.4 %strip_edges.1 = (bf16[48,512]{1,0:T(8,128)(2,1)S(1)}, bf16[48,512]{1,0:T(8,128)(2,1)S(1)}) custom-call(bf16[2,3,4,512,128]{4,3,2,1,0:T(8,128)(2,1)S(1)} %copy-done), custom_call_target="tpu_custom_call" | custom-call | flops 100000000 | bytes 3200000 | tf_op jit(solution)/shard_map/strip_edges/pallas_call | solution.py:74
  3.9 0.0 copy-start.2
  3.9 0.0 copy-start.3
  4.0 0.0 copy-start.4
  4.0 4.1 %collective-permute-start = (bf16[48,512]{1,0:T(8,128)(2,1)S(1)}, bf16[48,512]{1,0:T(8,128)(2,1)S(1)}, u32[]{:S(2)}, u32[]{:S(2)}) collective-permute-start(bf16[48,512]{1,0:T(8,128)(2,1)S(1)} %get-tuple-element.9.high_ref), channel_id=1, source_target_pairs={{0,1},{1,2},{2,3},{4,5},{5,6},{6,7},{8,9},{9,10},{10,11},{12,13},{... | collective-permute-start | bytes 147464 | tf_op jit(solution)/shard_map/ppermute | solution.py:441
  8.1 1.3 %collective-permute-start.1 = (bf16[48,512]{1,0:T(8,128)(2,1)S(1)}, bf16[48,512]{1,0:T(8,128)(2,1)S(1)}, u32[]{:S(2)}, u32[]{:S(2)}) collective-permute-start(bf16[48,512]{1,0:T(8,128)(2,1)S(1)} %get-tuple-element.8.low_ref), channel_id=1, source_target_pairs={{1,0},{2,1},{3,2},{5,4},{6,5},{7,6},{9,8},{10,9},{11,10},{13,12},{... | collective-permute-start | bytes 147464 | tf_op jit(solution)/shard_map/ppermute | solution.py:442
  9.4 3.6 %inner_codes.1 = (s16[32,80,128]{2,1,0:T(8,128)(2,1)}, f32[4,2,32,128]{3,2,1,0:T(8,128)S(1)}) custom-call(bf16[2,3,4,512,128]{4,3,2,1,0:T(8,128)(2,1)S(1)} %copy-done.1), custom_call_target="tpu_custom_call" | custom-call | flops 20000000 | bytes 4200000 | tf_op jit(solution)/shard_map/inner_codes/pallas_call | solution.py:151
  13.0 0.0 collective-permute-done.left_ref
  13.0 0.0 collective-permute-done.1.right_ref
  13.0 1.2 %with_tails.1 = s16[32,80,128]{2,1,0:T(8,128)(2,1)} custom-call(bf16[48,512]{1,0:T(8,128)(2,1)S(1)} %get-tuple-element.8.low_ref, bf16[48,512]{1,0:T(8,128)(2,1)S(1)} %get-tuple-element.9.high_ref, bf16[48,512]{1,0:T(8,128)(2,1)S(1)} %collective-permute-done.left_ref, ...), custom_call_target="tpu_custom_call", output_to_operand_aliasing={{}: (5, {})} | custom-call | flops 1000000 | bytes 500000 | tf_op jit(solution)/shard_map/with_tails/pallas_call | solution.py:244
  14.2 13.7 %all-to-all-start = ((s16[64,40,128]{2,1,0:T(8,128)(2,1)}), s16[64,40,128]{2,1,0:T(8,128)(2,1)S(1)}, u32[]{:S(2)}, u32[]{:S(2)}) async-start(s16[64,40,128]{2,1,0:T(8,128)(2,1)} %bitcast), calls=%async_computation | async-start | bytes 1310720 | tf_op jit(solution)/shard_map/all_to_all | solution.py:446
  27.8 0.0 copy-done.2
  27.8 0.0 copy-done.3
  27.9 0.0 copy-done.4
  27.9 4.0 %design_rows.1.rows_ref = bf16[816,384]{1,0:T(8,128)(2,1)S(1)} custom-call(f32[1,128]{1,0:T(1,128)S(1)} %bitcast.19, s32[1,128]{1,0:T(1,128)S(1)} %bitcast.20, s32[256,128]{1,0:T(8,128)S(1)} %copy-done.2), custom_call_target="tpu_custom_call" | custom-call | flops 4000000 | bytes 800000 | tf_op jit(solution)/shard_map/design_rows/pallas_call | solution.py:311
  31.8 16.1 %all-to-all-done = s16[64,40,128]{2,1,0:T(8,128)(2,1)S(1)} async-done(((s16[64,40,128]{2,1,0:T(8,128)(2,1)}), s16[64,40,128]{2,1,0:T(8,128)(2,1)S(1)}, u32[]{:S(2)}, u32[]{:S(2)}) %all-to-all-start) | async-done | bytes 655392 | tf_op jit(solution)/shard_map/all_to_all | solution.py:446
  48.0 4.8 %block_stats.1 = (f32[2,8,128]{2,1,0:T(8,128)S(1)}, s16[256,2,128]{2,1,0:T(2,128)(2,1)}) custom-call(s16[2560,128]{1,0:T(8,128)(2,1)S(1)} %bitcast.18, bf16[816,384]{1,0:T(8,128)(2,1)S(1)} %design_rows.1.rows_ref), custom_call_target="tpu_custom_call" | custom-call | flops 2000000000 | bytes 1000000 | tf_op jit(solution)/shard_map/block_stats/pallas_call | solution.py:417
  52.8 0.3 collective-permute-start.2
  53.1 8.7 %all-to-all-start.1 = ((s16[256,2,128]{2,1,0:T(2,128)(2,1)}), s16[256,2,128]{2,1,0:T(2,128)(2,1)S(1)}, u32[]{:S(2)}, u32[]{:S(2)}) async-start(s16[256,2,128]{2,1,0:T(2,128)(2,1)} %get-tuple-element.13), calls=%async_computation.1 | async-start | bytes 262144 | tf_op jit(solution)/shard_map/all_to_all | solution.py:456
  61.8 0.0 collective-permute-done.2
  61.8 0.6 pad_maximum_fusion
  62.4 12.1 %all-to-all-done.1 = s16[256,2,128]{2,1,0:T(2,128)(2,1)S(1)} async-done(((s16[256,2,128]{2,1,0:T(2,128)(2,1)}), s16[256,2,128]{2,1,0:T(2,128)(2,1)S(1)}, u32[]{:S(2)}, u32[]{:S(2)}) %all-to-all-start.1) | async-done | bytes 131104 | tf_op jit(solution)/shard_map/all_to_all | solution.py:456
  74.5 0.9 %multiply_reduce_fusion = f32[2,128]{1,0:T(2,128)} fusion(s16[256,2,128]{2,1,0:T(2,128)(2,1)S(1)} %all-to-all-done.1), kind=kLoop, calls=%fused_computation | loop fusion | flops 327424 | bytes 132096 | tf_op jit(solution)/shard_map/reduce_max | solution.py:458
  (5 shorter events, 0.0 us)
Async XLA Ops:
  0.6 1.9 %copy-start = (bf16[2,3,4,512,128]{4,3,2,1,0:T(8,128)(2,1)S(1)}, bf16[2,3,4,512,128]{4,3,2,1,0:T(8,128)(2,1)}, u32[]{:S(2)}) copy-start(bf16[2,3,4,512,128]{4,3,2,1,0:T(8,128)(2,1)} %disp_ref.3) | copy-start | bytes 9437188
  2.5 6.8 %copy-start.1 = (bf16[2,3,4,512,128]{4,3,2,1,0:T(8,128)(2,1)S(1)}, bf16[2,3,4,512,128]{4,3,2,1,0:T(8,128)(2,1)}, u32[]{:S(2)}) copy-start(bf16[2,3,4,512,128]{4,3,2,1,0:T(8,128)(2,1)} %disp_ref.3) | copy-start | bytes 9437188
  3.9 23.9 %copy-start.2 = (s32[256,128]{1,0:T(8,128)S(1)}, s32[256,128]{1,0:T(8,128)}, u32[]{:S(2)}) copy-start(s32[256,128]{1,0:T(8,128)} %perms_ref.1) | copy-start | bytes 393220
  3.9 23.9 %copy-start.3 = (f32[128]{0:T(128)S(1)}, f32[128]{0:T(128)}, u32[]{:S(2)}) copy-start(f32[128]{0:T(128)} %param.5) | copy-start | bytes 1540
  4.0 23.9 %copy-start.4 = (s32[128]{0:T(128)S(1)}, s32[128]{0:T(128)}, u32[]{:S(2)}) copy-start(s32[128]{0:T(128)} %param.6) | copy-start | bytes 1540
  4.0 9.0 %collective-permute-start = (bf16[48,512]{1,0:T(8,128)(2,1)S(1)}, bf16[48,512]{1,0:T(8,128)(2,1)S(1)}, u32[]{:S(2)}, u32[]{:S(2)}) collective-permute-start(bf16[48,512]{1,0:T(8,128)(2,1)S(1)} %get-tuple-element.9.high_ref), channel_id=1, source_target_pairs={{0,1},{1,2},{2,3},{4,5},{5,6},{6,7},{8,9},{9,10},{10,11},{12,13},{... | collective-permute-start | bytes 147464 | tf_op jit(solution)/shard_map/ppermute | solution.py:441
  8.1 4.9 %collective-permute-start.1 = (bf16[48,512]{1,0:T(8,128)(2,1)S(1)}, bf16[48,512]{1,0:T(8,128)(2,1)S(1)}, u32[]{:S(2)}, u32[]{:S(2)}) collective-permute-start(bf16[48,512]{1,0:T(8,128)(2,1)S(1)} %get-tuple-element.8.low_ref), channel_id=1, source_target_pairs={{1,0},{2,1},{3,2},{5,4},{6,5},{7,6},{9,8},{10,9},{11,10},{13,12},{... | collective-permute-start | bytes 147464 | tf_op jit(solution)/shard_map/ppermute | solution.py:442
  14.2 33.8 %all-to-all-start = ((s16[64,40,128]{2,1,0:T(8,128)(2,1)}), s16[64,40,128]{2,1,0:T(8,128)(2,1)S(1)}, u32[]{:S(2)}, u32[]{:S(2)}) async-start(s16[64,40,128]{2,1,0:T(8,128)(2,1)} %bitcast), calls=%async_computation | async-start | bytes 1310720 | tf_op jit(solution)/shard_map/all_to_all | solution.py:446
  52.8 9.0 %collective-permute-start.2 = (f32[8,128]{1,0:T(8,128)S(1)}, f32[8,128]{1,0:T(8,128)S(1)}, u32[]{:S(2)}, u32[]{:S(2)}) collective-permute-start(f32[8,128]{1,0:T(8,128)S(1)} %slice_bitcast_fusion), channel_id=1, source_target_pairs={{0,4},{4,0},{8,12},{12,8},{16,20},{20,16},{24,28},{28,24},{32,36},... | collective-permute-start | bytes 12296 | tf_op jit(solution)/shard_map/ppermute | solution.py:453
  53.1 21.4 %all-to-all-start.1 = ((s16[256,2,128]{2,1,0:T(2,128)(2,1)}), s16[256,2,128]{2,1,0:T(2,128)(2,1)S(1)}, u32[]{:S(2)}, u32[]{:S(2)}) async-start(s16[256,2,128]{2,1,0:T(2,128)(2,1)} %get-tuple-element.13), calls=%async_computation.1 | async-start | bytes 262144 | tf_op jit(solution)/shard_map/all_to_all | solution.py:456

commit v4 on v3

--- a/solution.py
+++ b/solution.py
@@ -52,96 +52,88 @@
     return jnp.log(det * 0.125)
 
 
-def edges_kernel(disp_ref, low_ref, high_ref):
+def edges_kernel(parts, disp_ref, low_ref, high_ref, field_ref, sem):
+    rows = ROWS // parts
+    copies = [
+        pltpu.make_async_copy(
+            disp_ref.at[:, :, :, h * rows : (h + 1) * rows, :],
+            field_ref.at[:, :, :, h * rows : (h + 1) * rows, :],
+            sem.at[h],
+        )
+        for h in range(parts)
+    ]
+    for copy in copies:
+        copy.start()
     row = lax.broadcasted_iota(jnp.int32, (32, 2 * LANES), 0)
     lane = lax.broadcasted_iota(jnp.int32, (32, 2 * LANES), 1)
     column = jnp.where(row < 16, row // 8, row // 8 - 2 + LANES - 2)
-    for c in range(COMPS):
-        acc = jnp.zeros((32, low_ref.shape[1]), F32)
-        for q in range(PLANES):
-            pick = ((row % 8 == 2 * q + lane // LANES) & (lane % LANES == column)).astype(F32)
-            both = jnp.concatenate([disp_ref[0, c, q], disp_ref[1, c, q]], axis=1)
-            acc = acc + lax.dot_general(
-                pick.astype(BF16), both, (((1,), (1,)), ((), ())), preferred_element_type=F32
-            )
-        low_ref[c * 16 : c * 16 + 16, :] = acc[0:16].astype(BF16)
-        high_ref[c * 16 : c * 16 + 16, :] = acc[16:32].astype(BF16)
+    picks = [
+        ((row % 8 == 2 * q + lane // LANES) & (lane % LANES == column)).astype(F32).astype(BF16)
+        for q in range(PLANES)
+    ]
+    for h in range(parts):
+        copies[h].wait()
+        at = slice(h * rows, (h + 1) * rows)
+        for c in range(COMPS):
+            acc = jnp.zeros((32, rows), F32)
+            for q in range(PLANES):
+                both = jnp.concatenate([field_ref[0, c, q, at, :], field_ref[1, c, q, at, :]], axis=1)
+                acc = acc + lax.dot_general(
+                    picks[q], both, (((1,), (1,)), ((), ())), preferred_element_type=F32
+                )
+            low_ref[c * 16 : c * 16 + 16, at] = acc[0:16].astype(BF16)
+            high_ref[c * 16 : c * 16 + 16, at] = acc[16:32].astype(BF16)
 
 
 def strip_edges(disp):
-    rows = 256
-    out = jax.ShapeDtypeStruct((COMPS * 16, ROWS), BF16)
+    parts = 4
+    out = pltpu.VMEM((COMPS * 16, ROWS), BF16)
     return pl.pallas_call(
-        edges_kernel,
-        grid=(ROWS // rows,),
-        in_specs=[pl.BlockSpec((PER, COMPS, PLANES, rows, LANES), lambda i: (0, 0, 0, i, 0))],
-        out_specs=[pl.BlockSpec((COMPS * 16, rows), lambda i: (0, i))] * 2,
-        out_shape=(out, out),
+        functools.partial(edges_kernel, parts),
+        in_specs=[pl.BlockSpec(memory_space=pltpu.HBM)],
+        out_specs=[pl.BlockSpec(memory_space=pltpu.VMEM)] * 3,
+        out_shape=(out, out, pltpu.VMEM(disp.shape, BF16)),
+        scratch_shapes=[pltpu.SemaphoreType.DMA((parts,))],
         compiler_params=pltpu.CompilerParams(vmem_limit_bytes=8 * 2**20),
         cost_estimate=pl.CostEstimate(flops=10**8, bytes_accessed=3_200_000, transcendentals=0),
         name="strip_edges",
-    )(disp)
-
-
-def inner_kernel(disp_ref, out_ref, beside_ref, field_ref, pad_ref, code_ref, in_sem):
-    pad, step, parts = 8, 16, 4
-    rows = ROWS // parts
+    )(pltpu.with_memory_space_constraint(disp, pltpu.HBM))
+
+
+def inner_kernel(disp_ref, out_ref, beside_ref, pad_ref, code_ref):
+    pad, step = 8, 16
+    blocks = ROWS // BLOCK
     zeros = jnp.zeros((pad, LANES), F32)
-    copies = [
-        [
-            pltpu.make_async_copy(
-                disp_ref.at[s, :, :, h * rows : (h + 1) * rows, :],
-                field_ref.at[s, :, :, h * rows : (h + 1) * rows, :],
-                in_sem.at[s, h],
-            )
-            for h in range(parts)
-        ]
-        for s in range(PER)
-    ]
-    for s in range(PER):
-        for h in range(parts):
-            copies[s][h].start()
     for k in range(2):
         code_ref[k, 0:pad, :] = zeros
         code_ref[k, pad + ROWS : 2 * pad + ROWS, :] = zeros
         for c in range(COMPS):
             pad_ref[k, c, 0:pad, :] = zeros
             pad_ref[k, c, pad + ROWS : 2 * pad + ROWS, :] = zeros
-
     for s in range(PER):
-        for h in range(parts + 1):
-            if h < parts:
-                copies[s][h].wait()
-                for p in range(2):
-                    for c in range(COMPS):
-                        pad_ref[p, c, pad + h * rows : pad + (h + 1) * rows, :] = field_ref[
-                            s, c, 1 + p, h * rows : (h + 1) * rows, :
-                        ].astype(F32)
-            if h > 0:
-
-                def body(i, carry):
-                    base = pl.multiple_of(i * step, step)
-                    for p in range(2):
-                        dz, dx, dy = [], [], []
-                        for c in range(COMPS):
-                            up = field_ref[s, c, p + 2, pl.ds(base, step), :].astype(F32)
-                            down = field_ref[s, c, p, pl.ds(base, step), :].astype(F32)
-                            dz.append(up - down)
-                            center = pad_ref[p, c, pl.ds(base + pad, step), :]
-                            dx.append(
-                                pad_ref[p, c, pl.ds(base + pad + 1, step), :]
-                                - pad_ref[p, c, pl.ds(base + pad - 1, step), :]
-                            )
-                            dy.append(pltpu.roll(center, LANES - 1, 1) - pltpu.roll(center, 1, 1))
-                        code = encode(log_det(dz, dx, dy))
-                        code_ref[p, pl.ds(base + pad, step), :] = code
-                        out_ref[i, 48 * p + 16 * s : 48 * p + 16 * s + 16, :] = packed(code)
-                    return carry
-
-                many = rows // step
-                lax.fori_loop((h - 1) * many, h * many, body, 0, unroll=many)
-        blocks = ROWS // BLOCK
         for p in range(2):
+            for c in range(COMPS):
+                pad_ref[p, c, pad : pad + ROWS, :] = disp_ref[s, c, 1 + p].astype(F32)
+
+            def body(i, carry):
+                base = pl.multiple_of(i * step, step)
+                dz, dx, dy = [], [], []
+                for c in range(COMPS):
+                    up = disp_ref[s, c, p + 2, pl.ds(base, step), :].astype(F32)
+                    down = disp_ref[s, c, p, pl.ds(base, step), :].astype(F32)
+                    dz.append(up - down)
+                    center = pad_ref[p, c, pl.ds(base + pad, step), :]
+                    dx.append(
+                        pad_ref[p, c, pl.ds(base + pad + 1, step), :]
+                        - pad_ref[p, c, pl.ds(base + pad - 1, step), :]
+                    )
+                    dy.append(pltpu.roll(center, LANES - 1, 1) - pltpu.roll(center, 1, 1))
+                code = encode(log_det(dz, dx, dy))
+                code_ref[p, pl.ds(base + pad, step), :] = code
+                out_ref[s, p, i] = packed(code)
+                return carry
+
+            lax.fori_loop(0, ROWS // step, body, 0, unroll=16)
             beside_ref[2 * p + s, 0] = code_ref[p, pl.ds(pad - 1, blocks, stride=BLOCK), :]
             beside_ref[2 * p + s, 1] = code_ref[p, pl.ds(pad + BLOCK, blocks, stride=BLOCK), :]
 
@@ -150,25 +142,34 @@
     blocks = ROWS // BLOCK
     return pl.pallas_call(
         inner_kernel,
-        in_specs=[pl.BlockSpec(memory_space=pl.ANY)],
+        in_specs=[pl.BlockSpec(memory_space=pltpu.VMEM)],
+        out_specs=[pl.BlockSpec(memory_space=pltpu.VMEM)] * 2,
         out_shape=(
-            jax.ShapeDtypeStruct((blocks, PAIR, LANES), I16),
-            jax.ShapeDtypeStruct((2 * PER, 2, blocks, LANES), F32),
+            pltpu.VMEM((PER, 2, blocks, BLOCK, LANES), I16),
+            pltpu.VMEM((2 * PER, 2, blocks, LANES), F32),
         ),
         scratch_shapes=[
-            pltpu.VMEM((PER, COMPS, PLANES, ROWS, LANES), BF16),
             pltpu.VMEM((2, COMPS, ROWS + 16, LANES), F32),
             pltpu.VMEM((2, ROWS + 32, LANES), F32),
-            pltpu.SemaphoreType.DMA((PER, 4)),
         ],
         compiler_params=pltpu.CompilerParams(vmem_limit_bytes=16 * 2**20),
         cost_estimate=pl.CostEstimate(flops=2 * 10**7, bytes_accessed=4_200_000, transcendentals=262144),
         name="inner_codes",
-    )(disp)
-
-
-def tail_kernel(low_ref, high_ref, left_ref, right_ref, beside_ref, chunk_ref, out_ref, pad_ref, side_ref, tail_ref, send_ref, sem):
-    del chunk_ref
+    )(pltpu.with_memory_space_constraint(disp, pltpu.VMEM))
+
+
+def tail_kernel(low_ref, high_ref, left_ref, right_ref, beside_ref, main_ref, out_ref, pad_ref, side_ref, tail_ref, send_ref, sem):
+    copies = [
+        pltpu.make_async_copy(
+            main_ref.at[s, p],
+            out_ref.at[:, 48 * p + BLOCK * s : 48 * p + BLOCK * s + BLOCK, :],
+            sem.at[2 * s + p],
+        )
+        for s in range(PER)
+        for p in range(2)
+    ]
+    for copy in copies:
+        copy.start()
     strips = lax.axis_size("strip")
     me = lax.axis_index("strip")
     keep_left = (me > 0).astype(F32)
@@ -232,32 +233,33 @@
             ]
             tail_ref[pl.ds(row + 3, blocks, stride=2 * TAIL), :] = jnp.zeros((blocks, LANES), F32)
     send_ref[...] = packed(tail_ref[0 : blocks * 2 * TAIL, :]).reshape(blocks, 2 * TAIL, LANES)
-    copy = pltpu.make_async_copy(send_ref, out_ref.at[:, MAIN : MAIN + 2 * TAIL, :], sem)
-    copy.start()
-    copy.wait()
-
-
-def with_tails(low, high, left, right, beside, chunks):
+    copies.append(
+        pltpu.make_async_copy(send_ref, out_ref.at[:, MAIN : MAIN + 2 * TAIL, :], sem.at[2 * PER])
+    )
+    copies[-1].start()
+    for copy in copies:
+        copy.wait()
+
+
+def with_tails(low, high, left, right, beside, main):
     blocks = ROWS // BLOCK
     vmem = pl.BlockSpec(memory_space=pltpu.VMEM)
-    anywhere = pl.BlockSpec(memory_space=pl.ANY)
     return pl.pallas_call(
         tail_kernel,
-        in_specs=[vmem] * 5 + [anywhere],
-        out_specs=anywhere,
-        out_shape=jax.ShapeDtypeStruct(chunks.shape, chunks.dtype),
-        input_output_aliases={5: 0},
+        in_specs=[vmem] * 6,
+        out_specs=pl.BlockSpec(memory_space=pltpu.HBM),
+        out_shape=pltpu.HBM((blocks, PAIR, LANES), I16),
         scratch_shapes=[
             pltpu.VMEM((4, 8, ROWS + 2 * LANES), F32),
             pltpu.VMEM((blocks * 8 + 8, LANES), F32),
             pltpu.VMEM((blocks * 2 * TAIL + 16, LANES), F32),
             pltpu.VMEM((blocks, 2 * TAIL, LANES), I16),
-            pltpu.SemaphoreType.DMA,
+            pltpu.SemaphoreType.DMA((2 * PER + 1,)),
         ],
         compiler_params=pltpu.CompilerParams(vmem_limit_bytes=8 * 2**20),
         cost_estimate=pl.CostEstimate(flops=10**6, bytes_accessed=5 * 10**5, transcendentals=5 * 10**4),
         name="with_tails",
-    )(low, high, left, right, beside, chunks)
+    )(*(pltpu.with_memory_space_constraint(x, pltpu.VMEM) for x in (low, high, left, right, beside, main)))
 
 
 def designs_kernel(age_ref, code_ref, perms_ref, out_ref):
@@ -437,12 +439,12 @@
 def on_device(displacement, age, group_codes, perms):
     senders = lax.axis_size("subj")
     strips = lax.axis_size("strip")
-    low, high = strip_edges(displacement)
+    low, high, field = strip_edges(displacement)
     left = lax.ppermute(high, "strip", [(i, i + 1) for i in range(strips - 1)])
     right = lax.ppermute(low, "strip", [(i + 1, i) for i in range(strips - 1)])
-    chunks, beside = inner_codes(displacement)
+    main, beside = inner_codes(field)
     rows = design_rows(age, group_codes, perms)
-    sent = with_tails(low, high, left, right, beside, chunks)
+    sent = with_tails(low, high, left, right, beside, main)
     codes = lax.all_to_all(
         sent.reshape(senders, CHUNK, LANES), "subj", split_axis=0, concat_axis=0, tiled=True
     )

time: 75.7 us -> 75 us (level)
  local copies, waits for them, and re-layouts: 1.91 us -> 0.02 us
  Pallas kernels: 14.9 us -> 15.8 us
    unnamed x10 -> x6, local copies, waits for them, and re-layouts: 1.91 us -> 0.02 us
    pallas_call x3, Pallas kernels: 6.15 us -> 6.95 us  [the longest x1 2.86 us: inner_codes(): pl.pallas_call(inner_kernel, in_specs=[pl.BlockSpec(memory_space=pltpu.VM...]
  transfers between devices with their start and end apart: 5 -> 5, of which waited for: 2 -> 3; matrix products, arithmetic and copies ran while one was open for 1% -> 1% of each run, Pallas kernels for 10% -> 9%
where the time goes in v4:
time: 75 us; the launch traced here: 74.7 us
  waiting for transfers between devices  28.9 us (39%)
  starting transfers between devices  27.7 us (37%)
  Pallas kernels  15.8 us (21%)
  other arithmetic  1.48 us (2%)
  between operations  0.77 us (1%)
    all_to_all x1, waiting for transfers between devices, on_device(): lax.all_to_all(sent.reshape(senders, CHUNK, LANES), 'subj', split_axis=0,...  16.1 us
    all_to_all x1, starting transfers between devices, on_device(): lax.all_to_all(sent.reshape(senders, CHUNK, LANES), 'subj', split_axis=0,...  13.8 us
    all_to_all x1, waiting for transfers between devices, on_device(): lax.all_to_all(mine, ('subj', 'strip'), split_axis=0, concat_axis=0, tile...  12.1 us
    all_to_all x1, starting transfers between devices, on_device(): lax.all_to_all(mine, ('subj', 'strip'), split_axis=0, concat_axis=0, tile...  8.3 us
    pallas_call x1, Pallas kernels, block_stats(): pl.pallas_call(functools.partial(stats_kernel, senders), out_shape=(jax.S...  4.88 us
    ppermute x1, starting transfers between devices, on_device(): left = lax.ppermute(high, 'strip', [(i, i + 1) for i in range(strips - 1)])  4.08 us
    pallas_call x1, Pallas kernels, design_rows(): pl.pallas_call(designs_kernel, out_shape=jax.ShapeDtypeStruct((3 * GROUP,...  3.96 us
    pallas_call x1, Pallas kernels, inner_codes(): pl.pallas_call(inner_kernel, in_specs=[pl.BlockSpec(memory_space=pltpu.VM...  2.86 us
  transfers between devices with their start and end apart: 5, of which 3 were waited for; matrix products, arithmetic and copies ran while one was open for 1% of the time, Pallas kernels for 9%

profile of v4, /device:TPU:1, one launch (start us, length us, event | category | flops | bytes accessed | tf_op | source)
XLA Modules:
  0.0 74.7 jit_solution(2585889385712855450)
XLA Ops:
  0.6 2.9 %strip_edges.1 = (bf16[48,512]{1,0:T(8,128)(2,1)S(1)}, bf16[48,512]{1,0:T(8,128)(2,1)S(1)}, bf16[2,3,4,512,128]{4,3,2,1,0:T(8,128)(2,1)S(1)}) custom-call(bf16[2,3,4,512,128]{4,3,2,1,0:T(8,128)(2,1)} %disp_ref.1), custom_call_target="tpu_custom_call" | custom-call | flops 100000000 | bytes 3200000 | tf_op jit(solution)/shard_map/strip_edges/pallas_call | solution.py:91
  3.5 0.0 copy-start
  3.5 0.0 copy-start.1
  3.5 0.0 copy-start.2
  3.5 4.1 %collective-permute-start = (bf16[48,512]{1,0:T(8,128)(2,1)S(1)}, bf16[48,512]{1,0:T(8,128)(2,1)S(1)}, u32[]{:S(2)}, u32[]{:S(2)}) collective-permute-start(bf16[48,512]{1,0:T(8,128)(2,1)S(1)} %get-tuple-element.10.high_ref), channel_id=1, source_target_pairs={{0,1},{1,2},{2,3},{4,5},{5,6},{6,7},{8,9},{9,10},{10,11},{12,13},{... | collective-permute-start | bytes 147464 | tf_op jit(solution)/shard_map/ppermute | solution.py:443
  7.6 1.3 %collective-permute-start.1 = (bf16[48,512]{1,0:T(8,128)(2,1)S(1)}, bf16[48,512]{1,0:T(8,128)(2,1)S(1)}, u32[]{:S(2)}, u32[]{:S(2)}) collective-permute-start(bf16[48,512]{1,0:T(8,128)(2,1)S(1)} %get-tuple-element.9.low_ref), channel_id=1, source_target_pairs={{1,0},{2,1},{3,2},{5,4},{6,5},{7,6},{9,8},{10,9},{11,10},{13,12},{... | collective-permute-start | bytes 147464 | tf_op jit(solution)/shard_map/ppermute | solution.py:444
  8.9 2.9 %inner_codes.1 = (s16[2,2,32,16,128]{4,3,2,1,0:T(8,128)(2,1)S(1)}, f32[4,2,32,128]{3,2,1,0:T(8,128)S(1)}) custom-call(bf16[2,3,4,512,128]{4,3,2,1,0:T(8,128)(2,1)S(1)} %get-tuple-element.11.disp_ref), custom_call_target="tpu_custom_call" | custom-call | flops 20000000 | bytes 4200000 | tf_op jit(solution)/shard_map/inner_codes/pallas_call | solution.py:143
  11.8 0.0 collective-permute-done.left_ref
  11.8 0.7 collective-permute-done.1.right_ref
  12.4 1.2 %with_tails.1 = s16[32,80,128]{2,1,0:T(8,128)(2,1)} custom-call(bf16[48,512]{1,0:T(8,128)(2,1)S(1)} %get-tuple-element.9.low_ref, bf16[48,512]{1,0:T(8,128)(2,1)S(1)} %get-tuple-element.10.high_ref, bf16[48,512]{1,0:T(8,128)(2,1)S(1)} %collective-permute-done.left_ref, bf16[48,512]{1,0:T(8,128)(2,1)S(1)} %collective-permute-done.1.right_ref, ...), custom_call_target="tpu_custom_call" | custom-call | flops 1000000 | bytes 500000 | tf_op jit(solution)/shard_map/with_tails/pallas_call | solution.py:247
  13.7 13.8 %all-to-all-start = ((s16[64,40,128]{2,1,0:T(8,128)(2,1)}), s16[64,40,128]{2,1,0:T(8,128)(2,1)S(1)}, u32[]{:S(2)}, u32[]{:S(2)}) async-start(s16[64,40,128]{2,1,0:T(8,128)(2,1)} %bitcast.21), calls=%async_computation | async-start | bytes 1310720 | tf_op jit(solution)/shard_map/all_to_all | solution.py:448
  27.5 0.0 copy-done
  27.5 0.0 copy-done.1
  27.5 0.0 copy-done.2
  27.5 4.0 %design_rows.1.rows_ref = bf16[816,384]{1,0:T(8,128)(2,1)S(1)} custom-call(f32[1,128]{1,0:T(1,128)S(1)} %bitcast.19, s32[1,128]{1,0:T(1,128)S(1)} %bitcast.20, s32[256,128]{1,0:T(8,128)S(1)} %copy-done), custom_call_target="tpu_custom_call" | custom-call | flops 4000000 | bytes 800000 | tf_op jit(solution)/shard_map/design_rows/pallas_call | solution.py:313
  31.5 16.1 %all-to-all-done = s16[64,40,128]{2,1,0:T(8,128)(2,1)S(1)} async-done(((s16[64,40,128]{2,1,0:T(8,128)(2,1)}), s16[64,40,128]{2,1,0:T(8,128)(2,1)S(1)}, u32[]{:S(2)}, u32[]{:S(2)}) %all-to-all-start) | async-done | bytes 655392 | tf_op jit(solution)/shard_map/all_to_all | solution.py:448
  47.6 4.9 %block_stats.1 = (f32[2,8,128]{2,1,0:T(8,128)S(1)}, s16[256,2,128]{2,1,0:T(2,128)(2,1)}) custom-call(s16[2560,128]{1,0:T(8,128)(2,1)S(1)} %bitcast.18, bf16[816,384]{1,0:T(8,128)(2,1)S(1)} %design_rows.1.rows_ref), custom_call_target="tpu_custom_call" | custom-call | flops 2000000000 | bytes 1000000 | tf_op jit(solution)/shard_map/block_stats/pallas_call | solution.py:419
  52.5 0.3 collective-permute-start.2
  52.8 8.3 %all-to-all-start.1 = ((s16[256,2,128]{2,1,0:T(2,128)(2,1)}), s16[256,2,128]{2,1,0:T(2,128)(2,1)S(1)}, u32[]{:S(2)}, u32[]{:S(2)}) async-start(s16[256,2,128]{2,1,0:T(2,128)(2,1)} %get-tuple-element.15), calls=%async_computation.1 | async-start | bytes 262144 | tf_op jit(solution)/shard_map/all_to_all | solution.py:458
  61.1 0.0 collective-permute-done.2
  61.1 0.6 pad_maximum_fusion
  61.7 12.1 %all-to-all-done.1 = s16[256,2,128]{2,1,0:T(2,128)(2,1)S(1)} async-done(((s16[256,2,128]{2,1,0:T(2,128)(2,1)}), s16[256,2,128]{2,1,0:T(2,128)(2,1)S(1)}, u32[]{:S(2)}, u32[]{:S(2)}) %all-to-all-start.1) | async-done | bytes 131104 | tf_op jit(solution)/shard_map/all_to_all | solution.py:458
  73.8 0.9 %multiply_reduce_fusion = f32[2,128]{1,0:T(2,128)} fusion(s16[256,2,128]{2,1,0:T(2,128)(2,1)S(1)} %all-to-all-done.1), kind=kLoop, calls=%fused_computation | loop fusion | flops 327424 | bytes 132096 | tf_op jit(solution)/shard_map/reduce_max | solution.py:460
  (2 shorter events, 0.0 us)
Async XLA Ops:
  3.5 24.0 %copy-start = (s32[256,128]{1,0:T(8,128)S(1)}, s32[256,128]{1,0:T(8,128)}, u32[]{:S(2)}) copy-start(s32[256,128]{1,0:T(8,128)} %perms_ref.1) | copy-start | bytes 393220
  3.5 24.0 %copy-start.1 = (f32[128]{0:T(128)S(1)}, f32[128]{0:T(128)}, u32[]{:S(2)}) copy-start(f32[128]{0:T(128)} %param.5) | copy-start | bytes 1540
  3.5 24.0 %copy-start.2 = (s32[128]{0:T(128)S(1)}, s32[128]{0:T(128)}, u32[]{:S(2)}) copy-start(s32[128]{0:T(128)} %param.6) | copy-start | bytes 1540
  3.5 8.3 %collective-permute-start = (bf16[48,512]{1,0:T(8,128)(2,1)S(1)}, bf16[48,512]{1,0:T(8,128)(2,1)S(1)}, u32[]{:S(2)}, u32[]{:S(2)}) collective-permute-start(bf16[48,512]{1,0:T(8,128)(2,1)S(1)} %get-tuple-element.10.high_ref), channel_id=1, source_target_pairs={{0,1},{1,2},{2,3},{4,5},{5,6},{6,7},{8,9},{9,10},{10,11},{12,13},{... | collective-permute-start | bytes 147464 | tf_op jit(solution)/shard_map/ppermute | solution.py:443
  7.6 4.8 %collective-permute-start.1 = (bf16[48,512]{1,0:T(8,128)(2,1)S(1)}, bf16[48,512]{1,0:T(8,128)(2,1)S(1)}, u32[]{:S(2)}, u32[]{:S(2)}) collective-permute-start(bf16[48,512]{1,0:T(8,128)(2,1)S(1)} %get-tuple-element.9.low_ref), channel_id=1, source_target_pairs={{1,0},{2,1},{3,2},{5,4},{6,5},{7,6},{9,8},{10,9},{11,10},{13,12},{... | collective-permute-start | bytes 147464 | tf_op jit(solution)/shard_map/ppermute | solution.py:444
  13.7 33.9 %all-to-all-start = ((s16[64,40,128]{2,1,0:T(8,128)(2,1)}), s16[64,40,128]{2,1,0:T(8,128)(2,1)S(1)}, u32[]{:S(2)}, u32[]{:S(2)}) async-start(s16[64,40,128]{2,1,0:T(8,128)(2,1)} %bitcast.21), calls=%async_computation | async-start | bytes 1310720 | tf_op jit(solution)/shard_map/all_to_all | solution.py:448
  52.5 8.6 %collective-permute-start.2 = (f32[8,128]{1,0:T(8,128)S(1)}, f32[8,128]{1,0:T(8,128)S(1)}, u32[]{:S(2)}, u32[]{:S(2)}) collective-permute-start(f32[8,128]{1,0:T(8,128)S(1)} %slice_bitcast_fusion), channel_id=1, source_target_pairs={{0,4},{4,0},{8,12},{12,8},{16,20},{20,16},{24,28},{28,24},{32,36},... | collective-permute-start | bytes 12296 | tf_op jit(solution)/shard_map/ppermute | solution.py:455
  52.8 21.0 %all-to-all-start.1 = ((s16[256,2,128]{2,1,0:T(2,128)(2,1)}), s16[256,2,128]{2,1,0:T(2,128)(2,1)S(1)}, u32[]{:S(2)}, u32[]{:S(2)}) async-start(s16[256,2,128]{2,1,0:T(2,128)(2,1)} %get-tuple-element.15), calls=%async_computation.1 | async-start | bytes 262144 | tf_op jit(solution)/shard_map/all_to_all | solution.py:458

commit v5 on v4

--- a/solution.py
+++ b/solution.py
@@ -64,9 +64,9 @@
     ]
     for copy in copies:
         copy.start()
-    row = lax.broadcasted_iota(jnp.int32, (32, 2 * LANES), 0)
-    lane = lax.broadcasted_iota(jnp.int32, (32, 2 * LANES), 1)
-    column = jnp.where(row < 16, row // 8, row // 8 - 2 + LANES - 2)
+    row = lax.broadcasted_iota(jnp.int32, (48, 2 * LANES), 0)
+    lane = lax.broadcasted_iota(jnp.int32, (48, 2 * LANES), 1)
+    column = jnp.where(row < 16, row // 8, row // 8 - 2 + LANES - 4)
     picks = [
         ((row % 8 == 2 * q + lane // LANES) & (lane % LANES == column)).astype(F32).astype(BF16)
         for q in range(PLANES)
@@ -75,24 +75,24 @@
         copies[h].wait()
         at = slice(h * rows, (h + 1) * rows)
         for c in range(COMPS):
-            acc = jnp.zeros((32, rows), F32)
+            acc = jnp.zeros((48, rows), F32)
             for q in range(PLANES):
                 both = jnp.concatenate([field_ref[0, c, q, at, :], field_ref[1, c, q, at, :]], axis=1)
                 acc = acc + lax.dot_general(
                     picks[q], both, (((1,), (1,)), ((), ())), preferred_element_type=F32
                 )
             low_ref[c * 16 : c * 16 + 16, at] = acc[0:16].astype(BF16)
-            high_ref[c * 16 : c * 16 + 16, at] = acc[16:32].astype(BF16)
+            high_ref[c * 32 : c * 32 + 32, at] = acc[16:48].astype(BF16)
 
 
 def strip_edges(disp):
     parts = 4
-    out = pltpu.VMEM((COMPS * 16, ROWS), BF16)
+    out = [pltpu.VMEM((COMPS * rows, ROWS), BF16) for rows in (16, 32)]
     return pl.pallas_call(
         functools.partial(edges_kernel, parts),
         in_specs=[pl.BlockSpec(memory_space=pltpu.HBM)],
         out_specs=[pl.BlockSpec(memory_space=pltpu.VMEM)] * 3,
-        out_shape=(out, out, pltpu.VMEM(disp.shape, BF16)),
+        out_shape=(*out, pltpu.VMEM(disp.shape, BF16)),
         scratch_shapes=[pltpu.SemaphoreType.DMA((parts,))],
         compiler_params=pltpu.CompilerParams(vmem_limit_bytes=8 * 2**20),
         cost_estimate=pl.CostEstimate(flops=10**8, bytes_accessed=3_200_000, transcendentals=0),
@@ -158,7 +158,7 @@
     )(pltpu.with_memory_space_constraint(disp, pltpu.VMEM))
 
 
-def tail_kernel(low_ref, high_ref, left_ref, right_ref, beside_ref, main_ref, out_ref, pad_ref, side_ref, tail_ref, send_ref, sem):
+def tail_kernel(low_ref, high_ref, left_ref, beside_ref, main_ref, out_ref, pad_ref, side_ref, tail_ref, send_ref, sem):
     copies = [
         pltpu.make_async_copy(
             main_ref.at[s, p],
@@ -170,14 +170,14 @@
     ]
     for copy in copies:
         copy.start()
-    strips = lax.axis_size("strip")
-    me = lax.axis_index("strip")
-    keep_left = (me > 0).astype(F32)
-    keep_right = (me < strips - 1).astype(F32)
+    inside = (lax.axis_index("strip") > 0).astype(F32)
     lane = lax.broadcasted_iota(jnp.int32, (8, ROWS), 1)
 
     def columns(ref):
-        return [[ref[16 * c + 8 * e : 16 * c + 8 * e + 8, :] for e in range(2)] for c in range(COMPS)]
+        many = ref.shape[0] // (8 * COMPS)
+        return [
+            [ref[8 * (many * c + e) : 8 * (many * c + e) + 8, :] for e in range(many)] for c in range(COMPS)
+        ]
 
     def codes(around):
         dz, dx, dy = [], [], []
@@ -190,38 +190,35 @@
             dy.append(after - before)
         return encode(log_det(dz, dx, dy))
 
-    low, high, left, right = (
-        columns(ref[...].astype(F32)) for ref in (low_ref, high_ref, left_ref, right_ref)
-    )
-    wide_left = [left[c] + low[c] for c in range(COMPS)]
-    wide_right = [high[c] + right[c] for c in range(COMPS)]
-    four = [
-        codes([w[0:3] for w in wide_left]) * keep_left,
-        codes([w[1:4] for w in wide_left]),
-        codes([w[0:3] for w in wide_right]),
-        codes([w[1:4] for w in wide_right]) * keep_right,
+    low, high, left = (columns(ref[...].astype(F32)) for ref in (low_ref, high_ref, left_ref))
+    five = [
+        codes([w[0:3] for w in left]),
+        codes([w[1:4] for w in left]),
+        codes([(w[2], w[3], v[0] * inside) for w, v in zip(left, low)]),
+        codes([(w[3] * inside, v[0], v[1]) for w, v in zip(left, low)]),
+        codes([w[1:4] for w in high]),
     ]
     zeros = jnp.zeros((8, LANES), F32)
-    for k in range(4):
+    for k in range(5):
         pad_ref[k, :, 0:LANES] = zeros
-        pad_ref[k, :, LANES : LANES + ROWS] = four[k]
+        pad_ref[k, :, LANES : LANES + ROWS] = five[k]
         pad_ref[k, :, LANES + ROWS : 2 * LANES + ROWS] = zeros
     here = lax.broadcasted_iota(jnp.int32, (8, LANES), 1)
     blocks = ROWS // BLOCK
     for j in range(blocks):
         start = LANES + j * BLOCK - 1
         line = zeros
-        for k in range(4):
+        for k in range(5):
             window, offset = start // LANES, start % LANES
             first = pltpu.roll(
-                pad_ref[k, :, window * LANES : (window + 1) * LANES], (32 * k - offset) % LANES, 1
+                pad_ref[k, :, window * LANES : (window + 1) * LANES], (24 * k - offset) % LANES, 1
             )
             if offset + 18 > LANES:
                 second = pltpu.roll(
-                    pad_ref[k, :, (window + 1) * LANES : (window + 2) * LANES], (32 * k - offset) % LANES, 1
+                    pad_ref[k, :, (window + 1) * LANES : (window + 2) * LANES], (24 * k - offset) % LANES, 1
                 )
-                first = jnp.where(here - 32 * k < LANES - offset, first, second)
-            line = first if k == 0 else jnp.where(here < 32 * k, line, first)
+                first = jnp.where(here - 24 * k < LANES - offset, first, second)
+            line = first if k == 0 else jnp.where(here < 24 * k, line, first)
         side_ref[j * 8 : j * 8 + 8, :] = line
     for p in range(2):
         for s in range(PER):
@@ -241,16 +238,16 @@
         copy.wait()
 
 
-def with_tails(low, high, left, right, beside, main):
+def with_tails(low, high, left, beside, main):
     blocks = ROWS // BLOCK
     vmem = pl.BlockSpec(memory_space=pltpu.VMEM)
     return pl.pallas_call(
         tail_kernel,
-        in_specs=[vmem] * 6,
+        in_specs=[vmem] * 5,
         out_specs=pl.BlockSpec(memory_space=pltpu.HBM),
         out_shape=pltpu.HBM((blocks, PAIR, LANES), I16),
         scratch_shapes=[
-            pltpu.VMEM((4, 8, ROWS + 2 * LANES), F32),
+            pltpu.VMEM((5, 8, ROWS + 2 * LANES), F32),
             pltpu.VMEM((blocks * 8 + 8, LANES), F32),
             pltpu.VMEM((blocks * 2 * TAIL + 16, LANES), F32),
             pltpu.VMEM((blocks, 2 * TAIL, LANES), I16),
@@ -259,7 +256,7 @@
         compiler_params=pltpu.CompilerParams(vmem_limit_bytes=8 * 2**20),
         cost_estimate=pl.CostEstimate(flops=10**6, bytes_accessed=5 * 10**5, transcendentals=5 * 10**4),
         name="with_tails",
-    )(*(pltpu.with_memory_space_constraint(x, pltpu.VMEM) for x in (low, high, left, right, beside, main)))
+    )(*(pltpu.with_memory_space_constraint(x, pltpu.VMEM) for x in (low, high, left, beside, main)))
 
 
 def designs_kernel(age_ref, code_ref, perms_ref, out_ref):
@@ -349,16 +346,16 @@
         y_ref[2 * subjects : 3 * subjects, at] = high
 
     far = lane // 2 + jnp.where(lane % 2 == 0, 97, 1)
-    near = (lane - 36) // 2 + jnp.where(lane % 2 == 0, 64, 32)
+    near = (lane - 36) // 3 + 24 * ((lane - 36) % 3 + 1)
     sides = jnp.take_along_axis(
         gathered([tail + 2, tail + 6]),
-        jnp.where(lane < 32, far, jnp.where((lane >= 36) & (lane < 72), near, 0)),
+        jnp.where(lane < 32, far, jnp.where((lane >= 36) & (lane < 90), near, 0)),
         axis=1,
     )
 
     def mended(y, r):
-        ends = pltpu.roll(sides, LANES - 39 - 2 * r, 1)
-        return jnp.where((lane == 0) | (lane == LANES - 1), ends, y)
+        ends = pltpu.roll(sides, LANES - 41 - 3 * r, 1)
+        return jnp.where((lane == 0) | (lane >= LANES - 2), ends, y)
 
     for r in range(BLOCK):
         place(r, mended(gathered([main + r, main + BLOCK + r]), r))
@@ -375,6 +372,10 @@
         top_ref[:, at] = q3
 
     here = lax.broadcasted_iota(jnp.int32, (8, LANES), 1)
+    first = lax.axis_index("strip") == 0
+    seam = (here == LANES - 3) | (here == LANES - 2)
+    from_before = (here == LANES - 2) | ((here == 0) & first)
+    from_after = (here == LANES - 3) | ((here == LANES - 1) & first)
     unscale = ((subjects - 4) / 0.15) ** 0.5
 
     def pseudo_t(g, r):
@@ -386,9 +387,9 @@
         mine = block(r)
         above = block(r - 1 if r > 0 else BLOCK)
         below = block(r + 1 if r < BLOCK - 1 else BLOCK + 1)
-        ends = pltpu.roll(block(BLOCK + 2), LANES - 1 - 2 * r, 1)
-        before = jnp.where(here == 0, ends, pltpu.roll(mine, 1, 1))
-        after = jnp.where(here == LANES - 1, ends, pltpu.roll(mine, LANES - 1, 1))
+        ends = jnp.where(seam, pltpu.roll(block(BLOCK + 2), LANES - 3 - 2 * r, 1), FLOOR)
+        before = jnp.where(from_before, ends, pltpu.roll(mine, 1, 1))
+        after = jnp.where(from_after, ends, pltpu.roll(mine, LANES - 1, 1))
         beside = (above + below) + (before + after)
         variance = CENTRE * mine + beside
         return top_ref[at, r * LANES : (r + 1) * LANES] * lax.rsqrt(variance)
@@ -440,11 +441,10 @@
     senders = lax.axis_size("subj")
     strips = lax.axis_size("strip")
     low, high, field = strip_edges(displacement)
-    left = lax.ppermute(high, "strip", [(i, i + 1) for i in range(strips - 1)])
-    right = lax.ppermute(low, "strip", [(i + 1, i) for i in range(strips - 1)])
+    left = lax.ppermute(high, "strip", [(i, (i + 1) % strips) for i in range(strips)])
     main, beside = inner_codes(field)
     rows = design_rows(age, group_codes, perms)
-    sent = with_tails(low, high, left, right, beside, main)
+    sent = with_tails(low, high, left, beside, main)
     codes = lax.all_to_all(
         sent.reshape(senders, CHUNK, LANES), "subj", split_axis=0, concat_axis=0, tiled=True
     )
@@ -454,6 +454,8 @@
     odd = lax.axis_index("subj") % 2 == 1
     swapped = lax.ppermute(tested[1], "subj", [(i, i ^ 1) for i in range(senders)])
     t_map = jnp.stack([jnp.where(odd, swapped, tested[0]), jnp.where(odd, tested[0], swapped)])
+    beyond = lax.ppermute(t_map, "strip", [((i + 1) % strips, i) for i in range(strips)])
+    t_map = jnp.where(lax.broadcasted_iota(jnp.int32, t_map.shape, 2) >= LANES - 2, beyond, t_map)
 
     theirs = lax.all_to_all(mine, ("subj", "strip"), split_axis=0, concat_axis=0, tiled=True)
     root = theirs.astype(F32) * (REACH_T**0.25 / LEVELS)

time: 75 us -> 70.5 us (0.940)
  waiting for transfers between devices: 28.9 us -> 26 us
  starting transfers between devices: 27.7 us -> 26.1 us
    all_to_all x1, waiting for transfers between devices: 12.1 us -> 8.64 us  [on_device(): lax.all_to_all(mine, ('subj', 'strip'), split_axis=0, concat_axis=0, tile...]
    all_to_all x1, starting transfers between devices: 8.3 us -> 7.38 us  [on_device(): lax.all_to_all(mine, ('subj', 'strip'), split_axis=0, concat_axis=0, tile...]
  transfers between devices with their start and end apart: 5 -> 5, of which waited for: 3 -> 4; matrix products, arithmetic and copies ran while one was open for 1% -> 1% of each run, Pallas kernels for 9% -> 10%
where the time goes in v5:
time: 70.5 us; the launch traced here: 70.3 us
  starting transfers between devices  26.1 us (37%)
  waiting for transfers between devices  26 us (37%)
  Pallas kernels  15.9 us (23%)
  other arithmetic  1.49 us (2%)
  between operations  0.75 us (1%)
    all_to_all x1, waiting for transfers between devices, on_device(): lax.all_to_all(sent.reshape(senders, CHUNK, LANES), 'subj', split_axis=0,...  16.1 us
    all_to_all x1, starting transfers between devices, on_device(): lax.all_to_all(sent.reshape(senders, CHUNK, LANES), 'subj', split_axis=0,...  13.7 us
    all_to_all x1, waiting for transfers between devices, on_device(): lax.all_to_all(mine, ('subj', 'strip'), split_axis=0, concat_axis=0, tile...  8.64 us
    all_to_all x1, starting transfers between devices, on_device(): lax.all_to_all(mine, ('subj', 'strip'), split_axis=0, concat_axis=0, tile...  7.38 us
    pallas_call x1, Pallas kernels, block_stats(): pl.pallas_call(functools.partial(stats_kernel, senders), out_shape=(jax.S...  4.93 us
    pallas_call x1, Pallas kernels, design_rows(): pl.pallas_call(designs_kernel, out_shape=jax.ShapeDtypeStruct((3 * GROUP,...  3.96 us
    pallas_call x1, Pallas kernels, strip_edges(): pl.pallas_call(functools.partial(edges_kernel, parts), in_specs=[pl.Block...  2.9 us
    pallas_call x1, Pallas kernels, inner_codes(): pl.pallas_call(inner_kernel, in_specs=[pl.BlockSpec(memory_space=pltpu.VM...  2.85 us
  transfers between devices with their start and end apart: 5, of which 4 were waited for; matrix products, arithmetic and copies ran while one was open for 1% of the time, Pallas kernels for 10%

profile of v5, /device:TPU:1, one launch (start us, length us, event | category | flops | bytes accessed | tf_op | source)
XLA Modules:
  0.0 70.3 jit_solution(7550334090547315124)
XLA Ops:
  0.6 2.9 %strip_edges.1 = (bf16[48,512]{1,0:T(8,128)(2,1)S(1)}, bf16[96,512]{1,0:T(8,128)(2,1)S(1)}, bf16[2,3,4,512,128]{4,3,2,1,0:T(8,128)(2,1)S(1)}) custom-call(bf16[2,3,4,512,128]{4,3,2,1,0:T(8,128)(2,1)} %disp_ref.1), custom_call_target="tpu_custom_call" | custom-call | flops 100000000 | bytes 3200000 | tf_op jit(solution)/shard_map/strip_edges/pallas_call | solution.py:91
  3.5 0.0 copy-start
  3.5 0.0 copy-start.1
  3.6 0.0 copy-start.2
  3.6 2.1 %collective-permute-start = (bf16[96,512]{1,0:T(8,128)(2,1)S(1)}, bf16[96,512]{1,0:T(8,128)(2,1)S(1)}, u32[]{:S(2)}, u32[]{:S(2)}) collective-permute-start(bf16[96,512]{1,0:T(8,128)(2,1)S(1)} %get-tuple-element.10.high_ref), channel_id=1, source_target_pairs={{0,1},{1,2},{2,3},{3,0},{4,5},{5,6},{6,7},{7,4},{8,9},{9,10},{10,1... | collective-permute-start | bytes 294920 | tf_op jit(solution)/shard_map/ppermute | solution.py:444
  5.7 2.9 %inner_codes.1 = (s16[2,2,32,16,128]{4,3,2,1,0:T(8,128)(2,1)S(1)}, f32[4,2,32,128]{3,2,1,0:T(8,128)S(1)}) custom-call(bf16[2,3,4,512,128]{4,3,2,1,0:T(8,128)(2,1)S(1)} %get-tuple-element.11.disp_ref), custom_call_target="tpu_custom_call" | custom-call | flops 20000000 | bytes 4200000 | tf_op jit(solution)/shard_map/inner_codes/pallas_call | solution.py:143
  8.5 0.4 collective-permute-done.left_ref
  9.0 1.3 %with_tails.1 = s16[32,80,128]{2,1,0:T(8,128)(2,1)} custom-call(bf16[48,512]{1,0:T(8,128)(2,1)S(1)} %get-tuple-element.9.low_ref, bf16[96,512]{1,0:T(8,128)(2,1)S(1)} %get-tuple-element.10.high_ref, bf16[96,512]{1,0:T(8,128)(2,1)S(1)} %collective-permute-done.left_ref, f32[4,2,32,128]{3,2,1,0:T(8,128)S(1)} %get-tuple-element.12.beside_ref, ...), custom_call_target="tpu_custom_call" | custom-call | flops 1000000 | bytes 500000 | tf_op jit(solution)/shard_map/with_tails/pallas_call | solution.py:244
  10.3 13.7 %all-to-all-start = ((s16[64,40,128]{2,1,0:T(8,128)(2,1)}), s16[64,40,128]{2,1,0:T(8,128)(2,1)S(1)}, u32[]{:S(2)}, u32[]{:S(2)}) async-start(s16[64,40,128]{2,1,0:T(8,128)(2,1)} %bitcast.21), calls=%async_computation | async-start | bytes 1310720 | tf_op jit(solution)/shard_map/all_to_all | solution.py:448
  24.0 0.0 copy-done
  24.0 0.0 copy-done.1
  24.0 0.0 copy-done.2
  24.0 4.0 %design_rows.1.rows_ref = bf16[816,384]{1,0:T(8,128)(2,1)S(1)} custom-call(f32[1,128]{1,0:T(1,128)S(1)} %bitcast.19, s32[1,128]{1,0:T(1,128)S(1)} %bitcast.20, s32[256,128]{1,0:T(8,128)S(1)} %copy-done), custom_call_target="tpu_custom_call" | custom-call | flops 4000000 | bytes 800000 | tf_op jit(solution)/shard_map/design_rows/pallas_call | solution.py:310
  28.0 16.1 %all-to-all-done = s16[64,40,128]{2,1,0:T(8,128)(2,1)S(1)} async-done(((s16[64,40,128]{2,1,0:T(8,128)(2,1)}), s16[64,40,128]{2,1,0:T(8,128)(2,1)S(1)}, u32[]{:S(2)}, u32[]{:S(2)}) %all-to-all-start) | async-done | bytes 655392 | tf_op jit(solution)/shard_map/all_to_all | solution.py:448
  44.1 4.9 %block_stats.1 = (f32[2,8,128]{2,1,0:T(8,128)S(1)}, s16[256,2,128]{2,1,0:T(2,128)(2,1)}) custom-call(s16[2560,128]{1,0:T(8,128)(2,1)S(1)} %bitcast.18, bf16[816,384]{1,0:T(8,128)(2,1)S(1)} %design_rows.1.rows_ref), custom_call_target="tpu_custom_call" | custom-call | flops 2000000000 | bytes 1000000 | tf_op jit(solution)/shard_map/block_stats/pallas_call | solution.py:420
  49.0 0.3 collective-permute-start.1
  49.3 7.4 %all-to-all-start.1 = ((s16[256,2,128]{2,1,0:T(2,128)(2,1)}), s16[256,2,128]{2,1,0:T(2,128)(2,1)S(1)}, u32[]{:S(2)}, u32[]{:S(2)}) async-start(s16[256,2,128]{2,1,0:T(2,128)(2,1)} %get-tuple-element.15), calls=%async_computation.1 | async-start | bytes 262144 | tf_op jit(solution)/shard_map/all_to_all | solution.py:460
  56.7 0.0 collective-permute-done.1
  56.7 2.7 %collective-permute-start.2 = (f32[2,8,128]{2,1,0:T(8,128)S(1)}, f32[2,8,128]{2,1,0:T(8,128)S(1)}, u32[]{:S(2)}, u32[]{:S(2)}) collective-permute-start(f32[2,8,128]{2,1,0:T(8,128)S(1)} %pad_maximum_fusion), channel_id=1, source_target_pairs={{1,0},{2,1},{3,2},{0,3},{5,4},{6,5},{7,6},{4,7},{9,8},{10,9},{11,1... | collective-permute-start | bytes 24584 | tf_op jit(solution)/shard_map/ppermute | solution.py:457
  59.4 0.8 %collective-permute-done.2 = f32[2,8,128]{2,1,0:T(8,128)S(1)} collective-permute-done((f32[2,8,128]{2,1,0:T(8,128)S(1)}, f32[2,8,128]{2,1,0:T(8,128)S(1)}, u32[]{:S(2)}, u32[]{:S(2)}) %collective-permute-start.2) | collective-permute-done | bytes 8224 | tf_op jit(solution)/shard_map/ppermute | solution.py:457
  60.2 0.6 broadcast_select_fusion
  60.8 8.6 %all-to-all-done.1 = s16[256,2,128]{2,1,0:T(2,128)(2,1)S(1)} async-done(((s16[256,2,128]{2,1,0:T(2,128)(2,1)}), s16[256,2,128]{2,1,0:T(2,128)(2,1)S(1)}, u32[]{:S(2)}, u32[]{:S(2)}) %all-to-all-start.1) | async-done | bytes 131104 | tf_op jit(solution)/shard_map/all_to_all | solution.py:460
  69.4 0.9 %multiply_reduce_fusion = f32[2,128]{1,0:T(2,128)} fusion(s16[256,2,128]{2,1,0:T(2,128)(2,1)S(1)} %all-to-all-done.1), kind=kLoop, calls=%fused_computation | loop fusion | flops 327424 | bytes 132096 | tf_op jit(solution)/shard_map/reduce_max | solution.py:462
  (4 shorter events, 0.0 us)
Async XLA Ops:
  3.5 20.4 %copy-start = (s32[256,128]{1,0:T(8,128)S(1)}, s32[256,128]{1,0:T(8,128)}, u32[]{:S(2)}) copy-start(s32[256,128]{1,0:T(8,128)} %perms_ref.1) | copy-start | bytes 393220
  3.5 20.4 %copy-start.1 = (f32[128]{0:T(128)S(1)}, f32[128]{0:T(128)}, u32[]{:S(2)}) copy-start(f32[128]{0:T(128)} %param.5) | copy-start | bytes 1540
  3.6 20.4 %copy-start.2 = (s32[128]{0:T(128)S(1)}, s32[128]{0:T(128)}, u32[]{:S(2)}) copy-start(s32[128]{0:T(128)} %param.6) | copy-start | bytes 1540
  3.6 5.4 %collective-permute-start = (bf16[96,512]{1,0:T(8,128)(2,1)S(1)}, bf16[96,512]{1,0:T(8,128)(2,1)S(1)}, u32[]{:S(2)}, u32[]{:S(2)}) collective-permute-start(bf16[96,512]{1,0:T(8,128)(2,1)S(1)} %get-tuple-element.10.high_ref), channel_id=1, source_target_pairs={{0,1},{1,2},{2,3},{3,0},{4,5},{5,6},{6,7},{7,4},{8,9},{9,10},{10,1... | collective-permute-start | bytes 294920 | tf_op jit(solution)/shard_map/ppermute | solution.py:444
  10.3 33.8 %all-to-all-start = ((s16[64,40,128]{2,1,0:T(8,128)(2,1)}), s16[64,40,128]{2,1,0:T(8,128)(2,1)S(1)}, u32[]{:S(2)}, u32[]{:S(2)}) async-start(s16[64,40,128]{2,1,0:T(8,128)(2,1)} %bitcast.21), calls=%async_computation | async-start | bytes 1310720 | tf_op jit(solution)/shard_map/all_to_all | solution.py:448
  49.0 7.7 %collective-permute-start.1 = (f32[8,128]{1,0:T(8,128)S(1)}, f32[8,128]{1,0:T(8,128)S(1)}, u32[]{:S(2)}, u32[]{:S(2)}) collective-permute-start(f32[8,128]{1,0:T(8,128)S(1)} %slice_bitcast_fusion), channel_id=1, source_target_pairs={{0,4},{4,0},{8,12},{12,8},{16,20},{20,16},{24,28},{28,24},{32,36},... | collective-permute-start | bytes 12296 | tf_op jit(solution)/shard_map/ppermute | solution.py:455
  49.3 20.1 %all-to-all-start.1 = ((s16[256,2,128]{2,1,0:T(2,128)(2,1)}), s16[256,2,128]{2,1,0:T(2,128)(2,1)S(1)}, u32[]{:S(2)}, u32[]{:S(2)}) async-start(s16[256,2,128]{2,1,0:T(2,128)(2,1)} %get-tuple-element.15), calls=%async_computation.1 | async-start | bytes 262144 | tf_op jit(solution)/shard_map/all_to_all | solution.py:460
  56.7 3.5 %collective-permute-start.2 = (f32[2,8,128]{2,1,0:T(8,128)S(1)}, f32[2,8,128]{2,1,0:T(8,128)S(1)}, u32[]{:S(2)}, u32[]{:S(2)}) collective-permute-start(f32[2,8,128]{2,1,0:T(8,128)S(1)} %pad_maximum_fusion), channel_id=1, source_target_pairs={{1,0},{2,1},{3,2},{0,3},{5,4},{6,5},{7,6},{4,7},{9,8},{10,9},{11,1... | collective-permute-start | bytes 24584 | tf_op jit(solution)/shard_map/ppermute | solution.py:457

commit v6 on v5

--- a/solution.py
+++ b/solution.py
@@ -133,7 +133,7 @@
                 out_ref[s, p, i] = packed(code)
                 return carry
 
-            lax.fori_loop(0, ROWS // step, body, 0, unroll=16)
+            lax.fori_loop(0, ROWS // step, body, 0, unroll=32)
             beside_ref[2 * p + s, 0] = code_ref[p, pl.ds(pad - 1, blocks, stride=BLOCK), :]
             beside_ref[2 * p + s, 1] = code_ref[p, pl.ds(pad + BLOCK, blocks, stride=BLOCK), :]
 
@@ -357,14 +357,19 @@
         ends = pltpu.roll(sides, LANES - 41 - 3 * r, 1)
         return jnp.where((lane == 0) | (lane >= LANES - 2), ends, y)
 
-    for r in range(BLOCK):
-        place(r, mended(gathered([main + r, main + BLOCK + r]), r))
-    place(BLOCK, mended(gathered([tail, tail + 4]), -1))
-    place(BLOCK + 1, mended(gathered([tail + 1, tail + 5]), BLOCK))
-    place(BLOCK + 2, sides)
-
     blocks = BLOCK + 3
-    for start in range(0, blocks, 2):
+
+    def placed(block):
+        if block < BLOCK:
+            y = mended(gathered([main + block, main + BLOCK + block]), block)
+        elif block < BLOCK + 2:
+            h = block - BLOCK
+            y = mended(gathered([tail + h, tail + 4 + h]), BLOCK * h - 1 + h)
+        else:
+            y = sides
+        place(block, y)
+
+    def project(start):
         at = slice(start * LANES, min(start + 2, blocks) * LANES)
         proj = jnp.dot(rows_ref[...], y_ref[:, at], preferred_element_type=F32)
         q1, q2, q3 = (proj[k * GROUP : (k + 1) * GROUP] for k in range(3))
@@ -379,7 +384,7 @@
     unscale = ((subjects - 4) / 0.15) ** 0.5
 
     def pseudo_t(g, r):
-        at = pl.ds(pl.multiple_of(g * 8, 8), 8)
+        at = slice(g * 8, g * 8 + 8) if isinstance(g, int) else pl.ds(pl.multiple_of(g * 8, 8), 8)
 
         def block(b):
             return rss_ref[at, b * LANES : (b + 1) * LANES]
@@ -394,14 +399,28 @@
         variance = CENTRE * mine + beside
         return top_ref[at, r * LANES : (r + 1) * LANES] * lax.rsqrt(variance)
 
-    def body(g, carry):
-        best = jnp.zeros((8, LANES), F32)
-        for r in range(BLOCK):
-            best = jnp.maximum(best, jnp.abs(pseudo_t(g, r)))
-        best_ref[pl.ds(pl.multiple_of(g * 8, 8), 8), :] = best
-        return carry
-
-    lax.fori_loop(0, PERMS // 8, body, 0, unroll=32)
+    def peaks_of(first_row, last_row):
+        for g in range(PERMS // 8):
+            at = slice(g * 8, g * 8 + 8)
+            best = best_ref[at, :] if first_row > 0 else jnp.zeros((8, LANES), F32)
+            for r in range(first_row, last_row):
+                best = jnp.maximum(best, jnp.abs(pseudo_t(g, r)))
+            best_ref[at, :] = best
+
+    for block in (BLOCK, BLOCK + 1, BLOCK + 2):
+        placed(block)
+    project(BLOCK)
+    project(BLOCK + 2)
+    done = 0
+    for start in range(0, BLOCK, 2):
+        for block in range(start, start + 2):
+            placed(block)
+        project(start)
+        ready = start + 1 if start < BLOCK - 2 else BLOCK
+        if start % 4 == 2:
+            peaks_of(done, ready)
+            done = ready
+
     half = BLOCK // 2
     for r in range(BLOCK):
         tmap_ref[(r // half + odd) % 2, r % half : r % half + 1, :] = (
@@ -458,8 +477,8 @@
     t_map = jnp.where(lax.broadcasted_iota(jnp.int32, t_map.shape, 2) >= LANES - 2, beyond, t_map)
 
     theirs = lax.all_to_all(mine, ("subj", "strip"), split_axis=0, concat_axis=0, tiled=True)
-    root = theirs.astype(F32) * (REACH_T**0.25 / LEVELS)
-    return t_map, jnp.max((root * root) * (root * root), axis=0).reshape(PERMS)
+    root = jnp.max(theirs.astype(F32), axis=0).reshape(PERMS) * (REACH_T**0.25 / LEVELS)
+    return t_map, (root * root) * (root * root)
 
 
 def solution(mesh):

time: 70.5 us -> 70.1 us (level)
  Pallas kernels: 15.9 us -> 14.9 us
  transfers between devices with their start and end apart: 5 -> 5, of which waited for: 4 -> 4; matrix products, arithmetic and copies ran while one was open for 1% -> 1% of each run, Pallas kernels for 10% -> 9%
where the time goes in v6:
time: 70.1 us; the launch traced here: 69.9 us
  waiting for transfers between devices  26.6 us (38%)
  starting transfers between devices  26.1 us (37%)
  Pallas kernels  14.9 us (21%)
  other arithmetic  1.47 us (2%)
  between operations  0.75 us (1%)
    all_to_all x1, waiting for transfers between devices, on_device(): lax.all_to_all(sent.reshape(senders, CHUNK, LANES), 'subj', split_axis=0,...  16.1 us
    all_to_all x1, starting transfers between devices, on_device(): lax.all_to_all(sent.reshape(senders, CHUNK, LANES), 'subj', split_axis=0,...  13.7 us
    all_to_all x1, waiting for transfers between devices, on_device(): lax.all_to_all(mine, ('subj', 'strip'), split_axis=0, concat_axis=0, tile...  8.64 us
    all_to_all x1, starting transfers between devices, on_device(): lax.all_to_all(mine, ('subj', 'strip'), split_axis=0, concat_axis=0, tile...  7.38 us
    pallas_call x1, Pallas kernels, block_stats(): pl.pallas_call(functools.partial(stats_kernel, senders), out_shape=(jax.S...  4.54 us
    pallas_call x1, Pallas kernels, design_rows(): pl.pallas_call(designs_kernel, out_shape=jax.ShapeDtypeStruct((3 * GROUP,...  3.96 us
    pallas_call x1, Pallas kernels, strip_edges(): pl.pallas_call(functools.partial(edges_kernel, parts), in_specs=[pl.Block...  2.9 us
    ppermute x1, starting transfers between devices, on_device(): lax.ppermute(t_map, 'strip', [((i + 1) % strips, i) for i in range(strips)])  2.68 us
  transfers between devices with their start and end apart: 5, of which 4 were waited for; matrix products, arithmetic and copies ran while one was open for 1% of the time, Pallas kernels for 9%

profile of v6, /device:TPU:1, one launch (start us, length us, event | category | flops | bytes accessed | tf_op | source)
XLA Modules:
  0.0 69.9 jit_solution(18396546544897802138)
XLA Ops:
  0.6 2.9 %strip_edges.1 = (bf16[48,512]{1,0:T(8,128)(2,1)S(1)}, bf16[96,512]{1,0:T(8,128)(2,1)S(1)}, bf16[2,3,4,512,128]{4,3,2,1,0:T(8,128)(2,1)S(1)}) custom-call(bf16[2,3,4,512,128]{4,3,2,1,0:T(8,128)(2,1)} %disp_ref.1), custom_call_target="tpu_custom_call" | custom-call | flops 100000000 | bytes 3200000 | tf_op jit(solution)/shard_map/strip_edges/pallas_call | solution.py:91
  3.5 0.0 copy-start
  3.5 0.0 copy-start.1
  3.6 0.0 copy-start.2
  3.6 2.1 %collective-permute-start = (bf16[96,512]{1,0:T(8,128)(2,1)S(1)}, bf16[96,512]{1,0:T(8,128)(2,1)S(1)}, u32[]{:S(2)}, u32[]{:S(2)}) collective-permute-start(bf16[96,512]{1,0:T(8,128)(2,1)S(1)} %get-tuple-element.10.high_ref), channel_id=1, source_target_pairs={{0,1},{1,2},{2,3},{3,0},{4,5},{5,6},{6,7},{7,4},{8,9},{9,10},{10,1... | collective-permute-start | bytes 294920 | tf_op jit(solution)/shard_map/ppermute | solution.py:463
  5.7 2.2 %inner_codes.1 = (s16[2,2,32,16,128]{4,3,2,1,0:T(8,128)(2,1)S(1)}, f32[4,2,32,128]{3,2,1,0:T(8,128)S(1)}) custom-call(bf16[2,3,4,512,128]{4,3,2,1,0:T(8,128)(2,1)S(1)} %get-tuple-element.11.disp_ref), custom_call_target="tpu_custom_call" | custom-call | flops 20000000 | bytes 4200000 | tf_op jit(solution)/shard_map/inner_codes/pallas_call | solution.py:143
  7.9 1.0 %collective-permute-done.left_ref = bf16[96,512]{1,0:T(8,128)(2,1)S(1)} collective-permute-done((bf16[96,512]{1,0:T(8,128)(2,1)S(1)}, bf16[96,512]{1,0:T(8,128)(2,1)S(1)}, u32[]{:S(2)}, u32[]{:S(2)}) %collective-permute-start) | collective-permute-done | bytes 98336 | tf_op jit(solution)/shard_map/ppermute | solution.py:463
  9.0 1.3 %with_tails.1 = s16[32,80,128]{2,1,0:T(8,128)(2,1)} custom-call(bf16[48,512]{1,0:T(8,128)(2,1)S(1)} %get-tuple-element.9.low_ref, bf16[96,512]{1,0:T(8,128)(2,1)S(1)} %get-tuple-element.10.high_ref, bf16[96,512]{1,0:T(8,128)(2,1)S(1)} %collective-permute-done.left_ref, f32[4,2,32,128]{3,2,1,0:T(8,128)S(1)} %get-tuple-element.12.beside_ref, ...), custom_call_target="tpu_custom_call" | custom-call | flops 1000000 | bytes 500000 | tf_op jit(solution)/shard_map/with_tails/pallas_call | solution.py:244
  10.3 13.7 %all-to-all-start = ((s16[64,40,128]{2,1,0:T(8,128)(2,1)}), s16[64,40,128]{2,1,0:T(8,128)(2,1)S(1)}, u32[]{:S(2)}, u32[]{:S(2)}) async-start(s16[64,40,128]{2,1,0:T(8,128)(2,1)} %bitcast.22), calls=%async_computation | async-start | bytes 1310720 | tf_op jit(solution)/shard_map/all_to_all | solution.py:467
  24.0 0.0 copy-done
  24.0 0.0 copy-done.1
  24.0 0.0 copy-done.2
  24.0 4.0 %design_rows.1.rows_ref = bf16[816,384]{1,0:T(8,128)(2,1)S(1)} custom-call(f32[1,128]{1,0:T(1,128)S(1)} %bitcast.20, s32[1,128]{1,0:T(1,128)S(1)} %bitcast.21, s32[256,128]{1,0:T(8,128)S(1)} %copy-done), custom_call_target="tpu_custom_call" | custom-call | flops 4000000 | bytes 800000 | tf_op jit(solution)/shard_map/design_rows/pallas_call | solution.py:310
  28.0 16.1 %all-to-all-done = s16[64,40,128]{2,1,0:T(8,128)(2,1)S(1)} async-done(((s16[64,40,128]{2,1,0:T(8,128)(2,1)}), s16[64,40,128]{2,1,0:T(8,128)(2,1)S(1)}, u32[]{:S(2)}, u32[]{:S(2)}) %all-to-all-start) | async-done | bytes 655392 | tf_op jit(solution)/shard_map/all_to_all | solution.py:467
  44.1 4.5 %block_stats.1 = (f32[2,8,128]{2,1,0:T(8,128)S(1)}, s16[256,2,128]{2,1,0:T(2,128)(2,1)}) custom-call(s16[2560,128]{1,0:T(8,128)(2,1)S(1)} %bitcast.19, bf16[816,384]{1,0:T(8,128)(2,1)S(1)} %design_rows.1.rows_ref), custom_call_target="tpu_custom_call" | custom-call | flops 2000000000 | bytes 1000000 | tf_op jit(solution)/shard_map/block_stats/pallas_call | solution.py:439
  48.6 0.3 collective-permute-start.1
  48.9 7.4 %all-to-all-start.1 = ((s16[256,2,128]{2,1,0:T(2,128)(2,1)}), s16[256,2,128]{2,1,0:T(2,128)(2,1)S(1)}, u32[]{:S(2)}, u32[]{:S(2)}) async-start(s16[256,2,128]{2,1,0:T(2,128)(2,1)} %get-tuple-element.15), calls=%async_computation.1 | async-start | bytes 262144 | tf_op jit(solution)/shard_map/all_to_all | solution.py:479
  56.3 0.0 collective-permute-done.1
  56.4 2.7 %collective-permute-start.2 = (f32[2,8,128]{2,1,0:T(8,128)S(1)}, f32[2,8,128]{2,1,0:T(8,128)S(1)}, u32[]{:S(2)}, u32[]{:S(2)}) collective-permute-start(f32[2,8,128]{2,1,0:T(8,128)S(1)} %pad_maximum_fusion), channel_id=1, source_target_pairs={{1,0},{2,1},{3,2},{0,3},{5,4},{6,5},{7,6},{4,7},{9,8},{10,9},{11,1... | collective-permute-start | bytes 24584 | tf_op jit(solution)/shard_map/ppermute | solution.py:476
  59.0 0.8 %collective-permute-done.2 = f32[2,8,128]{2,1,0:T(8,128)S(1)} collective-permute-done((f32[2,8,128]{2,1,0:T(8,128)S(1)}, f32[2,8,128]{2,1,0:T(8,128)S(1)}, u32[]{:S(2)}, u32[]{:S(2)}) %collective-permute-start.2) | collective-permute-done | bytes 8224 | tf_op jit(solution)/shard_map/ppermute | solution.py:476
  59.8 0.6 broadcast_select_fusion
  60.4 8.6 %all-to-all-done.1 = s16[256,2,128]{2,1,0:T(2,128)(2,1)S(1)} async-done(((s16[256,2,128]{2,1,0:T(2,128)(2,1)}), s16[256,2,128]{2,1,0:T(2,128)(2,1)S(1)}, u32[]{:S(2)}, u32[]{:S(2)}) %all-to-all-start.1) | async-done | bytes 131104 | tf_op jit(solution)/shard_map/all_to_all | solution.py:479
  69.1 0.3 convert_reduce_fusion
  69.3 0.6 multiply_bitcast_fusion
  (4 shorter events, 0.0 us)
Async XLA Ops:
  3.5 20.4 %copy-start = (s32[256,128]{1,0:T(8,128)S(1)}, s32[256,128]{1,0:T(8,128)}, u32[]{:S(2)}) copy-start(s32[256,128]{1,0:T(8,128)} %perms_ref.1) | copy-start | bytes 393220
  3.5 20.4 %copy-start.1 = (f32[128]{0:T(128)S(1)}, f32[128]{0:T(128)}, u32[]{:S(2)}) copy-start(f32[128]{0:T(128)} %param.5) | copy-start | bytes 1540
  3.6 20.4 %copy-start.2 = (s32[128]{0:T(128)S(1)}, s32[128]{0:T(128)}, u32[]{:S(2)}) copy-start(s32[128]{0:T(128)} %param.6) | copy-start | bytes 1540
  3.6 5.4 %collective-permute-start = (bf16[96,512]{1,0:T(8,128)(2,1)S(1)}, bf16[96,512]{1,0:T(8,128)(2,1)S(1)}, u32[]{:S(2)}, u32[]{:S(2)}) collective-permute-start(bf16[96,512]{1,0:T(8,128)(2,1)S(1)} %get-tuple-element.10.high_ref), channel_id=1, source_target_pairs={{0,1},{1,2},{2,3},{3,0},{4,5},{5,6},{6,7},{7,4},{8,9},{9,10},{10,1... | collective-permute-start | bytes 294920 | tf_op jit(solution)/shard_map/ppermute | solution.py:463
  10.3 33.8 %all-to-all-start = ((s16[64,40,128]{2,1,0:T(8,128)(2,1)}), s16[64,40,128]{2,1,0:T(8,128)(2,1)S(1)}, u32[]{:S(2)}, u32[]{:S(2)}) async-start(s16[64,40,128]{2,1,0:T(8,128)(2,1)} %bitcast.22), calls=%async_computation | async-start | bytes 1310720 | tf_op jit(solution)/shard_map/all_to_all | solution.py:467
  48.6 7.7 %collective-permute-start.1 = (f32[8,128]{1,0:T(8,128)S(1)}, f32[8,128]{1,0:T(8,128)S(1)}, u32[]{:S(2)}, u32[]{:S(2)}) collective-permute-start(f32[8,128]{1,0:T(8,128)S(1)} %slice_bitcast_fusion), channel_id=1, source_target_pairs={{0,4},{4,0},{8,12},{12,8},{16,20},{20,16},{24,28},{28,24},{32,36},... | collective-permute-start | bytes 12296 | tf_op jit(solution)/shard_map/ppermute | solution.py:474
  48.9 20.1 %all-to-all-start.1 = ((s16[256,2,128]{2,1,0:T(2,128)(2,1)}), s16[256,2,128]{2,1,0:T(2,128)(2,1)S(1)}, u32[]{:S(2)}, u32[]{:S(2)}) async-start(s16[256,2,128]{2,1,0:T(2,128)(2,1)} %get-tuple-element.15), calls=%async_computation.1 | async-start | bytes 262144 | tf_op jit(solution)/shard_map/all_to_all | solution.py:479
  56.4 3.5 %collective-permute-start.2 = (f32[2,8,128]{2,1,0:T(8,128)S(1)}, f32[2,8,128]{2,1,0:T(8,128)S(1)}, u32[]{:S(2)}, u32[]{:S(2)}) collective-permute-start(f32[2,8,128]{2,1,0:T(8,128)S(1)} %pad_maximum_fusion), channel_id=1, source_target_pairs={{1,0},{2,1},{3,2},{0,3},{5,4},{6,5},{7,6},{4,7},{9,8},{10,9},{11,1... | collective-permute-start | bytes 24584 | tf_op jit(solution)/shard_map/ppermute | solution.py:476

commit v7 on v6

--- a/solution.py
+++ b/solution.py
@@ -11,10 +11,8 @@
 LANES = 128
 ROWS = 512
 BLOCK = 16
-MAIN, TAIL = 32, 8
-CHUNK = MAIN + TAIL
-PAIR = 2 * CHUNK
 PER = 2
+CHUNK = BLOCK + 3
 COMPS, PLANES = 3, 4
 PERMS, GROUP = 256, 272
 REACH = 0.6
@@ -36,8 +34,12 @@
     return (part * jnp.abs(part)) * (part * part)
 
 
-def packed(code):
-    return code.astype(jnp.int32).astype(I16)
+def words(first, second):
+    return (first.astype(jnp.int32) << 16) | (second.astype(jnp.int32) & 0xFFFF)
+
+
+def codes_of(word):
+    return (word >> 16).astype(F32), ((word << 16) >> 16).astype(F32)
 
 
 def log_det(dz, dx, dy):
@@ -100,20 +102,21 @@
     )(pltpu.with_memory_space_constraint(disp, pltpu.HBM))
 
 
-def inner_kernel(disp_ref, out_ref, beside_ref, pad_ref, code_ref):
+def inner_kernel(disp_ref, out_ref, pad_ref, code_ref):
     pad, step = 8, 16
     blocks = ROWS // BLOCK
     zeros = jnp.zeros((pad, LANES), F32)
-    for k in range(2):
-        code_ref[k, 0:pad, :] = zeros
-        code_ref[k, pad + ROWS : 2 * pad + ROWS, :] = zeros
+    for s in range(PER):
+        code_ref[s, 0:pad, :] = zeros
+        code_ref[s, pad + ROWS : 2 * pad + ROWS, :] = zeros
+    for p in range(2):
         for c in range(COMPS):
-            pad_ref[k, c, 0:pad, :] = zeros
-            pad_ref[k, c, pad + ROWS : 2 * pad + ROWS, :] = zeros
-    for s in range(PER):
-        for p in range(2):
+            pad_ref[p, c, 0:pad, :] = zeros
+            pad_ref[p, c, pad + ROWS : 2 * pad + ROWS, :] = zeros
+    for p in range(2):
+        for s in range(PER):
             for c in range(COMPS):
-                pad_ref[p, c, pad : pad + ROWS, :] = disp_ref[s, c, 1 + p].astype(F32)
+                pad_ref[s, c, pad : pad + ROWS, :] = disp_ref[s, c, 1 + p].astype(F32)
 
             def body(i, carry):
                 base = pl.multiple_of(i * step, step)
@@ -122,32 +125,33 @@
                     up = disp_ref[s, c, p + 2, pl.ds(base, step), :].astype(F32)
                     down = disp_ref[s, c, p, pl.ds(base, step), :].astype(F32)
                     dz.append(up - down)
-                    center = pad_ref[p, c, pl.ds(base + pad, step), :]
+                    center = pad_ref[s, c, pl.ds(base + pad, step), :]
                     dx.append(
-                        pad_ref[p, c, pl.ds(base + pad + 1, step), :]
-                        - pad_ref[p, c, pl.ds(base + pad - 1, step), :]
+                        pad_ref[s, c, pl.ds(base + pad + 1, step), :]
+                        - pad_ref[s, c, pl.ds(base + pad - 1, step), :]
                     )
                     dy.append(pltpu.roll(center, LANES - 1, 1) - pltpu.roll(center, 1, 1))
                 code = encode(log_det(dz, dx, dy))
-                code_ref[p, pl.ds(base + pad, step), :] = code
-                out_ref[s, p, i] = packed(code)
+                code_ref[s, pl.ds(base + pad, step), :] = code
+                if s == PER - 1:
+                    out_ref[pl.ds((2 * i + p) * CHUNK, step), :] = words(
+                        code_ref[0, pl.ds(base + pad, step), :], code
+                    )
                 return carry
 
             lax.fori_loop(0, ROWS // step, body, 0, unroll=32)
-            beside_ref[2 * p + s, 0] = code_ref[p, pl.ds(pad - 1, blocks, stride=BLOCK), :]
-            beside_ref[2 * p + s, 1] = code_ref[p, pl.ds(pad + BLOCK, blocks, stride=BLOCK), :]
-
-
-def inner_codes(disp):
-    blocks = ROWS // BLOCK
+        for h, start in enumerate((pad - 1, pad + BLOCK)):
+            out_ref[pl.ds(p * CHUNK + BLOCK + h, blocks, stride=2 * CHUNK), :] = words(
+                *(code_ref[s, pl.ds(start, blocks, stride=BLOCK), :] for s in range(PER))
+            )
+
+
+def inner_codes(disp, chunks):
     return pl.pallas_call(
         inner_kernel,
         in_specs=[pl.BlockSpec(memory_space=pltpu.VMEM)],
-        out_specs=[pl.BlockSpec(memory_space=pltpu.VMEM)] * 2,
-        out_shape=(
-            pltpu.VMEM((PER, 2, blocks, BLOCK, LANES), I16),
-            pltpu.VMEM((2 * PER, 2, blocks, LANES), F32),
-        ),
+        out_specs=pl.BlockSpec(memory_space=pltpu.VMEM),
+        out_shape=pltpu.VMEM((chunks * CHUNK + 2 * CHUNK + 2, LANES), jnp.int32),
         scratch_shapes=[
             pltpu.VMEM((2, COMPS, ROWS + 16, LANES), F32),
             pltpu.VMEM((2, ROWS + 32, LANES), F32),
@@ -158,18 +162,8 @@
     )(pltpu.with_memory_space_constraint(disp, pltpu.VMEM))
 
 
-def tail_kernel(low_ref, high_ref, left_ref, beside_ref, main_ref, out_ref, pad_ref, side_ref, tail_ref, send_ref, sem):
-    copies = [
-        pltpu.make_async_copy(
-            main_ref.at[s, p],
-            out_ref.at[:, 48 * p + BLOCK * s : 48 * p + BLOCK * s + BLOCK, :],
-            sem.at[2 * s + p],
-        )
-        for s in range(PER)
-        for p in range(2)
-    ]
-    for copy in copies:
-        copy.start()
+def tail_kernel(low_ref, high_ref, left_ref, main_ref, out_ref, pad_ref, side_ref, send_ref, sem):
+    send_ref[...] = main_ref[...]
     inside = (lax.axis_index("strip") > 0).astype(F32)
     lane = lax.broadcasted_iota(jnp.int32, (8, ROWS), 1)
 
@@ -221,42 +215,32 @@
             line = first if k == 0 else jnp.where(here < 24 * k, line, first)
         side_ref[j * 8 : j * 8 + 8, :] = line
     for p in range(2):
-        for s in range(PER):
-            row = TAIL * p + 4 * s
-            for h in range(2):
-                tail_ref[pl.ds(row + h, blocks, stride=2 * TAIL), :] = beside_ref[2 * p + s, h]
-            tail_ref[pl.ds(row + 2, blocks, stride=2 * TAIL), :] = side_ref[
-                pl.ds(2 + 2 * p + s, blocks, stride=8), :
-            ]
-            tail_ref[pl.ds(row + 3, blocks, stride=2 * TAIL), :] = jnp.zeros((blocks, LANES), F32)
-    send_ref[...] = packed(tail_ref[0 : blocks * 2 * TAIL, :]).reshape(blocks, 2 * TAIL, LANES)
-    copies.append(
-        pltpu.make_async_copy(send_ref, out_ref.at[:, MAIN : MAIN + 2 * TAIL, :], sem.at[2 * PER])
-    )
-    copies[-1].start()
-    for copy in copies:
-        copy.wait()
-
-
-def with_tails(low, high, left, beside, main):
+        send_ref[pl.ds(p * CHUNK + BLOCK + 2, blocks, stride=2 * CHUNK), :] = words(
+            *(side_ref[pl.ds(2 + 2 * p + s, blocks, stride=8), :] for s in range(PER))
+        )
+    copy = pltpu.make_async_copy(send_ref.at[0 : out_ref.shape[0], :], out_ref, sem)
+    copy.start()
+    copy.wait()
+
+
+def with_tails(low, high, left, main, chunks):
     blocks = ROWS // BLOCK
     vmem = pl.BlockSpec(memory_space=pltpu.VMEM)
     return pl.pallas_call(
         tail_kernel,
-        in_specs=[vmem] * 5,
+        in_specs=[vmem] * 4,
         out_specs=pl.BlockSpec(memory_space=pltpu.HBM),
-        out_shape=pltpu.HBM((blocks, PAIR, LANES), I16),
+        out_shape=pltpu.HBM((chunks * CHUNK, LANES), jnp.int32),
         scratch_shapes=[
             pltpu.VMEM((5, 8, ROWS + 2 * LANES), F32),
             pltpu.VMEM((blocks * 8 + 8, LANES), F32),
-            pltpu.VMEM((blocks * 2 * TAIL + 16, LANES), F32),
-            pltpu.VMEM((blocks, 2 * TAIL, LANES), I16),
-            pltpu.SemaphoreType.DMA((2 * PER + 1,)),
+            pltpu.VMEM(main.shape, jnp.int32),
+            pltpu.SemaphoreType.DMA,
         ],
         compiler_params=pltpu.CompilerParams(vmem_limit_bytes=8 * 2**20),
         cost_estimate=pl.CostEstimate(flops=10**6, bytes_accessed=5 * 10**5, transcendentals=5 * 10**4),
         name="with_tails",
-    )(*(pltpu.with_memory_space_constraint(x, pltpu.VMEM) for x in (low, high, left, beside, main)))
+    )(*(pltpu.with_memory_space_constraint(x, pltpu.VMEM) for x in (low, high, left, main)))
 
 
 def designs_kernel(age_ref, code_ref, perms_ref, out_ref):
@@ -320,20 +304,19 @@
     subjects = PER * senders
     lane = lax.broadcasted_iota(jnp.int32, (subjects, LANES), 1)
     odd = lax.axis_index("subj") % 2
-    main = odd * TAIL
-    tail = (1 - odd) * MAIN
-    per = 4 * CHUNK
+    per = 4 * CHUNK * 2
 
     def unpack(i, carry):
-        at = pl.ds(pl.multiple_of(i * per, 32), per)
-        value_ref[at, :] = decode(code_ref[at, :].astype(F32))
+        at = pl.ds(pl.multiple_of(i * per, 8), per)
+        for s, code in enumerate(codes_of(code_ref[at, :])):
+            value_ref[s, at, :] = decode(code)
         return carry
 
     lax.fori_loop(0, senders * CHUNK // per, unpack, 0, unroll=4)
 
-    def gathered(offsets):
+    def gathered(row):
         return jnp.concatenate(
-            [value_ref[pl.ds(offset, senders, stride=CHUNK), :] for offset in offsets], axis=0
+            [value_ref[s, pl.ds(row, senders, stride=CHUNK), :] for s in range(PER)], axis=0
         )
 
     def place(block, y):
@@ -348,7 +331,7 @@
     far = lane // 2 + jnp.where(lane % 2 == 0, 97, 1)
     near = (lane - 36) // 3 + 24 * ((lane - 36) % 3 + 1)
     sides = jnp.take_along_axis(
-        gathered([tail + 2, tail + 6]),
+        gathered(BLOCK + 2),
         jnp.where(lane < 32, far, jnp.where((lane >= 36) & (lane < 90), near, 0)),
         axis=1,
     )
@@ -360,11 +343,8 @@
     blocks = BLOCK + 3
 
     def placed(block):
-        if block < BLOCK:
-            y = mended(gathered([main + block, main + BLOCK + block]), block)
-        elif block < BLOCK + 2:
-            h = block - BLOCK
-            y = mended(gathered([tail + h, tail + 4 + h]), BLOCK * h - 1 + h)
+        if block < BLOCK + 2:
+            y = mended(gathered(block), -1 if block == BLOCK else min(block, BLOCK))
         else:
             y = sides
         place(block, y)
@@ -430,7 +410,7 @@
     code = jnp.minimum(jnp.sqrt(jnp.sqrt(code)), 1.0) * LEVELS + 0.5
     lines = jnp.concatenate([code[:, k * LANES : (k + 1) * LANES] for k in range(PERMS // LANES)] * 4, axis=0)
     everyone = peaks_ref.shape[0]
-    peaks_ref[...] = jnp.broadcast_to(packed(lines)[None], (everyone // 4, 8, LANES)).reshape(everyone, 2, LANES)
+    peaks_ref[...] = jnp.broadcast_to(lines.astype(jnp.int32).astype(I16)[None], (everyone // 4, 8, LANES)).reshape(everyone, 2, LANES)
 
 
 def block_stats(codes, rows, senders, everyone):
@@ -443,7 +423,7 @@
             jax.ShapeDtypeStruct((everyone, PERMS // LANES, LANES), I16),
         ),
         scratch_shapes=[
-            pltpu.VMEM((senders * CHUNK + CHUNK, LANES), F32),
+            pltpu.VMEM((PER, senders * CHUNK + CHUNK + 5, LANES), F32),
             pltpu.VMEM((3 * subjects, columns), BF16),
             pltpu.VMEM((8, columns), F32),
             pltpu.VMEM((GROUP, columns), F32),
@@ -461,11 +441,11 @@
     strips = lax.axis_size("strip")
     low, high, field = strip_edges(displacement)
     left = lax.ppermute(high, "strip", [(i, (i + 1) % strips) for i in range(strips)])
-    main, beside = inner_codes(field)
+    main = inner_codes(field, senders)
     rows = design_rows(age, group_codes, perms)
-    sent = with_tails(low, high, left, beside, main)
+    sent = with_tails(low, high, left, main, senders)
     codes = lax.all_to_all(
-        sent.reshape(senders, CHUNK, LANES), "subj", split_axis=0, concat_axis=0, tiled=True
+        sent.reshape(senders, CHUNK, 1, LANES), "subj", split_axis=0, concat_axis=0, tiled=True
     )
     everyone = senders * strips
     tested, mine = block_stats(codes.reshape(senders * CHUNK, LANES), rows, senders, everyone)

time: 70.1 us -> 69.4 us (0.990)
    all_to_all x1, waiting for transfers between devices: 16.1 us -> 15.4 us  [on_device(): lax.all_to_all(sent.reshape(senders, CHUNK, 1, LANES), 'subj', split_axis...]
where the time goes in v7:
time: 69.4 us; the launch traced here: 69.2 us
  starting transfers between devices  26.1 us (38%)
  waiting for transfers between devices  26.1 us (38%)
  Pallas kernels  14.8 us (21%)
  other arithmetic  1.47 us (2%)
  between operations  0.72 us (1%)
    all_to_all x1, waiting for transfers between devices, on_device(): lax.all_to_all(sent.reshape(senders, CHUNK, 1, LANES), 'subj', split_axis...  15.4 us
    all_to_all x1, starting transfers between devices, on_device(): lax.all_to_all(sent.reshape(senders, CHUNK, 1, LANES), 'subj', split_axis...  13.7 us
    all_to_all x1, waiting for transfers between devices, on_device(): lax.all_to_all(mine, ('subj', 'strip'), split_axis=0, concat_axis=0, tile...  8.64 us
    all_to_all x1, starting transfers between devices, on_device(): lax.all_to_all(mine, ('subj', 'strip'), split_axis=0, concat_axis=0, tile...  7.36 us
    pallas_call x1, Pallas kernels, block_stats(): pl.pallas_call(functools.partial(stats_kernel, senders), out_shape=(jax.S...  4.49 us
    pallas_call x1, Pallas kernels, design_rows(): pl.pallas_call(designs_kernel, out_shape=jax.ShapeDtypeStruct((3 * GROUP,...  3.96 us
    pallas_call x1, Pallas kernels, strip_edges(): pl.pallas_call(functools.partial(edges_kernel, parts), in_specs=[pl.Block...  2.9 us
    ppermute x1, starting transfers between devices, on_device(): lax.ppermute(t_map, 'strip', [((i + 1) % strips, i) for i in range(strips)])  2.68 us
  transfers between devices with their start and end apart: 5, of which 4 were waited for; matrix products, arithmetic and copies ran while one was open for 1% of the time, Pallas kernels for 9%

profile of v7, /device:TPU:1, one launch (start us, length us, event | category | flops | bytes accessed | tf_op | source)
XLA Modules:
  0.0 69.2 jit_solution(8101624684583475148)
XLA Ops:
  0.6 2.9 %strip_edges.1 = (bf16[48,512]{1,0:T(8,128)(2,1)S(1)}, bf16[96,512]{1,0:T(8,128)(2,1)S(1)}, bf16[2,3,4,512,128]{4,3,2,1,0:T(8,128)(2,1)S(1)}) custom-call(bf16[2,3,4,512,128]{4,3,2,1,0:T(8,128)(2,1)} %disp_ref.1), custom_call_target="tpu_custom_call" | custom-call | flops 100000000 | bytes 3200000 | tf_op jit(solution)/shard_map/strip_edges/pallas_call | solution.py:93
  3.5 2.1 %collective-permute-start = (bf16[96,512]{1,0:T(8,128)(2,1)S(1)}, bf16[96,512]{1,0:T(8,128)(2,1)S(1)}, u32[]{:S(2)}, u32[]{:S(2)}) collective-permute-start(bf16[96,512]{1,0:T(8,128)(2,1)S(1)} %get-tuple-element.8.high_ref), channel_id=1, source_target_pairs={{0,1},{1,2},{2,3},{3,0},{4,5},{5,6},{6,7},{7,4},{8,9},{9,10},{10,1... | collective-permute-start | bytes 294920 | tf_op jit(solution)/shard_map/ppermute | solution.py:443
  5.6 0.0 copy-start
  5.6 0.0 copy-start.1
  5.7 0.0 copy-start.2
  5.7 2.1 %inner_codes.1.main_ref = s32[1256,128]{1,0:T(8,128)S(1)} custom-call(bf16[2,3,4,512,128]{4,3,2,1,0:T(8,128)(2,1)S(1)} %get-tuple-element.9.disp_ref), custom_call_target="tpu_custom_call" | custom-call | flops 20000000 | bytes 4200000 | tf_op jit(solution)/shard_map/inner_codes/pallas_call | solution.py:150
  7.7 1.2 %collective-permute-done.left_ref = bf16[96,512]{1,0:T(8,128)(2,1)S(1)} collective-permute-done((bf16[96,512]{1,0:T(8,128)(2,1)S(1)}, bf16[96,512]{1,0:T(8,128)(2,1)S(1)}, u32[]{:S(2)}, u32[]{:S(2)}) %collective-permute-start) | collective-permute-done | bytes 98336 | tf_op jit(solution)/shard_map/ppermute | solution.py:443
  8.9 1.4 %with_tails.1 = s32[1216,128]{1,0:T(8,128)} custom-call(bf16[48,512]{1,0:T(8,128)(2,1)S(1)} %get-tuple-element.7.low_ref, bf16[96,512]{1,0:T(8,128)(2,1)S(1)} %get-tuple-element.8.high_ref, bf16[96,512]{1,0:T(8,128)(2,1)S(1)} %collective-permute-done.left_ref, s32[1256,128]{1,0:T(8,128)S(1)} %inner_codes.1.main_ref), custom_call_target="tpu_custom_call" | custom-call | flops 1000000 | bytes 500000 | tf_op jit(solution)/shard_map/with_tails/pallas_call | solution.py:229
  10.3 13.7 %all-to-all-start = ((s32[64,19,1,128]{3,2,1,0:T(1,128)}), s32[64,19,1,128]{3,2,1,0:T(1,128)S(1)}, u32[]{:S(2)}, u32[]{:S(2)}) async-start(s32[64,19,1,128]{3,2,1,0:T(1,128)} %bitcast.22), calls=%async_computation | async-start | bytes 1245184 | tf_op jit(solution)/shard_map/all_to_all | solution.py:447
  24.0 0.0 copy-done
  24.0 0.0 copy-done.1
  24.0 0.0 copy-done.2
  24.0 4.0 %design_rows.1.rows_ref = bf16[816,384]{1,0:T(8,128)(2,1)S(1)} custom-call(f32[1,128]{1,0:T(1,128)S(1)} %bitcast.20, s32[1,128]{1,0:T(1,128)S(1)} %bitcast.21, s32[256,128]{1,0:T(8,128)S(1)} %copy-done), custom_call_target="tpu_custom_call" | custom-call | flops 4000000 | bytes 800000 | tf_op jit(solution)/shard_map/design_rows/pallas_call | solution.py:294
  28.0 15.4 %all-to-all-done = s32[64,19,1,128]{3,2,1,0:T(1,128)S(1)} async-done(((s32[64,19,1,128]{3,2,1,0:T(1,128)}), s32[64,19,1,128]{3,2,1,0:T(1,128)S(1)}, u32[]{:S(2)}, u32[]{:S(2)}) %all-to-all-start) | async-done | bytes 622624 | tf_op jit(solution)/shard_map/all_to_all | solution.py:447
  43.4 4.5 %block_stats.1 = (f32[2,8,128]{2,1,0:T(8,128)S(1)}, s16[256,2,128]{2,1,0:T(2,128)(2,1)}) custom-call(s32[1216,128]{1,0:T(8,128)S(1)} %bitcast.19, bf16[816,384]{1,0:T(8,128)(2,1)S(1)} %design_rows.1.rows_ref), custom_call_target="tpu_custom_call" | custom-call | flops 2000000000 | bytes 1000000 | tf_op jit(solution)/shard_map/block_stats/pallas_call | solution.py:419
  47.9 0.3 collective-permute-start.1
  48.2 7.4 %all-to-all-start.1 = ((s16[256,2,128]{2,1,0:T(2,128)(2,1)}), s16[256,2,128]{2,1,0:T(2,128)(2,1)S(1)}, u32[]{:S(2)}, u32[]{:S(2)}) async-start(s16[256,2,128]{2,1,0:T(2,128)(2,1)} %get-tuple-element.11), calls=%async_computation.1 | async-start | bytes 262144 | tf_op jit(solution)/shard_map/all_to_all | solution.py:459
  55.6 0.0 collective-permute-done.1
  55.6 2.7 %collective-permute-start.2 = (f32[2,8,128]{2,1,0:T(8,128)S(1)}, f32[2,8,128]{2,1,0:T(8,128)S(1)}, u32[]{:S(2)}, u32[]{:S(2)}) collective-permute-start(f32[2,8,128]{2,1,0:T(8,128)S(1)} %pad_maximum_fusion), channel_id=1, source_target_pairs={{1,0},{2,1},{3,2},{0,3},{5,4},{6,5},{7,6},{4,7},{9,8},{10,9},{11,1... | collective-permute-start | bytes 24584 | tf_op jit(solution)/shard_map/ppermute | solution.py:456
  58.3 0.8 %collective-permute-done.2 = f32[2,8,128]{2,1,0:T(8,128)S(1)} collective-permute-done((f32[2,8,128]{2,1,0:T(8,128)S(1)}, f32[2,8,128]{2,1,0:T(8,128)S(1)}, u32[]{:S(2)}, u32[]{:S(2)}) %collective-permute-start.2) | collective-permute-done | bytes 8224 | tf_op jit(solution)/shard_map/ppermute | solution.py:456
  59.1 0.6 broadcast_select_fusion
  59.7 8.6 %all-to-all-done.1 = s16[256,2,128]{2,1,0:T(2,128)(2,1)S(1)} async-done(((s16[256,2,128]{2,1,0:T(2,128)(2,1)}), s16[256,2,128]{2,1,0:T(2,128)(2,1)S(1)}, u32[]{:S(2)}, u32[]{:S(2)}) %all-to-all-start.1) | async-done | bytes 131104 | tf_op jit(solution)/shard_map/all_to_all | solution.py:459
  68.3 0.3 convert_reduce_fusion
  68.6 0.6 multiply_bitcast_fusion
  (4 shorter events, 0.0 us)
Async XLA Ops:
  3.5 5.4 %collective-permute-start = (bf16[96,512]{1,0:T(8,128)(2,1)S(1)}, bf16[96,512]{1,0:T(8,128)(2,1)S(1)}, u32[]{:S(2)}, u32[]{:S(2)}) collective-permute-start(bf16[96,512]{1,0:T(8,128)(2,1)S(1)} %get-tuple-element.8.high_ref), channel_id=1, source_target_pairs={{0,1},{1,2},{2,3},{3,0},{4,5},{5,6},{6,7},{7,4},{8,9},{9,10},{10,1... | collective-permute-start | bytes 294920 | tf_op jit(solution)/shard_map/ppermute | solution.py:443
  5.6 18.3 %copy-start = (s32[256,128]{1,0:T(8,128)S(1)}, s32[256,128]{1,0:T(8,128)}, u32[]{:S(2)}) copy-start(s32[256,128]{1,0:T(8,128)} %perms_ref.1) | copy-start | bytes 393220
  5.6 18.3 %copy-start.1 = (f32[128]{0:T(128)S(1)}, f32[128]{0:T(128)}, u32[]{:S(2)}) copy-start(f32[128]{0:T(128)} %param.5) | copy-start | bytes 1540
  5.7 18.3 %copy-start.2 = (s32[128]{0:T(128)S(1)}, s32[128]{0:T(128)}, u32[]{:S(2)}) copy-start(s32[128]{0:T(128)} %param.6) | copy-start | bytes 1540
  10.3 33.1 %all-to-all-start = ((s32[64,19,1,128]{3,2,1,0:T(1,128)}), s32[64,19,1,128]{3,2,1,0:T(1,128)S(1)}, u32[]{:S(2)}, u32[]{:S(2)}) async-start(s32[64,19,1,128]{3,2,1,0:T(1,128)} %bitcast.22), calls=%async_computation | async-start | bytes 1245184 | tf_op jit(solution)/shard_map/all_to_all | solution.py:447
  47.9 7.7 %collective-permute-start.1 = (f32[8,128]{1,0:T(8,128)S(1)}, f32[8,128]{1,0:T(8,128)S(1)}, u32[]{:S(2)}, u32[]{:S(2)}) collective-permute-start(f32[8,128]{1,0:T(8,128)S(1)} %slice_bitcast_fusion), channel_id=1, source_target_pairs={{0,4},{4,0},{8,12},{12,8},{16,20},{20,16},{24,28},{28,24},{32,36},... | collective-permute-start | bytes 12296 | tf_op jit(solution)/shard_map/ppermute | solution.py:454
  48.2 20.1 %all-to-all-start.1 = ((s16[256,2,128]{2,1,0:T(2,128)(2,1)}), s16[256,2,128]{2,1,0:T(2,128)(2,1)S(1)}, u32[]{:S(2)}, u32[]{:S(2)}) async-start(s16[256,2,128]{2,1,0:T(2,128)(2,1)} %get-tuple-element.11), calls=%async_computation.1 | async-start | bytes 262144 | tf_op jit(solution)/shard_map/all_to_all | solution.py:459
  55.6 3.5 %collective-permute-start.2 = (f32[2,8,128]{2,1,0:T(8,128)S(1)}, f32[2,8,128]{2,1,0:T(8,128)S(1)}, u32[]{:S(2)}, u32[]{:S(2)}) collective-permute-start(f32[2,8,128]{2,1,0:T(8,128)S(1)} %pad_maximum_fusion), channel_id=1, source_target_pairs={{1,0},{2,1},{3,2},{0,3},{5,4},{6,5},{7,6},{4,7},{9,8},{10,9},{11,1... | collective-permute-start | bytes 24584 | tf_op jit(solution)/shard_map/ppermute | solution.py:456

commit v8 on v7

--- a/solution.py
+++ b/solution.py
@@ -54,7 +54,38 @@
     return jnp.log(det * 0.125)
 
 
-def edges_kernel(parts, disp_ref, low_ref, high_ref, field_ref, sem):
+SENT = 7
+
+
+def edge_codes(around):
+    lane = lax.broadcasted_iota(jnp.int32, (8, ROWS), 1)
+    dz, dx, dy = [], [], []
+    for before, center, after in around:
+        dz.append(pltpu.roll(center, 6, 0) - pltpu.roll(center, 2, 0))
+        dx.append(
+            jnp.where(lane == ROWS - 1, 0.0, pltpu.roll(center, ROWS - 1, 1))
+            - jnp.where(lane == 0, 0.0, pltpu.roll(center, 1, 1))
+        )
+        dy.append(after - before)
+    return encode(log_det(dz, dx, dy))
+
+
+def two_in_tile(first, second):
+    row = lax.broadcasted_iota(jnp.int32, first.shape, 0)
+    return jnp.where((row >= 2) & (row < 6), first, pltpu.roll(second, 4, 0))
+
+
+def split_code(code):
+    shift = 1.5 * 2.0**31
+    high = (code + shift) - shift
+    return two_in_tile(high, code - high)
+
+
+def joined_code(tile):
+    return tile + pltpu.roll(tile, 4, 0)
+
+
+def edges_kernel(parts, disp_ref, low_ref, sent_ref, field_ref, high_ref, sem):
     rows = ROWS // parts
     copies = [
         pltpu.make_async_copy(
@@ -84,18 +115,26 @@
                     picks[q], both, (((1,), (1,)), ((), ())), preferred_element_type=F32
                 )
             low_ref[c * 16 : c * 16 + 16, at] = acc[0:16].astype(BF16)
-            high_ref[c * 32 : c * 32 + 32, at] = acc[16:48].astype(BF16)
+            high_ref[c * 32 : c * 32 + 32, at] = acc[16:48]
+    high = [[high_ref[32 * c + 8 * e : 32 * c + 8 * e + 8, :] for e in range(4)] for c in range(COMPS)]
+    tiles = [w[3] for w in high] + [
+        two_in_tile(high[0][2], high[1][2]),
+        high[2][2],
+        split_code(edge_codes([w[0:3] for w in high])),
+        split_code(edge_codes([w[1:4] for w in high])),
+    ]
+    sent_ref[...] = jnp.concatenate(tiles, axis=0).astype(BF16)
 
 
 def strip_edges(disp):
     parts = 4
-    out = [pltpu.VMEM((COMPS * rows, ROWS), BF16) for rows in (16, 32)]
+    out = [pltpu.VMEM((rows, ROWS), BF16) for rows in (COMPS * 16, SENT * 8)]
     return pl.pallas_call(
         functools.partial(edges_kernel, parts),
         in_specs=[pl.BlockSpec(memory_space=pltpu.HBM)],
         out_specs=[pl.BlockSpec(memory_space=pltpu.VMEM)] * 3,
         out_shape=(*out, pltpu.VMEM(disp.shape, BF16)),
-        scratch_shapes=[pltpu.SemaphoreType.DMA((parts,))],
+        scratch_shapes=[pltpu.VMEM((COMPS * 32, ROWS), F32), pltpu.SemaphoreType.DMA((parts,))],
         compiler_params=pltpu.CompilerParams(vmem_limit_bytes=8 * 2**20),
         cost_estimate=pl.CostEstimate(flops=10**8, bytes_accessed=3_200_000, transcendentals=0),
         name="strip_edges",
@@ -162,35 +201,23 @@
     )(pltpu.with_memory_space_constraint(disp, pltpu.VMEM))
 
 
-def tail_kernel(low_ref, high_ref, left_ref, main_ref, out_ref, pad_ref, side_ref, send_ref, sem):
+def tail_kernel(low_ref, sent_ref, left_ref, main_ref, out_ref, pad_ref, side_ref, send_ref, sem):
     send_ref[...] = main_ref[...]
     inside = (lax.axis_index("strip") > 0).astype(F32)
-    lane = lax.broadcasted_iota(jnp.int32, (8, ROWS), 1)
-
-    def columns(ref):
-        many = ref.shape[0] // (8 * COMPS)
-        return [
-            [ref[8 * (many * c + e) : 8 * (many * c + e) + 8, :] for e in range(many)] for c in range(COMPS)
-        ]
-
-    def codes(around):
-        dz, dx, dy = [], [], []
-        for before, center, after in around:
-            dz.append(pltpu.roll(center, 6, 0) - pltpu.roll(center, 2, 0))
-            dx.append(
-                jnp.where(lane == ROWS - 1, 0.0, pltpu.roll(center, ROWS - 1, 1))
-                - jnp.where(lane == 0, 0.0, pltpu.roll(center, 1, 1))
-            )
-            dy.append(after - before)
-        return encode(log_det(dz, dx, dy))
-
-    low, high, left = (columns(ref[...].astype(F32)) for ref in (low_ref, high_ref, left_ref))
+
+    def tiles(ref):
+        field = ref[...].astype(F32)
+        return [field[8 * k : 8 * k + 8] for k in range(ref.shape[0] // 8)]
+
+    low, own, left = tiles(low_ref), tiles(sent_ref), tiles(left_ref)
+    last = left[0:3]
+    before = [left[3], pltpu.roll(left[3], 4, 0), left[4]]
     five = [
-        codes([w[0:3] for w in left]),
-        codes([w[1:4] for w in left]),
-        codes([(w[2], w[3], v[0] * inside) for w, v in zip(left, low)]),
-        codes([(w[3] * inside, v[0], v[1]) for w, v in zip(left, low)]),
-        codes([w[1:4] for w in high]),
+        joined_code(left[5]),
+        joined_code(left[6]),
+        edge_codes([(before[c], last[c], low[2 * c] * inside) for c in range(COMPS)]),
+        edge_codes([(last[c] * inside, low[2 * c], low[2 * c + 1]) for c in range(COMPS)]),
+        joined_code(own[6]),
     ]
     zeros = jnp.zeros((8, LANES), F32)
     for k in range(5):
@@ -223,7 +250,7 @@
     copy.wait()
 
 
-def with_tails(low, high, left, main, chunks):
+def with_tails(low, sent, left, main, chunks):
     blocks = ROWS // BLOCK
     vmem = pl.BlockSpec(memory_space=pltpu.VMEM)
     return pl.pallas_call(
@@ -240,7 +267,7 @@
         compiler_params=pltpu.CompilerParams(vmem_limit_bytes=8 * 2**20),
         cost_estimate=pl.CostEstimate(flops=10**6, bytes_accessed=5 * 10**5, transcendentals=5 * 10**4),
         name="with_tails",
-    )(*(pltpu.with_memory_space_constraint(x, pltpu.VMEM) for x in (low, high, left, main)))
+    )(*(pltpu.with_memory_space_constraint(x, pltpu.VMEM) for x in (low, sent, left, main)))
 
 
 def designs_kernel(age_ref, code_ref, perms_ref, out_ref):
@@ -439,11 +466,11 @@
 def on_device(displacement, age, group_codes, perms):
     senders = lax.axis_size("subj")
     strips = lax.axis_size("strip")
-    low, high, field = strip_edges(displacement)
-    left = lax.ppermute(high, "strip", [(i, (i + 1) % strips) for i in range(strips)])
+    low, after, field = strip_edges(displacement)
+    left = lax.ppermute(after, "strip", [(i, (i + 1) % strips) for i in range(strips)])
     main = inner_codes(field, senders)
     rows = design_rows(age, group_codes, perms)
-    sent = with_tails(low, high, left, main, senders)
+    sent = with_tails(low, after, left, main, senders)
     codes = lax.all_to_all(
         sent.reshape(senders, CHUNK, 1, LANES), "subj", split_axis=0, concat_axis=0, tiled=True
     )

time: 69.4 us -> 69 us (level)
  no operation moved by 1% of the time
where the time goes in v8:
time: 69 us; the launch traced here: 68.7 us
  starting transfers between devices  26.1 us (38%)
  waiting for transfers between devices  25.6 us (37%)
  Pallas kernels  14.7 us (21%)
  other arithmetic  1.47 us (2%)
  between operations  0.72 us (1%)
    all_to_all x1, waiting for transfers between devices, on_device(): lax.all_to_all(sent.reshape(senders, CHUNK, 1, LANES), 'subj', split_axis...  15.4 us
    all_to_all x1, starting transfers between devices, on_device(): lax.all_to_all(sent.reshape(senders, CHUNK, 1, LANES), 'subj', split_axis...  13.7 us
    all_to_all x1, waiting for transfers between devices, on_device(): lax.all_to_all(mine, ('subj', 'strip'), split_axis=0, concat_axis=0, tile...  8.64 us
    all_to_all x1, starting transfers between devices, on_device(): lax.all_to_all(mine, ('subj', 'strip'), split_axis=0, concat_axis=0, tile...  7.36 us
    pallas_call x1, Pallas kernels, block_stats(): pl.pallas_call(functools.partial(stats_kernel, senders), out_shape=(jax.S...  4.49 us
    pallas_call x1, Pallas kernels, design_rows(): pl.pallas_call(designs_kernel, out_shape=jax.ShapeDtypeStruct((3 * GROUP,...  3.96 us
    pallas_call x1, Pallas kernels, strip_edges(): pl.pallas_call(functools.partial(edges_kernel, parts), in_specs=[pl.Block...  3.01 us
    ppermute x1, starting transfers between devices, on_device(): lax.ppermute(t_map, 'strip', [((i + 1) % strips, i) for i in range(strips)])  2.68 us
  transfers between devices with their start and end apart: 5, of which 4 were waited for; matrix products, arithmetic and copies ran while one was open for 1% of the time, Pallas kernels for 9%

profile of v8, /device:TPU:1, one launch (start us, length us, event | category | flops | bytes accessed | tf_op | source)
XLA Modules:
  0.0 68.7 jit_solution(517585013846201981)
XLA Ops:
  0.6 3.0 %strip_edges.1 = (bf16[48,512]{1,0:T(8,128)(2,1)S(1)}, bf16[56,512]{1,0:T(8,128)(2,1)S(1)}, bf16[2,3,4,512,128]{4,3,2,1,0:T(8,128)(2,1)S(1)}) custom-call(bf16[2,3,4,512,128]{4,3,2,1,0:T(8,128)(2,1)} %disp_ref.1), custom_call_target="tpu_custom_call" | custom-call | flops 100000000 | bytes 3200000 | tf_op jit(solution)/shard_map/strip_edges/pallas_call | solution.py:132
  3.6 2.1 %collective-permute-start = (bf16[56,512]{1,0:T(8,128)(2,1)S(1)}, bf16[56,512]{1,0:T(8,128)(2,1)S(1)}, u32[]{:S(2)}, u32[]{:S(2)}) collective-permute-start(bf16[56,512]{1,0:T(8,128)(2,1)S(1)} %get-tuple-element.8.sent_ref), channel_id=1, source_target_pairs={{0,1},{1,2},{2,3},{3,0},{4,5},{5,6},{6,7},{7,4},{8,9},{9,10},{10,1... | collective-permute-start | bytes 172040 | tf_op jit(solution)/shard_map/ppermute | solution.py:470
  5.8 0.0 copy-start
  5.8 0.0 copy-start.1
  5.8 0.0 copy-start.2
  5.8 2.1 %inner_codes.1.main_ref = s32[1256,128]{1,0:T(8,128)S(1)} custom-call(bf16[2,3,4,512,128]{4,3,2,1,0:T(8,128)(2,1)S(1)} %get-tuple-element.9.disp_ref), custom_call_target="tpu_custom_call" | custom-call | flops 20000000 | bytes 4200000 | tf_op jit(solution)/shard_map/inner_codes/pallas_call | solution.py:189
  7.8 0.8 %collective-permute-done.left_ref = bf16[56,512]{1,0:T(8,128)(2,1)S(1)} collective-permute-done((bf16[56,512]{1,0:T(8,128)(2,1)S(1)}, bf16[56,512]{1,0:T(8,128)(2,1)S(1)}, u32[]{:S(2)}, u32[]{:S(2)}) %collective-permute-start) | collective-permute-done | bytes 57376 | tf_op jit(solution)/shard_map/ppermute | solution.py:470
  8.6 1.2 %with_tails.1 = s32[1216,128]{1,0:T(8,128)} custom-call(bf16[48,512]{1,0:T(8,128)(2,1)S(1)} %get-tuple-element.7.low_ref, bf16[56,512]{1,0:T(8,128)(2,1)S(1)} %get-tuple-element.8.sent_ref, bf16[56,512]{1,0:T(8,128)(2,1)S(1)} %collective-permute-done.left_ref, s32[1256,128]{1,0:T(8,128)S(1)} %inner_codes.1.main_ref), custom_call_target="tpu_custom_call" | custom-call | flops 1000000 | bytes 500000 | tf_op jit(solution)/shard_map/with_tails/pallas_call | solution.py:256
  9.8 13.7 %all-to-all-start = ((s32[64,19,1,128]{3,2,1,0:T(1,128)}), s32[64,19,1,128]{3,2,1,0:T(1,128)S(1)}, u32[]{:S(2)}, u32[]{:S(2)}) async-start(s32[64,19,1,128]{3,2,1,0:T(1,128)} %bitcast.22), calls=%async_computation | async-start | bytes 1245184 | tf_op jit(solution)/shard_map/all_to_all | solution.py:474
  23.5 0.0 copy-done
  23.5 0.0 copy-done.1
  23.5 0.0 copy-done.2
  23.5 4.0 %design_rows.1.rows_ref = bf16[816,384]{1,0:T(8,128)(2,1)S(1)} custom-call(f32[1,128]{1,0:T(1,128)S(1)} %bitcast.20, s32[1,128]{1,0:T(1,128)S(1)} %bitcast.21, s32[256,128]{1,0:T(8,128)S(1)} %copy-done), custom_call_target="tpu_custom_call" | custom-call | flops 4000000 | bytes 800000 | tf_op jit(solution)/shard_map/design_rows/pallas_call | solution.py:321
  27.5 15.4 %all-to-all-done = s32[64,19,1,128]{3,2,1,0:T(1,128)S(1)} async-done(((s32[64,19,1,128]{3,2,1,0:T(1,128)}), s32[64,19,1,128]{3,2,1,0:T(1,128)S(1)}, u32[]{:S(2)}, u32[]{:S(2)}) %all-to-all-start) | async-done | bytes 622624 | tf_op jit(solution)/shard_map/all_to_all | solution.py:474
  42.9 4.5 %block_stats.1 = (f32[2,8,128]{2,1,0:T(8,128)S(1)}, s16[256,2,128]{2,1,0:T(2,128)(2,1)}) custom-call(s32[1216,128]{1,0:T(8,128)S(1)} %bitcast.19, bf16[816,384]{1,0:T(8,128)(2,1)S(1)} %design_rows.1.rows_ref), custom_call_target="tpu_custom_call" | custom-call | flops 2000000000 | bytes 1000000 | tf_op jit(solution)/shard_map/block_stats/pallas_call | solution.py:446
  47.4 0.3 collective-permute-start.1
  47.8 7.4 %all-to-all-start.1 = ((s16[256,2,128]{2,1,0:T(2,128)(2,1)}), s16[256,2,128]{2,1,0:T(2,128)(2,1)S(1)}, u32[]{:S(2)}, u32[]{:S(2)}) async-start(s16[256,2,128]{2,1,0:T(2,128)(2,1)} %get-tuple-element.11), calls=%async_computation.1 | async-start | bytes 262144 | tf_op jit(solution)/shard_map/all_to_all | solution.py:486
  55.1 0.0 collective-permute-done.1
  55.2 2.7 %collective-permute-start.2 = (f32[2,8,128]{2,1,0:T(8,128)S(1)}, f32[2,8,128]{2,1,0:T(8,128)S(1)}, u32[]{:S(2)}, u32[]{:S(2)}) collective-permute-start(f32[2,8,128]{2,1,0:T(8,128)S(1)} %pad_maximum_fusion), channel_id=1, source_target_pairs={{1,0},{2,1},{3,2},{0,3},{5,4},{6,5},{7,6},{4,7},{9,8},{10,9},{11,1... | collective-permute-start | bytes 24584 | tf_op jit(solution)/shard_map/ppermute | solution.py:483
  57.8 0.8 %collective-permute-done.2 = f32[2,8,128]{2,1,0:T(8,128)S(1)} collective-permute-done((f32[2,8,128]{2,1,0:T(8,128)S(1)}, f32[2,8,128]{2,1,0:T(8,128)S(1)}, u32[]{:S(2)}, u32[]{:S(2)}) %collective-permute-start.2) | collective-permute-done | bytes 8224 | tf_op jit(solution)/shard_map/ppermute | solution.py:483
  58.6 0.6 broadcast_select_fusion
  59.2 8.6 %all-to-all-done.1 = s16[256,2,128]{2,1,0:T(2,128)(2,1)S(1)} async-done(((s16[256,2,128]{2,1,0:T(2,128)(2,1)}), s16[256,2,128]{2,1,0:T(2,128)(2,1)S(1)}, u32[]{:S(2)}, u32[]{:S(2)}) %all-to-all-start.1) | async-done | bytes 131104 | tf_op jit(solution)/shard_map/all_to_all | solution.py:486
  67.9 0.3 convert_reduce_fusion
  68.2 0.6 multiply_bitcast_fusion
  (4 shorter events, 0.0 us)
Async XLA Ops:
  3.6 5.0 %collective-permute-start = (bf16[56,512]{1,0:T(8,128)(2,1)S(1)}, bf16[56,512]{1,0:T(8,128)(2,1)S(1)}, u32[]{:S(2)}, u32[]{:S(2)}) collective-permute-start(bf16[56,512]{1,0:T(8,128)(2,1)S(1)} %get-tuple-element.8.sent_ref), channel_id=1, source_target_pairs={{0,1},{1,2},{2,3},{3,0},{4,5},{5,6},{6,7},{7,4},{8,9},{9,10},{10,1... | collective-permute-start | bytes 172040 | tf_op jit(solution)/shard_map/ppermute | solution.py:470
  5.8 17.8 %copy-start = (s32[256,128]{1,0:T(8,128)S(1)}, s32[256,128]{1,0:T(8,128)}, u32[]{:S(2)}) copy-start(s32[256,128]{1,0:T(8,128)} %perms_ref.1) | copy-start | bytes 393220
  5.8 17.8 %copy-start.1 = (f32[128]{0:T(128)S(1)}, f32[128]{0:T(128)}, u32[]{:S(2)}) copy-start(f32[128]{0:T(128)} %param.5) | copy-start | bytes 1540
  5.8 17.8 %copy-start.2 = (s32[128]{0:T(128)S(1)}, s32[128]{0:T(128)}, u32[]{:S(2)}) copy-start(s32[128]{0:T(128)} %param.6) | copy-start | bytes 1540
  9.8 33.1 %all-to-all-start = ((s32[64,19,1,128]{3,2,1,0:T(1,128)}), s32[64,19,1,128]{3,2,1,0:T(1,128)S(1)}, u32[]{:S(2)}, u32[]{:S(2)}) async-start(s32[64,19,1,128]{3,2,1,0:T(1,128)} %bitcast.22), calls=%async_computation | async-start | bytes 1245184 | tf_op jit(solution)/shard_map/all_to_all | solution.py:474
  47.4 7.7 %collective-permute-start.1 = (f32[8,128]{1,0:T(8,128)S(1)}, f32[8,128]{1,0:T(8,128)S(1)}, u32[]{:S(2)}, u32[]{:S(2)}) collective-permute-start(f32[8,128]{1,0:T(8,128)S(1)} %slice_bitcast_fusion), channel_id=1, source_target_pairs={{0,4},{4,0},{8,12},{12,8},{16,20},{20,16},{24,28},{28,24},{32,36},... | collective-permute-start | bytes 12296 | tf_op jit(solution)/shard_map/ppermute | solution.py:481
  47.8 20.1 %all-to-all-start.1 = ((s16[256,2,128]{2,1,0:T(2,128)(2,1)}), s16[256,2,128]{2,1,0:T(2,128)(2,1)S(1)}, u32[]{:S(2)}, u32[]{:S(2)}) async-start(s16[256,2,128]{2,1,0:T(2,128)(2,1)} %get-tuple-element.11), calls=%async_computation.1 | async-start | bytes 262144 | tf_op jit(solution)/shard_map/all_to_all | solution.py:486
  55.2 3.5 %collective-permute-start.2 = (f32[2,8,128]{2,1,0:T(8,128)S(1)}, f32[2,8,128]{2,1,0:T(8,128)S(1)}, u32[]{:S(2)}, u32[]{:S(2)}) collective-permute-start(f32[2,8,128]{2,1,0:T(8,128)S(1)} %pad_maximum_fusion), channel_id=1, source_target_pairs={{1,0},{2,1},{3,2},{0,3},{5,4},{6,5},{7,6},{4,7},{9,8},{10,9},{11,1... | collective-permute-start | bytes 24584 | tf_op jit(solution)/shard_map/ppermute | solution.py:483

commit v9 on v8

--- a/solution.py
+++ b/solution.py
@@ -85,18 +85,14 @@
     return tile + pltpu.roll(tile, 4, 0)
 
 
-def edges_kernel(parts, disp_ref, low_ref, sent_ref, field_ref, high_ref, sem):
-    rows = ROWS // parts
+def edges_kernel(disp_ref, low_ref, sent_ref, field_ref, high_ref, sem):
     copies = [
-        pltpu.make_async_copy(
-            disp_ref.at[:, :, :, h * rows : (h + 1) * rows, :],
-            field_ref.at[:, :, :, h * rows : (h + 1) * rows, :],
-            sem.at[h],
-        )
-        for h in range(parts)
+        [pltpu.make_async_copy(disp_ref.at[s, c], field_ref.at[s, c], sem.at[c, s]) for s in range(PER)]
+        for c in range(COMPS)
     ]
-    for copy in copies:
-        copy.start()
+    for pair in copies:
+        for copy in pair:
+            copy.start()
     row = lax.broadcasted_iota(jnp.int32, (48, 2 * LANES), 0)
     lane = lax.broadcasted_iota(jnp.int32, (48, 2 * LANES), 1)
     column = jnp.where(row < 16, row // 8, row // 8 - 2 + LANES - 4)
@@ -104,18 +100,17 @@
         ((row % 8 == 2 * q + lane // LANES) & (lane % LANES == column)).astype(F32).astype(BF16)
         for q in range(PLANES)
     ]
-    for h in range(parts):
-        copies[h].wait()
-        at = slice(h * rows, (h + 1) * rows)
-        for c in range(COMPS):
-            acc = jnp.zeros((48, rows), F32)
-            for q in range(PLANES):
-                both = jnp.concatenate([field_ref[0, c, q, at, :], field_ref[1, c, q, at, :]], axis=1)
-                acc = acc + lax.dot_general(
-                    picks[q], both, (((1,), (1,)), ((), ())), preferred_element_type=F32
-                )
-            low_ref[c * 16 : c * 16 + 16, at] = acc[0:16].astype(BF16)
-            high_ref[c * 32 : c * 32 + 32, at] = acc[16:48]
+    for c in range(COMPS):
+        for copy in copies[c]:
+            copy.wait()
+        acc = jnp.zeros((48, ROWS), F32)
+        for q in range(PLANES):
+            both = jnp.concatenate([field_ref[0, c, q], field_ref[1, c, q]], axis=1)
+            acc = acc + lax.dot_general(
+                picks[q], both, (((1,), (1,)), ((), ())), preferred_element_type=F32
+            )
+        low_ref[c * 16 : c * 16 + 16, :] = acc[0:16].astype(BF16)
+        high_ref[c * 32 : c * 32 + 32, :] = acc[16:48]
     high = [[high_ref[32 * c + 8 * e : 32 * c + 8 * e + 8, :] for e in range(4)] for c in range(COMPS)]
     tiles = [w[3] for w in high] + [
         two_in_tile(high[0][2], high[1][2]),
@@ -127,14 +122,13 @@
 
 
 def strip_edges(disp):
-    parts = 4
     out = [pltpu.VMEM((rows, ROWS), BF16) for rows in (COMPS * 16, SENT * 8)]
     return pl.pallas_call(
-        functools.partial(edges_kernel, parts),
+        edges_kernel,
         in_specs=[pl.BlockSpec(memory_space=pltpu.HBM)],
         out_specs=[pl.BlockSpec(memory_space=pltpu.VMEM)] * 3,
         out_shape=(*out, pltpu.VMEM(disp.shape, BF16)),
-        scratch_shapes=[pltpu.VMEM((COMPS * 32, ROWS), F32), pltpu.SemaphoreType.DMA((parts,))],
+        scratch_shapes=[pltpu.VMEM((COMPS * 32, ROWS), F32), pltpu.SemaphoreType.DMA((COMPS, PER))],
         compiler_params=pltpu.CompilerParams(vmem_limit_bytes=8 * 2**20),
         cost_estimate=pl.CostEstimate(flops=10**8, bytes_accessed=3_200_000, transcendentals=0),
         name="strip_edges",
@@ -339,7 +333,7 @@
             value_ref[s, at, :] = decode(code)
         return carry
 
-    lax.fori_loop(0, senders * CHUNK // per, unpack, 0, unroll=4)
+    lax.fori_loop(0, senders * CHUNK // per, unpack, 0, unroll=8)
 
     def gathered(row):
         return jnp.concatenate(
@@ -463,6 +457,22 @@
     )(codes, rows)
 
 
+def largest_kernel(code_ref, out_ref):
+    lines = PERMS // LANES
+    code = jnp.max(code_ref[...].astype(F32), axis=0).reshape(16 // lines, lines, LANES)
+    root = jnp.max(code, axis=0) * (REACH_T**0.25 / LEVELS)
+    out_ref[...] = (root * root) * (root * root)
+
+
+def largest(codes):
+    return pl.pallas_call(
+        largest_kernel,
+        out_shape=jax.ShapeDtypeStruct((PERMS // LANES, LANES), F32),
+        compiler_params=pltpu.CompilerParams(vmem_limit_bytes=4 * 2**20),
+        name="largest",
+    )(codes)
+
+
 def on_device(displacement, age, group_codes, perms):
     senders = lax.axis_size("subj")
     strips = lax.axis_size("strip")
@@ -484,8 +494,7 @@
     t_map = jnp.where(lax.broadcasted_iota(jnp.int32, t_map.shape, 2) >= LANES - 2, beyond, t_map)
 
     theirs = lax.all_to_all(mine, ("subj", "strip"), split_axis=0, concat_axis=0, tiled=True)
-    root = jnp.max(theirs.astype(F32), axis=0).reshape(PERMS) * (REACH_T**0.25 / LEVELS)
-    return t_map, (root * root) * (root * root)
+    return t_map, largest(theirs.reshape(-1, 16, LANES)).reshape(PERMS)
 
 
 def solution(mesh):

time: 69 us -> 68.4 us (level)
  other arithmetic: 1.47 us -> 0.62 us
    pallas_call x1 -> x2, Pallas kernels: 3.01 us -> 3.26 us  [the longest x1 2.66 us: strip_edges(): pl.pallas_call(edges_kernel, in_specs=[pl.BlockSpec(memory_space=pltpu.HB...]
where the time goes in v9:
time: 68.4 us; the launch traced here: 68.1 us
  starting transfers between devices  26.1 us (38%)
  waiting for transfers between devices  25.6 us (37%)
  Pallas kernels  15 us (22%)
  between operations  0.72 us (1%)
    all_to_all x1, waiting for transfers between devices, on_device(): lax.all_to_all(sent.reshape(senders, CHUNK, 1, LANES), 'subj', split_axis...  15.4 us
    all_to_all x1, starting transfers between devices, on_device(): lax.all_to_all(sent.reshape(senders, CHUNK, 1, LANES), 'subj', split_axis...  13.7 us
    all_to_all x1, waiting for transfers between devices, on_device(): lax.all_to_all(mine, ('subj', 'strip'), split_axis=0, concat_axis=0, tile...  8.65 us
    all_to_all x1, starting transfers between devices, on_device(): lax.all_to_all(mine, ('subj', 'strip'), split_axis=0, concat_axis=0, tile...  7.35 us
    pallas_call x1, Pallas kernels, block_stats(): pl.pallas_call(functools.partial(stats_kernel, senders), out_shape=(jax.S...  4.46 us
    pallas_call x1, Pallas kernels, design_rows(): pl.pallas_call(designs_kernel, out_shape=jax.ShapeDtypeStruct((3 * GROUP,...  3.96 us
    ppermute x1, starting transfers between devices, on_device(): lax.ppermute(t_map, 'strip', [((i + 1) % strips, i) for i in range(strips)])  2.68 us
    pallas_call x1, Pallas kernels, strip_edges(): pl.pallas_call(edges_kernel, in_specs=[pl.BlockSpec(memory_space=pltpu.HB...  2.66 us
  transfers between devices with their start and end apart: 5, of which 4 were waited for; matrix products, arithmetic and copies ran while one was open for 1% of the time, Pallas kernels for 9%

profile of v9, /device:TPU:1, one launch (start us, length us, event | category | flops | bytes accessed | tf_op | source)
XLA Modules:
  0.0 68.1 jit_solution(16065959683371287268)
XLA Ops:
  0.6 2.7 %strip_edges.1 = (bf16[48,512]{1,0:T(8,128)(2,1)S(1)}, bf16[56,512]{1,0:T(8,128)(2,1)S(1)}, bf16[2,3,4,512,128]{4,3,2,1,0:T(8,128)(2,1)S(1)}) custom-call(bf16[2,3,4,512,128]{4,3,2,1,0:T(8,128)(2,1)} %disp_ref.1), custom_call_target="tpu_custom_call" | custom-call | flops 100000000 | bytes 3200000 | tf_op jit(solution)/shard_map/strip_edges/pallas_call | solution.py:126
  3.3 2.1 %collective-permute-start = (bf16[56,512]{1,0:T(8,128)(2,1)S(1)}, bf16[56,512]{1,0:T(8,128)(2,1)S(1)}, u32[]{:S(2)}, u32[]{:S(2)}) collective-permute-start(bf16[56,512]{1,0:T(8,128)(2,1)S(1)} %get-tuple-element.8.sent_ref), channel_id=1, source_target_pairs={{0,1},{1,2},{2,3},{3,0},{4,5},{5,6},{6,7},{7,4},{8,9},{9,10},{10,1... | collective-permute-start | bytes 172040 | tf_op jit(solution)/shard_map/ppermute | solution.py:480
  5.4 0.0 copy-start
  5.4 0.0 copy-start.1
  5.4 0.0 copy-start.2
  5.4 2.1 %inner_codes.1.main_ref = s32[1256,128]{1,0:T(8,128)S(1)} custom-call(bf16[2,3,4,512,128]{4,3,2,1,0:T(8,128)(2,1)S(1)} %get-tuple-element.9.disp_ref), custom_call_target="tpu_custom_call" | custom-call | flops 20000000 | bytes 4200000 | tf_op jit(solution)/shard_map/inner_codes/pallas_call | solution.py:183
  7.5 0.8 %collective-permute-done.left_ref = bf16[56,512]{1,0:T(8,128)(2,1)S(1)} collective-permute-done((bf16[56,512]{1,0:T(8,128)(2,1)S(1)}, bf16[56,512]{1,0:T(8,128)(2,1)S(1)}, u32[]{:S(2)}, u32[]{:S(2)}) %collective-permute-start) | collective-permute-done | bytes 57376 | tf_op jit(solution)/shard_map/ppermute | solution.py:480
  8.3 1.2 %with_tails.1 = s32[1216,128]{1,0:T(8,128)} custom-call(bf16[48,512]{1,0:T(8,128)(2,1)S(1)} %get-tuple-element.7.low_ref, bf16[56,512]{1,0:T(8,128)(2,1)S(1)} %get-tuple-element.8.sent_ref, bf16[56,512]{1,0:T(8,128)(2,1)S(1)} %collective-permute-done.left_ref, s32[1256,128]{1,0:T(8,128)S(1)} %inner_codes.1.main_ref), custom_call_target="tpu_custom_call" | custom-call | flops 1000000 | bytes 500000 | tf_op jit(solution)/shard_map/with_tails/pallas_call | solution.py:250
  9.5 13.7 %all-to-all-start = ((s32[64,19,1,128]{3,2,1,0:T(1,128)}), s32[64,19,1,128]{3,2,1,0:T(1,128)S(1)}, u32[]{:S(2)}, u32[]{:S(2)}) async-start(s32[64,19,1,128]{3,2,1,0:T(1,128)} %bitcast.23), calls=%async_computation | async-start | bytes 1245184 | tf_op jit(solution)/shard_map/all_to_all | solution.py:484
  23.2 0.0 copy-done
  23.2 0.0 copy-done.1
  23.2 0.0 copy-done.2
  23.2 4.0 %design_rows.1.rows_ref = bf16[816,384]{1,0:T(8,128)(2,1)S(1)} custom-call(f32[1,128]{1,0:T(1,128)S(1)} %bitcast.21, s32[1,128]{1,0:T(1,128)S(1)} %bitcast.22, s32[256,128]{1,0:T(8,128)S(1)} %copy-done), custom_call_target="tpu_custom_call" | custom-call | flops 4000000 | bytes 800000 | tf_op jit(solution)/shard_map/design_rows/pallas_call | solution.py:315
  27.2 15.4 %all-to-all-done = s32[64,19,1,128]{3,2,1,0:T(1,128)S(1)} async-done(((s32[64,19,1,128]{3,2,1,0:T(1,128)}), s32[64,19,1,128]{3,2,1,0:T(1,128)S(1)}, u32[]{:S(2)}, u32[]{:S(2)}) %all-to-all-start) | async-done | bytes 622624 | tf_op jit(solution)/shard_map/all_to_all | solution.py:484
  42.6 4.5 %block_stats.1 = (f32[2,8,128]{2,1,0:T(8,128)S(1)}, s16[256,2,128]{2,1,0:T(2,128)(2,1)}) custom-call(s32[1216,128]{1,0:T(8,128)S(1)} %bitcast.19, bf16[816,384]{1,0:T(8,128)(2,1)S(1)} %design_rows.1.rows_ref), custom_call_target="tpu_custom_call" | custom-call | flops 2000000000 | bytes 1000000 | tf_op jit(solution)/shard_map/block_stats/pallas_call | solution.py:440
  47.1 0.3 collective-permute-start.1
  47.4 7.4 %all-to-all-start.1 = ((s16[256,2,128]{2,1,0:T(2,128)(2,1)}), s16[256,2,128]{2,1,0:T(2,128)(2,1)S(1)}, u32[]{:S(2)}, u32[]{:S(2)}) async-start(s16[256,2,128]{2,1,0:T(2,128)(2,1)} %get-tuple-element.11), calls=%async_computation.1 | async-start | bytes 262144 | tf_op jit(solution)/shard_map/all_to_all | solution.py:496
  54.8 0.0 collective-permute-done.1
  54.8 2.7 %collective-permute-start.2 = (f32[2,8,128]{2,1,0:T(8,128)S(1)}, f32[2,8,128]{2,1,0:T(8,128)S(1)}, u32[]{:S(2)}, u32[]{:S(2)}) collective-permute-start(f32[2,8,128]{2,1,0:T(8,128)S(1)} %pad_maximum_fusion), channel_id=1, source_target_pairs={{1,0},{2,1},{3,2},{0,3},{5,4},{6,5},{7,6},{4,7},{9,8},{10,9},{11,1... | collective-permute-start | bytes 24584 | tf_op jit(solution)/shard_map/ppermute | solution.py:493
  57.5 0.8 %collective-permute-done.2 = f32[2,8,128]{2,1,0:T(8,128)S(1)} collective-permute-done((f32[2,8,128]{2,1,0:T(8,128)S(1)}, f32[2,8,128]{2,1,0:T(8,128)S(1)}, u32[]{:S(2)}, u32[]{:S(2)}) %collective-permute-start.2) | collective-permute-done | bytes 8224 | tf_op jit(solution)/shard_map/ppermute | solution.py:493
  58.3 0.6 broadcast_select_fusion
  58.9 8.7 %all-to-all-done.1 = s16[256,2,128]{2,1,0:T(2,128)(2,1)S(1)} async-done(((s16[256,2,128]{2,1,0:T(2,128)(2,1)}), s16[256,2,128]{2,1,0:T(2,128)(2,1)S(1)}, u32[]{:S(2)}, u32[]{:S(2)}) %all-to-all-start.1) | async-done | bytes 131104 | tf_op jit(solution)/shard_map/all_to_all | solution.py:496
  67.5 0.6 largest.1
  (4 shorter events, 0.0 us)
Async XLA Ops:
  3.3 5.0 %collective-permute-start = (bf16[56,512]{1,0:T(8,128)(2,1)S(1)}, bf16[56,512]{1,0:T(8,128)(2,1)S(1)}, u32[]{:S(2)}, u32[]{:S(2)}) collective-permute-start(bf16[56,512]{1,0:T(8,128)(2,1)S(1)} %get-tuple-element.8.sent_ref), channel_id=1, source_target_pairs={{0,1},{1,2},{2,3},{3,0},{4,5},{5,6},{6,7},{7,4},{8,9},{9,10},{10,1... | collective-permute-start | bytes 172040 | tf_op jit(solution)/shard_map/ppermute | solution.py:480
  5.4 17.8 %copy-start = (s32[256,128]{1,0:T(8,128)S(1)}, s32[256,128]{1,0:T(8,128)}, u32[]{:S(2)}) copy-start(s32[256,128]{1,0:T(8,128)} %perms_ref.1) | copy-start | bytes 393220
  5.4 17.8 %copy-start.1 = (f32[128]{0:T(128)S(1)}, f32[128]{0:T(128)}, u32[]{:S(2)}) copy-start(f32[128]{0:T(128)} %param.5) | copy-start | bytes 1540
  5.4 17.8 %copy-start.2 = (s32[128]{0:T(128)S(1)}, s32[128]{0:T(128)}, u32[]{:S(2)}) copy-start(s32[128]{0:T(128)} %param.6) | copy-start | bytes 1540
  9.5 33.1 %all-to-all-start = ((s32[64,19,1,128]{3,2,1,0:T(1,128)}), s32[64,19,1,128]{3,2,1,0:T(1,128)S(1)}, u32[]{:S(2)}, u32[]{:S(2)}) async-start(s32[64,19,1,128]{3,2,1,0:T(1,128)} %bitcast.23), calls=%async_computation | async-start | bytes 1245184 | tf_op jit(solution)/shard_map/all_to_all | solution.py:484
  47.1 7.7 %collective-permute-start.1 = (f32[8,128]{1,0:T(8,128)S(1)}, f32[8,128]{1,0:T(8,128)S(1)}, u32[]{:S(2)}, u32[]{:S(2)}) collective-permute-start(f32[8,128]{1,0:T(8,128)S(1)} %slice_bitcast_fusion), channel_id=1, source_target_pairs={{0,4},{4,0},{8,12},{12,8},{16,20},{20,16},{24,28},{28,24},{32,36},... | collective-permute-start | bytes 12296 | tf_op jit(solution)/shard_map/ppermute | solution.py:491
  47.4 20.1 %all-to-all-start.1 = ((s16[256,2,128]{2,1,0:T(2,128)(2,1)}), s16[256,2,128]{2,1,0:T(2,128)(2,1)S(1)}, u32[]{:S(2)}, u32[]{:S(2)}) async-start(s16[256,2,128]{2,1,0:T(2,128)(2,1)} %get-tuple-element.11), calls=%async_computation.1 | async-start | bytes 262144 | tf_op jit(solution)/shard_map/all_to_all | solution.py:496
  54.8 3.5 %collective-permute-start.2 = (f32[2,8,128]{2,1,0:T(8,128)S(1)}, f32[2,8,128]{2,1,0:T(8,128)S(1)}, u32[]{:S(2)}, u32[]{:S(2)}) collective-permute-start(f32[2,8,128]{2,1,0:T(8,128)S(1)} %pad_maximum_fusion), channel_id=1, source_target_pairs={{1,0},{2,1},{3,2},{0,3},{5,4},{6,5},{7,6},{4,7},{9,8},{10,9},{11,1... | collective-permute-start | bytes 24584 | tf_op jit(solution)/shard_map/ppermute | solution.py:493

commit v10 on v9

--- a/solution.py
+++ b/solution.py
@@ -87,8 +87,12 @@
 
 def edges_kernel(disp_ref, low_ref, sent_ref, field_ref, high_ref, sem):
     copies = [
-        [pltpu.make_async_copy(disp_ref.at[s, c], field_ref.at[s, c], sem.at[c, s]) for s in range(PER)]
+        [
+            pltpu.make_async_copy(disp_ref.at[s, c, q : q + 2], field_ref.at[s, c, q : q + 2], sem.at[c, q // 2, s])
+            for s in range(PER)
+        ]
         for c in range(COMPS)
+        for q in range(0, PLANES, 2)
     ]
     for pair in copies:
         for copy in pair:
@@ -101,10 +105,11 @@
         for q in range(PLANES)
     ]
     for c in range(COMPS):
-        for copy in copies[c]:
-            copy.wait()
         acc = jnp.zeros((48, ROWS), F32)
         for q in range(PLANES):
+            if q % 2 == 0:
+                for copy in copies[c * (PLANES // 2) + q // 2]:
+                    copy.wait()
             both = jnp.concatenate([field_ref[0, c, q], field_ref[1, c, q]], axis=1)
             acc = acc + lax.dot_general(
                 picks[q], both, (((1,), (1,)), ((), ())), preferred_element_type=F32
@@ -128,7 +133,7 @@
         in_specs=[pl.BlockSpec(memory_space=pltpu.HBM)],
         out_specs=[pl.BlockSpec(memory_space=pltpu.VMEM)] * 3,
         out_shape=(*out, pltpu.VMEM(disp.shape, BF16)),
-        scratch_shapes=[pltpu.VMEM((COMPS * 32, ROWS), F32), pltpu.SemaphoreType.DMA((COMPS, PER))],
+        scratch_shapes=[pltpu.VMEM((COMPS * 32, ROWS), F32), pltpu.SemaphoreType.DMA((COMPS, PLANES // 2, PER))],
         compiler_params=pltpu.CompilerParams(vmem_limit_bytes=8 * 2**20),
         cost_estimate=pl.CostEstimate(flops=10**8, bytes_accessed=3_200_000, transcendentals=0),
         name="strip_edges",
@@ -220,6 +225,7 @@
         pad_ref[k, :, LANES + ROWS : 2 * LANES + ROWS] = zeros
     here = lax.broadcasted_iota(jnp.int32, (8, LANES), 1)
     blocks = ROWS // BLOCK
+    some, copies = blocks // 4, []
     for j in range(blocks):
         start = LANES + j * BLOCK - 1
         line = zeros
@@ -235,13 +241,20 @@
                 first = jnp.where(here - 24 * k < LANES - offset, first, second)
             line = first if k == 0 else jnp.where(here < 24 * k, line, first)
         side_ref[j * 8 : j * 8 + 8, :] = line
-    for p in range(2):
-        send_ref[pl.ds(p * CHUNK + BLOCK + 2, blocks, stride=2 * CHUNK), :] = words(
-            *(side_ref[pl.ds(2 + 2 * p + s, blocks, stride=8), :] for s in range(PER))
-        )
-    copy = pltpu.make_async_copy(send_ref.at[0 : out_ref.shape[0], :], out_ref, sem)
-    copy.start()
-    copy.wait()
+        if (j + 1) % some == 0:
+            begin = j + 1 - some
+            for p in range(2):
+                at = pl.ds((2 * begin + p) * CHUNK + BLOCK + 2, some, stride=2 * CHUNK)
+                send_ref[at, :] = words(
+                    *(side_ref[pl.ds(8 * begin + 2 + 2 * p + s, some, stride=8), :] for s in range(PER))
+                )
+            part = slice(2 * begin * CHUNK, 2 * (j + 1) * CHUNK)
+            copies.append(
+                pltpu.make_async_copy(send_ref.at[part, :], out_ref.at[part, :], sem.at[len(copies)])
+            )
+            copies[-1].start()
+    for copy in copies:
+        copy.wait()
 
 
 def with_tails(low, sent, left, main, chunks):
@@ -256,7 +269,7 @@
             pltpu.VMEM((5, 8, ROWS + 2 * LANES), F32),
             pltpu.VMEM((blocks * 8 + 8, LANES), F32),
             pltpu.VMEM(main.shape, jnp.int32),
-            pltpu.SemaphoreType.DMA,
+            pltpu.SemaphoreType.DMA((4,)),
         ],
         compiler_params=pltpu.CompilerParams(vmem_limit_bytes=8 * 2**20),
         cost_estimate=pl.CostEstimate(flops=10**6, bytes_accessed=5 * 10**5, transcendentals=5 * 10**4),

time: 68.4 us -> 68.2 us (level)
  no operation moved by 1% of the time
where the time goes in v10:
time: 68.2 us; the launch traced here: 67.9 us
  starting transfers between devices  26.1 us (38%)
  waiting for transfers between devices  25.6 us (38%)
  Pallas kernels  14.8 us (22%)
  between operations  0.72 us (1%)
    all_to_all x1, waiting for transfers between devices, on_device(): lax.all_to_all(sent.reshape(senders, CHUNK, 1, LANES), 'subj', split_axis...  15.4 us
    all_to_all x1, starting transfers between devices, on_device(): lax.all_to_all(sent.reshape(senders, CHUNK, 1, LANES), 'subj', split_axis...  13.7 us
    all_to_all x1, waiting for transfers between devices, on_device(): lax.all_to_all(mine, ('subj', 'strip'), split_axis=0, concat_axis=0, tile...  8.65 us
    all_to_all x1, starting transfers between devices, on_device(): lax.all_to_all(mine, ('subj', 'strip'), split_axis=0, concat_axis=0, tile...  7.35 us
    pallas_call x1, Pallas kernels, block_stats(): pl.pallas_call(functools.partial(stats_kernel, senders), out_shape=(jax.S...  4.46 us
    pallas_call x1, Pallas kernels, design_rows(): pl.pallas_call(designs_kernel, out_shape=jax.ShapeDtypeStruct((3 * GROUP,...  3.96 us
    ppermute x1, starting transfers between devices, on_device(): lax.ppermute(t_map, 'strip', [((i + 1) % strips, i) for i in range(strips)])  2.68 us
    pallas_call x1, Pallas kernels, strip_edges(): pl.pallas_call(edges_kernel, in_specs=[pl.BlockSpec(memory_space=pltpu.HB...  2.58 us
  transfers between devices with their start and end apart: 5, of which 4 were waited for; matrix products, arithmetic and copies ran while one was open for 1% of the time, Pallas kernels for 9%

profile of v10, /device:TPU:1, one launch (start us, length us, event | category | flops | bytes accessed | tf_op | source)
XLA Modules:
  0.0 67.9 jit_solution(1745301574002394231)
XLA Ops:
  0.6 2.6 %strip_edges.1 = (bf16[48,512]{1,0:T(8,128)(2,1)S(1)}, bf16[56,512]{1,0:T(8,128)(2,1)S(1)}, bf16[2,3,4,512,128]{4,3,2,1,0:T(8,128)(2,1)S(1)}) custom-call(bf16[2,3,4,512,128]{4,3,2,1,0:T(8,128)(2,1)} %disp_ref.1), custom_call_target="tpu_custom_call" | custom-call | flops 100000000 | bytes 3200000 | tf_op jit(solution)/shard_map/strip_edges/pallas_call | solution.py:131
  3.2 2.1 %collective-permute-start = (bf16[56,512]{1,0:T(8,128)(2,1)S(1)}, bf16[56,512]{1,0:T(8,128)(2,1)S(1)}, u32[]{:S(2)}, u32[]{:S(2)}) collective-permute-start(bf16[56,512]{1,0:T(8,128)(2,1)S(1)} %get-tuple-element.8.sent_ref), channel_id=1, source_target_pairs={{0,1},{1,2},{2,3},{3,0},{4,5},{5,6},{6,7},{7,4},{8,9},{9,10},{10,1... | collective-permute-start | bytes 172040 | tf_op jit(solution)/shard_map/ppermute | solution.py:493
  5.3 0.0 copy-start
  5.3 0.0 copy-start.1
  5.3 0.0 copy-start.2
  5.3 2.1 %inner_codes.1.main_ref = s32[1256,128]{1,0:T(8,128)S(1)} custom-call(bf16[2,3,4,512,128]{4,3,2,1,0:T(8,128)(2,1)S(1)} %get-tuple-element.9.disp_ref), custom_call_target="tpu_custom_call" | custom-call | flops 20000000 | bytes 4200000 | tf_op jit(solution)/shard_map/inner_codes/pallas_call | solution.py:188
  7.4 0.8 %collective-permute-done.left_ref = bf16[56,512]{1,0:T(8,128)(2,1)S(1)} collective-permute-done((bf16[56,512]{1,0:T(8,128)(2,1)S(1)}, bf16[56,512]{1,0:T(8,128)(2,1)S(1)}, u32[]{:S(2)}, u32[]{:S(2)}) %collective-permute-start) | collective-permute-done | bytes 57376 | tf_op jit(solution)/shard_map/ppermute | solution.py:493
  8.2 1.1 %with_tails.1 = s32[1216,128]{1,0:T(8,128)} custom-call(bf16[48,512]{1,0:T(8,128)(2,1)S(1)} %get-tuple-element.7.low_ref, bf16[56,512]{1,0:T(8,128)(2,1)S(1)} %get-tuple-element.8.sent_ref, bf16[56,512]{1,0:T(8,128)(2,1)S(1)} %collective-permute-done.left_ref, s32[1256,128]{1,0:T(8,128)S(1)} %inner_codes.1.main_ref), custom_call_target="tpu_custom_call" | custom-call | flops 1000000 | bytes 500000 | tf_op jit(solution)/shard_map/with_tails/pallas_call | solution.py:263
  9.3 13.7 %all-to-all-start = ((s32[64,19,1,128]{3,2,1,0:T(1,128)}), s32[64,19,1,128]{3,2,1,0:T(1,128)S(1)}, u32[]{:S(2)}, u32[]{:S(2)}) async-start(s32[64,19,1,128]{3,2,1,0:T(1,128)} %bitcast.23), calls=%async_computation | async-start | bytes 1245184 | tf_op jit(solution)/shard_map/all_to_all | solution.py:497
  23.0 0.0 copy-done
  23.0 0.0 copy-done.1
  23.0 0.0 copy-done.2
  23.0 4.0 %design_rows.1.rows_ref = bf16[816,384]{1,0:T(8,128)(2,1)S(1)} custom-call(f32[1,128]{1,0:T(1,128)S(1)} %bitcast.21, s32[1,128]{1,0:T(1,128)S(1)} %bitcast.22, s32[256,128]{1,0:T(8,128)S(1)} %copy-done), custom_call_target="tpu_custom_call" | custom-call | flops 4000000 | bytes 800000 | tf_op jit(solution)/shard_map/design_rows/pallas_call | solution.py:328
  27.0 15.4 %all-to-all-done = s32[64,19,1,128]{3,2,1,0:T(1,128)S(1)} async-done(((s32[64,19,1,128]{3,2,1,0:T(1,128)}), s32[64,19,1,128]{3,2,1,0:T(1,128)S(1)}, u32[]{:S(2)}, u32[]{:S(2)}) %all-to-all-start) | async-done | bytes 622624 | tf_op jit(solution)/shard_map/all_to_all | solution.py:497
  42.4 4.5 %block_stats.1 = (f32[2,8,128]{2,1,0:T(8,128)S(1)}, s16[256,2,128]{2,1,0:T(2,128)(2,1)}) custom-call(s32[1216,128]{1,0:T(8,128)S(1)} %bitcast.19, bf16[816,384]{1,0:T(8,128)(2,1)S(1)} %design_rows.1.rows_ref), custom_call_target="tpu_custom_call" | custom-call | flops 2000000000 | bytes 1000000 | tf_op jit(solution)/shard_map/block_stats/pallas_call | solution.py:453
  46.9 0.3 collective-permute-start.1
  47.2 7.4 %all-to-all-start.1 = ((s16[256,2,128]{2,1,0:T(2,128)(2,1)}), s16[256,2,128]{2,1,0:T(2,128)(2,1)S(1)}, u32[]{:S(2)}, u32[]{:S(2)}) async-start(s16[256,2,128]{2,1,0:T(2,128)(2,1)} %get-tuple-element.11), calls=%async_computation.1 | async-start | bytes 262144 | tf_op jit(solution)/shard_map/all_to_all | solution.py:509
  54.6 0.0 collective-permute-done.1
  54.6 2.7 %collective-permute-start.2 = (f32[2,8,128]{2,1,0:T(8,128)S(1)}, f32[2,8,128]{2,1,0:T(8,128)S(1)}, u32[]{:S(2)}, u32[]{:S(2)}) collective-permute-start(f32[2,8,128]{2,1,0:T(8,128)S(1)} %pad_maximum_fusion), channel_id=1, source_target_pairs={{1,0},{2,1},{3,2},{0,3},{5,4},{6,5},{7,6},{4,7},{9,8},{10,9},{11,1... | collective-permute-start | bytes 24584 | tf_op jit(solution)/shard_map/ppermute | solution.py:506
  57.3 0.8 %collective-permute-done.2 = f32[2,8,128]{2,1,0:T(8,128)S(1)} collective-permute-done((f32[2,8,128]{2,1,0:T(8,128)S(1)}, f32[2,8,128]{2,1,0:T(8,128)S(1)}, u32[]{:S(2)}, u32[]{:S(2)}) %collective-permute-start.2) | collective-permute-done | bytes 8224 | tf_op jit(solution)/shard_map/ppermute | solution.py:506
  58.1 0.6 broadcast_select_fusion
  58.7 8.7 %all-to-all-done.1 = s16[256,2,128]{2,1,0:T(2,128)(2,1)S(1)} async-done(((s16[256,2,128]{2,1,0:T(2,128)(2,1)}), s16[256,2,128]{2,1,0:T(2,128)(2,1)S(1)}, u32[]{:S(2)}, u32[]{:S(2)}) %all-to-all-start.1) | async-done | bytes 131104 | tf_op jit(solution)/shard_map/all_to_all | solution.py:509
  67.3 0.6 largest.1
  (4 shorter events, 0.0 us)
Async XLA Ops:
  3.2 5.0 %collective-permute-start = (bf16[56,512]{1,0:T(8,128)(2,1)S(1)}, bf16[56,512]{1,0:T(8,128)(2,1)S(1)}, u32[]{:S(2)}, u32[]{:S(2)}) collective-permute-start(bf16[56,512]{1,0:T(8,128)(2,1)S(1)} %get-tuple-element.8.sent_ref), channel_id=1, source_target_pairs={{0,1},{1,2},{2,3},{3,0},{4,5},{5,6},{6,7},{7,4},{8,9},{9,10},{10,1... | collective-permute-start | bytes 172040 | tf_op jit(solution)/shard_map/ppermute | solution.py:493
  5.3 17.7 %copy-start = (s32[256,128]{1,0:T(8,128)S(1)}, s32[256,128]{1,0:T(8,128)}, u32[]{:S(2)}) copy-start(s32[256,128]{1,0:T(8,128)} %perms_ref.1) | copy-start | bytes 393220
  5.3 17.7 %copy-start.1 = (f32[128]{0:T(128)S(1)}, f32[128]{0:T(128)}, u32[]{:S(2)}) copy-start(f32[128]{0:T(128)} %param.5) | copy-start | bytes 1540
  5.3 17.7 %copy-start.2 = (s32[128]{0:T(128)S(1)}, s32[128]{0:T(128)}, u32[]{:S(2)}) copy-start(s32[128]{0:T(128)} %param.6) | copy-start | bytes 1540
  9.3 33.1 %all-to-all-start = ((s32[64,19,1,128]{3,2,1,0:T(1,128)}), s32[64,19,1,128]{3,2,1,0:T(1,128)S(1)}, u32[]{:S(2)}, u32[]{:S(2)}) async-start(s32[64,19,1,128]{3,2,1,0:T(1,128)} %bitcast.23), calls=%async_computation | async-start | bytes 1245184 | tf_op jit(solution)/shard_map/all_to_all | solution.py:497
  46.9 7.7 %collective-permute-start.1 = (f32[8,128]{1,0:T(8,128)S(1)}, f32[8,128]{1,0:T(8,128)S(1)}, u32[]{:S(2)}, u32[]{:S(2)}) collective-permute-start(f32[8,128]{1,0:T(8,128)S(1)} %slice_bitcast_fusion), channel_id=1, source_target_pairs={{0,4},{4,0},{8,12},{12,8},{16,20},{20,16},{24,28},{28,24},{32,36},... | collective-permute-start | bytes 12296 | tf_op jit(solution)/shard_map/ppermute | solution.py:504
  47.2 20.1 %all-to-all-start.1 = ((s16[256,2,128]{2,1,0:T(2,128)(2,1)}), s16[256,2,128]{2,1,0:T(2,128)(2,1)S(1)}, u32[]{:S(2)}, u32[]{:S(2)}) async-start(s16[256,2,128]{2,1,0:T(2,128)(2,1)} %get-tuple-element.11), calls=%async_computation.1 | async-start | bytes 262144 | tf_op jit(solution)/shard_map/all_to_all | solution.py:509
  54.6 3.5 %collective-permute-start.2 = (f32[2,8,128]{2,1,0:T(8,128)S(1)}, f32[2,8,128]{2,1,0:T(8,128)S(1)}, u32[]{:S(2)}, u32[]{:S(2)}) collective-permute-start(f32[2,8,128]{2,1,0:T(8,128)S(1)} %pad_maximum_fusion), channel_id=1, source_target_pairs={{1,0},{2,1},{3,2},{0,3},{5,4},{6,5},{7,6},{4,7},{9,8},{10,9},{11,1... | collective-permute-start | bytes 24584 | tf_op jit(solution)/shard_map/ppermute | solution.py:506
